TPU v7x, 32 devices: a whole 2x2x4 slice. The times are simulated.
32 devices in a mesh: cluster: 4 (over z), member: 8 (over y, x, core).
Axes of the slice: x: 2, y: 2, z: 4, core: 2. Of those that a mesh axis runs over, the one named last changes fastest.
Arguments:
- dual_load: float32 [4, 8, 64, 2, 1024], P('cluster', 'member'), may hold values from -110 to 110
- dual_operator: bfloat16 [2048, 2048], replicated, may hold values from -1.5859375 to 3.5859375, as said below
- index_map: int32 [4, 8, 2048], P('cluster', 'member'), may hold values from 0 to 2047, as said below
- stiffness: float32 [4, 8], P('cluster', 'member'), may hold values from 1 to 10
- coarse_basis: float32 [4, 8, 6, 2048], P('cluster', 'member'), may hold values from -2.5 to 2.5
- dirichlet_blocks: bfloat16 [4, 8, 16, 128, 128], P('cluster', 'member'), may hold values from -1 to 2.5, as said below
- coarse_inverse: float32 [24, 24], replicated, may hold values from -1 to 1, as said below
Outputs:
- multipliers: float32 [4, 8, 64, 2, 1024], P('cluster', 'member')
- residual: float32 [4, 8, 64, 2, 1024], P('cluster', 'member')
Inputs may be any that keep to these rules, and one draw needn't show every extreme that they name: `dual_operator`: symmetric. `dirichlet_blocks`: each block is symmetric. `coarse_inverse`: symmetric. `index_map`: each subdomain's row names every position once.
All inputs are finite; a program needn't handle non-finite values.
Results may differ from a plain program's by a relative error of at most 0.0038.
Values sent between devices are 32-bit elements; how exact they have to be, the bound alone decides.
No kernel may reach another device: no remote copies, remote signals or barrier semaphores. Data moves between devices by JAX's collectives and lax.ppermute only.
A program may use at most 64 MiB of HBM per device.

v0:
```python
import jax
import jax.numpy as jnp
from jax import lax
from jax.sharding import PartitionSpec as P

ITERS = 2


exact_precision = lax.Precision.HIGHEST


def with_halo(array, sides, width):
    for axis, dim in sides:
        count, length = (lax.axis_size(axis), array.shape[dim])
        up = [(i, (i + 1) % count) for i in range(count - 1)]
        down = [(j, i) for i, j in up]
        last = lax.slice_in_dim(array, length - width, length, axis=dim)
        initial = lax.slice_in_dim(array, 0, width, axis=dim)
        before = lax.ppermute(last, axis, up)
        after = lax.ppermute(initial, axis, down)
        array = jnp.concatenate([before, array, after], axis=dim)
    return array


def per_device(
    dual_load, dual_operator, index_map, stiffness, coarse_basis, dirichlet_blocks, coarse_inverse
):
    load_cases = dual_load.shape[2]
    face_slots = dual_load.shape[4]
    slot_count = 2 * face_slots
    ordering = index_map.reshape(slot_count)
    inverse = (
        jnp.zeros((slot_count,), jnp.int32)
        .at[ordering]
        .set(jnp.arange(slot_count, dtype=jnp.int32))
    )
    softness = 1.0 / stiffness.reshape(())
    basis_rows = coarse_basis.reshape(coarse_basis.shape[2], slot_count)
    mode_count = basis_rows.shape[0]
    blocks = dirichlet_blocks.reshape(dirichlet_blocks.shape[2:])
    block_count = blocks.shape[0]
    block_size = blocks.shape[1]
    cluster_id = lax.axis_index("cluster")
    member_id = lax.axis_index("member")
    cluster_total = lax.axis_size("cluster")
    member_total = lax.axis_size("member")
    chain_pos = cluster_id * member_total + member_id
    chain_len = cluster_total * member_total
    low_side = jnp.where(chain_pos > 0, 0.5, 1.0)
    high_side = jnp.where(chain_pos < chain_len - 1, 0.5, 1.0)
    weights = jnp.stack([low_side, high_side]).astype(jnp.float32).reshape(1, 2, 1)

    def assemble(vector):
        padded = with_halo(vector, ((("cluster", "member"), 1),), 1)
        return vector + jnp.stack([padded[:, 0], padded[:, 3]], axis=1)

    def restrict(vector):
        return lax.dot_general(
            vector.reshape(load_cases, slot_count),
            basis_rows,
            (((1,), (1,)), ((), ())),
            precision=exact_precision,
        )

    def expand(own_amounts):
        return jnp.dot(own_amounts, basis_rows, precision=exact_precision).reshape(
            load_cases, 2, face_slots
        )

    def solve(totals):
        return lax.dot_general(
            totals, coarse_inverse, (((1,), (1,)), ((), ())), precision=exact_precision
        )

    residual = assemble(dual_load.reshape(load_cases, 2, face_slots))
    multipliers = jnp.zeros_like(residual)
    direction = residual
    rho_prev = None

    def coarse_totals(first, second, scalars):
        summed = lax.psum((first, second, scalars), "member")
        return (
            lax.all_gather(summed[0], "cluster", axis=1, tiled=True),
            lax.all_gather(summed[1], "cluster", axis=1, tiled=True),
            lax.all_gather(summed[2], "cluster", axis=1, tiled=True),
        )

    def correction(all_amounts):
        own_amounts = lax.dynamic_slice_in_dim(all_amounts, cluster_id * mode_count, mode_count, 1)
        return assemble(expand(own_amounts))

    empty_modes = jnp.zeros((load_cases, mode_count), jnp.float32)
    empty_scalars = jnp.zeros((load_cases, 1), jnp.float32)
    coarse_res, unused_modes, unused_scalars = coarse_totals(
        restrict(residual), empty_modes, empty_scalars
    )
    for sweep in range(ITERS):
        projected = residual - correction(solve(coarse_res))
        scaled = (
            (weights * projected).astype(jnp.bfloat16).reshape(load_cases, block_count, block_size)
        )
        blocked = jnp.einsum("rnj,nij->rni", scaled, blocks, preferred_element_type=jnp.float32)
        smoothed = assemble(weights * blocked.reshape(load_cases, 2, face_slots))
        cross_part = jnp.sum(weights * projected * smoothed, axis=(1, 2))[:, None]
        coarse_smooth, coarse_proj, cross_terms = coarse_totals(
            restrict(smoothed), restrict(projected), cross_part
        )
        smooth_amounts = solve(coarse_smooth)
        search = smoothed - correction(smooth_amounts)
        rho_now = jnp.sum(cross_terms, axis=1) - jnp.sum(coarse_proj * smooth_amounts, axis=1)
        if sweep == 0:
            direction = search
        else:
            direction = search + (rho_now / rho_prev)[:, None, None] * direction
        rho_prev = rho_now
        flattened = direction.astype(jnp.bfloat16).reshape(load_cases, slot_count)
        local_order = jnp.take(flattened, inverse, axis=1)
        product = jnp.dot(local_order, dual_operator, preferred_element_type=jnp.float32)
        local_image = (softness * jnp.take(product, ordering, axis=1)).reshape(
            load_cases, 2, face_slots
        )
        applied = assemble(local_image)
        energy_part = jnp.sum(direction * local_image, axis=(1, 2))[:, None]
        coarse_image, unused_modes, energy_terms = coarse_totals(
            restrict(applied), empty_modes, energy_part
        )
        step_size = rho_now / jnp.sum(energy_terms, axis=1)
        multipliers = multipliers + step_size[:, None, None] * direction
        residual = residual - step_size[:, None, None] * applied
        coarse_res = coarse_res - step_size[:, None] * coarse_image
    return (multipliers.reshape(dual_load.shape), residual.reshape(dual_load.shape))


def solution(mesh):
    in_specs = (
        P("cluster", "member", None, None, None),
        P(),
        P("cluster", "member", None),
        P("cluster", "member"),
        P("cluster", "member", None, None),
        P("cluster", "member", None, None, None),
        P(),
    )
    out_specs = (P("cluster", "member", None, None, None), P("cluster", "member", None, None, None))
    return jax.shard_map(
        per_device, mesh=mesh, in_specs=in_specs, out_specs=out_specs, check_vma=False
    )
```

profile of v0, /device:TPU:0, one launch (start us, length us, event | category | flops | bytes accessed | tf_op | source)
XLA Modules:
  0.0 363.6 jit_solution(14993864914463754904)
XLA Ops:
  2.0 2.4 collective-permute-start
  6.6 3.3 collective-permute-done.1
  13.8 20.4 %psum.70 = f32[64,6]{0,1:T(8,128)S(1)} all-reduce(f32[64,6]{0,1:T(8,128)S(1)} %fusion.34), channel_id=1, replica_groups=mesh['cluster'=4,'member'=8] {'member'}, use_global_device_ids=true, to_apply=%region_0.0 | all-reduce | flops 384 | bytes 3072 | tf_op jit(solution)/shard_map/psum | solution.py:81
  34.2 13.3 %all-gather = f32[4,6,64]{2,1,0:T(8,128)S(1)} all-gather(f32[1,6,64]{2,1,0:T(8,128)S(1)} %bitcast.195), channel_id=1, replica_groups=mesh['cluster'=4,'member'=8] {'cluster'}, dimensions={0}, use_global_device_ids=true | all-gather | bytes 7680 | tf_op jit(solution)/shard_map/all_gather | solution.py:83
  50.4 3.0 collective-permute-start.2
  59.2 4.8 %collective-permute-start.4 = (f32[64,1,1024]{2,0,1:T(8,128)S(1)}, f32[64,1,1024]{2,0,1:T(8,128)S(1)}, u32[]{:S(2)}, u32[]{:S(2)}) collective-permute-start(f32[64,1,1024]{2,0,1:T(8,128)S(1)} %get-tuple-element.47), channel_id=1, source_target_pairs={{0,1},{1,2},{2,3},{3,4},{4,5},{5,6},{6,7},{7,8},{8,9},{9,10},{10,1... | collective-permute-start | bytes 786440 | tf_op jit(solution)/shard_map/ppermute | solution.py:19
  65.2 8.7 %scatter_custom_fusion = s32[2048]{0:T(1024)} fusion(s32[2048]{0:T(1024)} %bitcast.197, s32[2048]{0:T(1024)} %iota.3, s32[]{:T(128)} %constant.6.clone.1), kind=kCustom, calls=%fused_computation.100 | custom fusion | bytes 8704 | tf_op jit(solution)/shard_map/scatter | solution.py:35
  77.4 17.1 %psum.73 = f32[64,6]{0,1:T(8,128)S(1)} all-reduce(f32[64,6]{0,1:T(8,128)S(1)} %fusion.28), channel_id=1, replica_groups=mesh['cluster'=4,'member'=8] {'member'}, use_global_device_ids=true, to_apply=%region_5.6 | all-reduce | flops 384 | bytes 3072 | tf_op jit(solution)/shard_map/psum | solution.py:81
  94.5 13.1 %all-gather.3 = f32[4,6,64]{2,1,0:T(8,128)S(1)} all-gather(f32[1,6,64]{2,1,0:T(8,128)S(1)} %bitcast.196), channel_id=1, replica_groups=mesh['cluster'=4,'member'=8] {'cluster'}, dimensions={0}, use_global_device_ids=true | all-gather | bytes 7680 | tf_op jit(solution)/shard_map/all_gather | solution.py:83
  110.4 3.2 collective-permute-start.6
  118.3 8.8 %gather_fusion = bf16[2048,64]{1,0:T(8,128)(2,1)} fusion(bf16[64,2048]{0,1:T(8,128)(2,1)S(1)} %bitcast.167, s32[2048]{0:T(1024)} %get-tuple-element.55), kind=kCustom, calls=%fused_computation.clone | custom fusion | bytes 532480 | tf_op jit(solution)/shard_map/jit(_take)/gather | solution.py:117
  127.1 7.2 %fusion.11 = f32[64,2048]{0,1:T(8,128)S(1)} fusion(bf16[2048,2048]{1,0:T(8,128)(2,1)} %param.12, bf16[2048,64]{1,0:T(8,128)(2,1)} %gather_fusion, pred[2048]{0:T(1024)(128)(4,1)} %compare_and_fusion.1), kind=kOutput, calls=%fused_computation.31 | convolution fusion | flops 537001984 | bytes 9177088 | tf_op jit(solution)/shard_map/dot_general | solution.py:118
  134.3 7.6 %gather_fusion.1 = f32[2048,64]{1,0:T(8,128)} fusion(f32[64,2048]{0,1:T(8,128)S(1)} %fusion.11, s32[2048]{0:T(1024)S(1)} %get-tuple-element.56), kind=kCustom, calls=%fused_computation.1.clone | custom fusion | bytes 1056768 | tf_op jit(solution)/shard_map/jit(_take)/gather | solution.py:119
  148.6 3.9 %collective-permute-done.9 = f32[64,1,1024]{2,0,1:T(8,128)S(1)} collective-permute-done((f32[64,1,1024]{2,0,1:T(8,128)S(1)}, f32[64,1,1024]{2,0,1:T(8,128)S(1)}, u32[]{:S(2)}, u32[]{:S(2)}) %collective-permute-start.9) | collective-permute-done | bytes 262176 | tf_op jit(solution)/shard_map/ppermute | solution.py:20
  153.9 21.7 %all-reduce.1 = (f32[64,6]{0,1:T(8,128)S(1)}, f32[64,1]{0,1:T(1,128)S(1)}, f32[64,6]{0,1:T(8,128)S(1)}, f32[64,1]{0,1:T(1,128)S(1)}) all-reduce(f32[64,6]{0,1:T(8,128)S(1)} %fusion.17, f32[64,1]{0,1:T(1,128)S(1)} %bitcast.203, f32[64,6]{0,1:T(8,128)S(1)} %fusion.30, ...), channel_id=1, replica_groups=mesh['cluster'=4,'member'=8] {'member'}, use_global_device_ids=true, to_apply=%region_11.14 | all-reduce | flops 896 | bytes 7168 | tf_op jit(solution)/shard_map/psum | solution.py:81
  175.6 8.9 %all-gather.4 = f32[4,1,64]{2,1,0:T(1,128)S(1)} all-gather(f32[1,1,64]{2,1,0:T(1,128)S(1)} %bitcast.208), channel_id=1, replica_groups=mesh['cluster'=4,'member'=8] {'cluster'}, dimensions={0}, use_global_device_ids=true | all-gather | bytes 1280 | tf_op jit(solution)/shard_map/all_gather | solution.py:85
  184.5 8.2 %all-gather.1 = f32[4,1,64]{2,1,0:T(1,128)S(1)} all-gather(f32[1,1,64]{2,1,0:T(1,128)S(1)} %bitcast.207), channel_id=1, replica_groups=mesh['cluster'=4,'member'=8] {'cluster'}, dimensions={0}, use_global_device_ids=true | all-gather | bytes 1280 | tf_op jit(solution)/shard_map/all_gather | solution.py:85
  192.7 13.1 %all-gather.2 = f32[4,6,64]{2,1,0:T(8,128)S(1)} all-gather(f32[1,6,64]{2,1,0:T(8,128)S(1)} %bitcast.199), channel_id=1, replica_groups=mesh['cluster'=4,'member'=8] {'cluster'}, dimensions={0}, use_global_device_ids=true | all-gather | bytes 7680 | tf_op jit(solution)/shard_map/all_gather | solution.py:84
  205.8 13.1 %all-gather.5 = f32[4,6,64]{2,1,0:T(8,128)S(1)} all-gather(f32[1,6,64]{2,1,0:T(8,128)S(1)} %bitcast.198), channel_id=1, replica_groups=mesh['cluster'=4,'member'=8] {'cluster'}, dimensions={0}, use_global_device_ids=true | all-gather | bytes 7680 | tf_op jit(solution)/shard_map/all_gather | solution.py:83
  221.6 3.0 collective-permute-start.10
  232.8 4.8 %collective-permute-start.12 = (f32[64,1,1024]{2,0,1:T(8,128)S(1)}, f32[64,1,1024]{2,0,1:T(8,128)S(1)}, u32[]{:S(2)}, u32[]{:S(2)}) collective-permute-start(f32[64,1,1024]{2,0,1:T(8,128)S(1)} %get-tuple-element.39), channel_id=1, source_target_pairs={{0,1},{1,2},{2,3},{3,4},{4,5},{5,6},{6,7},{7,8},{8,9},{9,10},{10,1... | collective-permute-start | bytes 786440 | tf_op jit(solution)/shard_map/ppermute | solution.py:19
  240.9 19.9 %all-reduce = (f32[64,6]{0,1:T(8,128)S(1)}, f32[64,1]{0,1:T(1,128)S(1)}, f32[64,6]{0,1:T(8,128)S(1)}) all-reduce(f32[64,6]{0,1:T(8,128)S(1)} %fusion.32, f32[64,1]{0,1:T(1,128)} %bitcast.204, f32[64,6]{0,1:T(8,128)} %fusion.25), channel_id=1, replica_groups=mesh['cluster'=4,'member'=8] {'member'}, use_global_device_ids=true, to_apply=%region_16.19 | all-reduce | flops 832 | bytes 6656 | tf_op jit(solution)/shard_map/psum | solution.py:81
  260.7 14.1 %all-gather.7 = f32[4,6,64]{2,1,0:T(8,128)S(1)} all-gather(f32[1,6,64]{2,1,0:T(8,128)S(1)} %bitcast.201), channel_id=1, replica_groups=mesh['cluster'=4,'member'=8] {'cluster'}, dimensions={0}, use_global_device_ids=true | all-gather | bytes 7680 | tf_op jit(solution)/shard_map/all_gather | solution.py:84
  274.8 13.1 %all-gather.8 = f32[4,6,64]{2,1,0:T(8,128)S(1)} all-gather(f32[1,6,64]{2,1,0:T(8,128)S(1)} %bitcast.200), channel_id=1, replica_groups=mesh['cluster'=4,'member'=8] {'cluster'}, dimensions={0}, use_global_device_ids=true | all-gather | bytes 7680 | tf_op jit(solution)/shard_map/all_gather | solution.py:83
  290.9 3.7 %collective-permute-start.14 = (f32[64,1,1024]{2,0,1:T(8,128)}, f32[64,1,1024]{2,0,1:T(8,128)}, u32[]{:S(2)}, u32[]{:S(2)}) collective-permute-start(f32[64,1,1024]{2,0,1:T(8,128)} %get-tuple-element.37), channel_id=1, source_target_pairs={{0,1},{1,2},{2,3},{3,4},{4,5},{5,6},{6,7},{7,8},{8,9},{9,10},{10,1... | collective-permute-start | bytes 786440 | tf_op jit(solution)/shard_map/ppermute | solution.py:19
  295.9 10.2 %all-gather.6 = f32[4,1,64]{2,1,0:T(1,128)S(1)} all-gather(f32[1,1,64]{2,1,0:T(1,128)S(1)} %bitcast.206), channel_id=1, replica_groups=mesh['cluster'=4,'member'=8] {'cluster'}, dimensions={0}, use_global_device_ids=true | all-gather | bytes 1280 | tf_op jit(solution)/shard_map/all_gather | solution.py:85
  309.3 8.1 %gather_fusion.2 = bf16[2048,64]{1,0:T(8,128)(2,1)} fusion(bf16[64,2048]{0,1:T(8,128)(2,1)S(1)} %bitcast.166, s32[2048]{0:T(1024)S(1)} %copy-done.12), kind=kCustom, calls=%fused_computation.2.clone | custom fusion | bytes 532480 | tf_op jit(solution)/shard_map/jit(_take)/gather | solution.py:117
  317.3 7.3 %fusion.9 = f32[64,2048]{0,1:T(8,128)S(1)} fusion(bf16[2048,2048]{1,0:T(8,128)(2,1)} %param.12, bf16[2048,64]{1,0:T(8,128)(2,1)} %gather_fusion.2, pred[2048]{0:T(1024)(128)(4,1)} %compare_and_fusion.1), kind=kOutput, calls=%fused_computation.28 | convolution fusion | flops 537001984 | bytes 9177088 | tf_op jit(solution)/shard_map/dot_general | solution.py:118
  324.6 7.6 %gather_fusion.3 = f32[2048,64]{1,0:T(8,128)} fusion(f32[64,2048]{0,1:T(8,128)S(1)} %fusion.9, s32[2048]{0:T(1024)S(1)} %get-tuple-element.56), kind=kCustom, calls=%fused_computation.3.clone | custom fusion | bytes 1056768 | tf_op jit(solution)/shard_map/jit(_take)/gather | solution.py:119
  335.3 11.8 %psum.79 = f32[64,1]{0,1:T(1,128)S(1)} all-reduce(f32[64,1]{0,1:T(1,128)S(1)} %bitcast.205), channel_id=1, replica_groups=mesh['cluster'=4,'member'=8] {'member'}, use_global_device_ids=true, to_apply=%region_19.22 | all-reduce | flops 64 | bytes 512 | tf_op jit(solution)/shard_map/psum | solution.py:81
  347.0 7.5 %all-gather.9 = f32[4,1,64]{2,1,0:T(1,128)S(1)} all-gather(f32[1,1,64]{2,1,0:T(1,128)S(1)} %bitcast.209), channel_id=1, replica_groups=mesh['cluster'=4,'member'=8] {'cluster'}, dimensions={0}, use_global_device_ids=true | all-gather | bytes 1280 | tf_op jit(solution)/shard_map/all_gather | solution.py:85
  355.9 3.0 collective-permute-start.16
  (165 shorter events, 65.5 us)
Async XLA Ops:
  0.6 54.7 %copy-start = (bf16[1,1,16,128,128]{4,3,2,1,0:T(8,128)(2,1)S(1)}, bf16[1,1,16,128,128]{4,3,2,1,0:T(8,128)(2,1)}, u32[]{:S(2)}) copy-start(bf16[1,1,16,128,128]{4,3,2,1,0:T(8,128)(2,1)} %param.16) | copy-start | bytes 1572868
  0.6 53.9 %copy-start.1 = (f32[1,1,64,2,1024]{4,3,2,1,0:T(2,128)S(1)}, f32[1,1,64,2,1024]{4,3,2,1,0:T(2,128)}, u32[]{:S(2)}) copy-start(f32[1,1,64,2,1024]{4,3,2,1,0:T(2,128)} %param.11) | copy-start | bytes 1572868
  2.0 62.0 %copy-start.13 = (s32[1,1,2048]{2,1,0:T(1,128)S(1)}, s32[1,1,2048]{2,1,0:T(1,128)}, u32[]{:S(2)}) copy-start(s32[1,1,2048]{2,1,0:T(1,128)} %param.13) | copy-start | bytes 24580
  2.0 4.5 %collective-permute-start = (f32[64,1,1024]{2,0,1:T(8,128)S(1)}, f32[64,1,1024]{2,0,1:T(8,128)S(1)}, u32[]{:S(2)}, u32[]{:S(2)}) collective-permute-start(f32[64,1,1024]{2,0,1:T(8,128)S(1)} %get-tuple-element.52), channel_id=1, source_target_pairs={{0,1},{1,2},{2,3},{3,4},{4,5},{5,6},{6,7},{7,8},{8,9},{9,10},{10,1... | collective-permute-start | bytes 786440 | tf_op jit(solution)/shard_map/ppermute | solution.py:19
  4.4 5.5 %collective-permute-start.1 = (f32[64,1,1024]{2,0,1:T(8,128)S(1)}, f32[64,1,1024]{2,0,1:T(8,128)S(1)}, u32[]{:S(2)}, u32[]{:S(2)}) collective-permute-start(f32[64,1,1024]{2,0,1:T(8,128)S(1)} %get-tuple-element.51), channel_id=1, source_target_pairs={{1,0},{2,1},{3,2},{4,3},{5,4},{6,5},{7,6},{8,7},{9,8},{10,9},{11,1... | collective-permute-start | bytes 786440 | tf_op jit(solution)/shard_map/ppermute | solution.py:20
  11.9 65.0 %copy-start.3 = (f32[1,1,6,2048]{3,1,2,0:T(1,128)S(1)}, f32[1,1,6,2048]{3,1,2,0:T(1,128)}, u32[]{:S(2)}) copy-start(f32[1,1,6,2048]{3,1,2,0:T(1,128)} %param.15) | copy-start | bytes 147460
  12.3 95.4 %copy-start.11 = (f32[24,24]{1,0:T(8,128)S(1)}, f32[24,24]{1,0:T(8,128)}, u32[]{:S(2)}) copy-start(f32[24,24]{1,0:T(8,128)} %param.17) | copy-start | bytes 6916
  49.1 4.5 %collective-permute-start.3 = (f32[64,1,1024]{2,0,1:T(8,128)S(1)}, f32[64,1,1024]{2,0,1:T(8,128)S(1)}, u32[]{:S(2)}, u32[]{:S(2)}) collective-permute-start(f32[64,1,1024]{2,0,1:T(8,128)S(1)} %get-tuple-element.50), channel_id=1, source_target_pairs={{1,0},{2,1},{3,2},{4,3},{5,4},{6,5},{7,6},{8,7},{9,8},{10,9},{11,1... | collective-permute-start | bytes 786440 | tf_op jit(solution)/shard_map/ppermute | solution.py:20
  50.4 4.2 %collective-permute-start.2 = (f32[64,1,1024]{2,0,1:T(8,128)S(1)}, f32[64,1,1024]{2,0,1:T(8,128)S(1)}, u32[]{:S(2)}, u32[]{:S(2)}) collective-permute-start(f32[64,1,1024]{2,0,1:T(8,128)S(1)} %get-tuple-element.49), channel_id=1, source_target_pairs={{0,1},{1,2},{2,3},{3,4},{4,5},{5,6},{6,7},{7,8},{8,9},{9,10},{10,1... | collective-permute-start | bytes 786440 | tf_op jit(solution)/shard_map/ppermute | solution.py:19
  58.0 17.3 %collective-permute-start.5 = (f32[64,1,1024]{2,0,1:T(8,128)}, f32[64,1,1024]{2,0,1:T(8,128)S(1)}, u32[]{:S(2)}, u32[]{:S(2)}) collective-permute-start(f32[64,1,1024]{2,0,1:T(8,128)} %get-tuple-element.48), channel_id=1, source_target_pairs={{1,0},{2,1},{3,2},{4,3},{5,4},{6,5},{7,6},{8,7},{9,8},{10,9},{11,1... | collective-permute-start | bytes 786440 | tf_op jit(solution)/shard_map/ppermute | solution.py:20
  59.2 16.0 %collective-permute-start.4 = (f32[64,1,1024]{2,0,1:T(8,128)S(1)}, f32[64,1,1024]{2,0,1:T(8,128)S(1)}, u32[]{:S(2)}, u32[]{:S(2)}) collective-permute-start(f32[64,1,1024]{2,0,1:T(8,128)S(1)} %get-tuple-element.47), channel_id=1, source_target_pairs={{0,1},{1,2},{2,3},{3,4},{4,5},{5,6},{6,7},{7,8},{8,9},{9,10},{10,1... | collective-permute-start | bytes 786440 | tf_op jit(solution)/shard_map/ppermute | solution.py:19
  109.1 8.0 %collective-permute-start.7 = (f32[64,1,1024]{2,0,1:T(8,128)S(1)}, f32[64,1,1024]{2,0,1:T(8,128)S(1)}, u32[]{:S(2)}, u32[]{:S(2)}) collective-permute-start(f32[64,1,1024]{2,0,1:T(8,128)S(1)} %get-tuple-element.46), channel_id=1, source_target_pairs={{1,0},{2,1},{3,2},{4,3},{5,4},{6,5},{7,6},{8,7},{9,8},{10,9},{11,1... | collective-permute-start | bytes 786440 | tf_op jit(solution)/shard_map/ppermute | solution.py:20
  110.4 6.7 %collective-permute-start.6 = (f32[64,1,1024]{2,0,1:T(8,128)S(1)}, f32[64,1,1024]{2,0,1:T(8,128)S(1)}, u32[]{:S(2)}, u32[]{:S(2)}) collective-permute-start(f32[64,1,1024]{2,0,1:T(8,128)S(1)} %get-tuple-element.45), channel_id=1, source_target_pairs={{0,1},{1,2},{2,3},{3,4},{4,5},{5,6},{6,7},{7,8},{8,9},{9,10},{10,1... | collective-permute-start | bytes 786440 | tf_op jit(solution)/shard_map/ppermute | solution.py:19
  134.3 19.6 %copy-start.23 = (f32[64]{0:T(128)S(1)}, f32[64]{0:T(128)}, u32[]{:S(2)}) copy-start(f32[64]{0:T(128)} %get-tuple-element.33) | copy-start | bytes 772
  134.3 71.5 %copy-start.15 = (f32[64,24]{0,1:T(8,128)S(1)}, f32[64,24]{0,1:T(8,128)}, u32[]{:S(2)}) copy-start(f32[64,24]{0,1:T(8,128)} %copy-done.14) | copy-start | bytes 18436
  134.3 91.5 %copy-start.17 = (f32[2]{0:T(128)S(1)}, f32[2]{0:T(128)}, u32[]{:S(2)}) copy-start(f32[2]{0:T(128)} %copy-done.16) | copy-start | bytes 28
  143.6 4.9 %collective-permute-start.8 = (f32[64,1,1024]{2,0,1:T(8,128)S(1)}, f32[64,1,1024]{2,0,1:T(8,128)S(1)}, u32[]{:S(2)}, u32[]{:S(2)}) collective-permute-start(f32[64,1,1024]{2,0,1:T(8,128)S(1)} %get-tuple-element.44), channel_id=1, source_target_pairs={{0,1},{1,2},{2,3},{3,4},{4,5},{5,6},{6,7},{7,8},{8,9},{9,10},{10,1... | collective-permute-start | bytes 786440 | tf_op jit(solution)/shard_map/ppermute | solution.py:19
  147.1 5.4 %collective-permute-start.9 = (f32[64,1,1024]{2,0,1:T(8,128)S(1)}, f32[64,1,1024]{2,0,1:T(8,128)S(1)}, u32[]{:S(2)}, u32[]{:S(2)}) collective-permute-start(f32[64,1,1024]{2,0,1:T(8,128)S(1)} %get-tuple-element.43), channel_id=1, source_target_pairs={{1,0},{2,1},{3,2},{4,3},{5,4},{6,5},{7,6},{8,7},{9,8},{10,9},{11,1... | collective-permute-start | bytes 786440 | tf_op jit(solution)/shard_map/ppermute | solution.py:20
  148.6 76.1 %copy-start.9 = (f32[64,1,1024]{2,0,1:T(8,128)}, f32[64,1,1024]{2,0,1:T(8,128)S(1)}, u32[]{:S(2)}) copy-start(f32[64,1,1024]{2,0,1:T(8,128)S(1)} %collective-permute-done.8) | copy-start | bytes 786436
  152.5 72.2 %copy-start.10 = (f32[64,1,1024]{2,0,1:T(8,128)}, f32[64,1,1024]{2,0,1:T(8,128)S(1)}, u32[]{:S(2)}) copy-start(f32[64,1,1024]{2,0,1:T(8,128)S(1)} %collective-permute-done.9) | copy-start | bytes 786436
  220.3 4.4 %collective-permute-start.11 = (f32[64,1,1024]{2,0,1:T(8,128)S(1)}, f32[64,1,1024]{2,0,1:T(8,128)S(1)}, u32[]{:S(2)}, u32[]{:S(2)}) collective-permute-start(f32[64,1,1024]{2,0,1:T(8,128)S(1)} %get-tuple-element.42), channel_id=1, source_target_pairs={{1,0},{2,1},{3,2},{4,3},{5,4},{6,5},{7,6},{8,7},{9,8},{10,9},{11,1... | collective-permute-start | bytes 786440 | tf_op jit(solution)/shard_map/ppermute | solution.py:20
  221.6 4.2 %collective-permute-start.10 = (f32[64,1,1024]{2,0,1:T(8,128)S(1)}, f32[64,1,1024]{2,0,1:T(8,128)S(1)}, u32[]{:S(2)}, u32[]{:S(2)}) collective-permute-start(f32[64,1,1024]{2,0,1:T(8,128)S(1)} %get-tuple-element.41), channel_id=1, source_target_pairs={{0,1},{1,2},{2,3},{3,4},{4,5},{5,6},{6,7},{7,8},{8,9},{9,10},{10,1... | collective-permute-start | bytes 786440 | tf_op jit(solution)/shard_map/ppermute | solution.py:19
  227.3 79.4 %copy-start.18 = (f32[2]{0:T(128)S(1)}, f32[2]{0:T(128)}, u32[]{:S(2)}) copy-start(f32[2]{0:T(128)} %copy-done.16) | copy-start | bytes 28
  228.2 81.0 %copy-start.12 = (s32[2048]{0:T(1024)S(1)}, s32[2048]{0:T(1024)}, u32[]{:S(2)}) copy-start(s32[2048]{0:T(1024)} %get-tuple-element.55) | copy-start | bytes 24580
  231.5 7.3 %collective-permute-start.13 = (f32[64,1,1024]{2,0,1:T(8,128)S(1)}, f32[64,1,1024]{2,0,1:T(8,128)S(1)}, u32[]{:S(2)}, u32[]{:S(2)}) collective-permute-start(f32[64,1,1024]{2,0,1:T(8,128)S(1)} %get-tuple-element.40), channel_id=1, source_target_pairs={{1,0},{2,1},{3,2},{4,3},{5,4},{6,5},{7,6},{8,7},{9,8},{10,9},{11,1... | collective-permute-start | bytes 786440 | tf_op jit(solution)/shard_map/ppermute | solution.py:20
  232.8 6.0 %collective-permute-start.12 = (f32[64,1,1024]{2,0,1:T(8,128)S(1)}, f32[64,1,1024]{2,0,1:T(8,128)S(1)}, u32[]{:S(2)}, u32[]{:S(2)}) collective-permute-start(f32[64,1,1024]{2,0,1:T(8,128)S(1)} %get-tuple-element.39), channel_id=1, source_target_pairs={{0,1},{1,2},{2,3},{3,4},{4,5},{5,6},{6,7},{7,8},{8,9},{9,10},{10,1... | collective-permute-start | bytes 786440 | tf_op jit(solution)/shard_map/ppermute | solution.py:19
  289.6 17.1 %collective-permute-start.15 = (f32[64,1,1024]{2,0,1:T(8,128)}, f32[64,1,1024]{2,0,1:T(8,128)}, u32[]{:S(2)}, u32[]{:S(2)}) collective-permute-start(f32[64,1,1024]{2,0,1:T(8,128)} %get-tuple-element.38), channel_id=1, source_target_pairs={{1,0},{2,1},{3,2},{4,3},{5,4},{6,5},{7,6},{8,7},{9,8},{10,9},{11,1... | collective-permute-start | bytes 786440 | tf_op jit(solution)/shard_map/ppermute | solution.py:20
  290.9 15.8 %collective-permute-start.14 = (f32[64,1,1024]{2,0,1:T(8,128)}, f32[64,1,1024]{2,0,1:T(8,128)}, u32[]{:S(2)}, u32[]{:S(2)}) collective-permute-start(f32[64,1,1024]{2,0,1:T(8,128)} %get-tuple-element.37), channel_id=1, source_target_pairs={{0,1},{1,2},{2,3},{3,4},{4,5},{5,6},{6,7},{7,8},{8,9},{9,10},{10,1... | collective-permute-start | bytes 786440 | tf_op jit(solution)/shard_map/ppermute | solution.py:19
  317.3 41.7 %copy-start.22 = (f32[64]{0:T(128)S(1)}, f32[64]{0:T(128)}, u32[]{:S(2)}) copy-start(f32[64]{0:T(128)} %copy-done.21) | copy-start | bytes 772
  324.6 35.8 %copy-start.7 = (f32[64,1,1024]{2,0,1:T(8,128)S(1)}, f32[64,1,1024]{2,0,1:T(8,128)}, u32[]{:S(2)}) copy-start(f32[64,1,1024]{2,0,1:T(8,128)} %copy-done.6) | copy-start | bytes 786436
  354.6 5.7 %collective-permute-start.17 = (f32[64,1,1024]{2,0,1:T(8,128)S(1)}, f32[64,1,1024]{2,0,1:T(8,128)S(1)}, u32[]{:S(2)}, u32[]{:S(2)}) collective-permute-start(f32[64,1,1024]{2,0,1:T(8,128)S(1)} %get-tuple-element.36), channel_id=1, source_target_pairs={{1,0},{2,1},{3,2},{4,3},{5,4},{6,5},{7,6},{8,7},{9,8},{10,9},{11,1... | collective-permute-start | bytes 786440 | tf_op jit(solution)/shard_map/ppermute | solution.py:20
  355.9 4.4 %collective-permute-start.16 = (f32[64,1,1024]{2,0,1:T(8,128)S(1)}, f32[64,1,1024]{2,0,1:T(8,128)S(1)}, u32[]{:S(2)}, u32[]{:S(2)}) collective-permute-start(f32[64,1,1024]{2,0,1:T(8,128)S(1)} %get-tuple-element.35), channel_id=1, source_target_pairs={{0,1},{1,2},{2,3},{3,4},{4,5},{5,6},{6,7},{7,8},{8,9},{9,10},{10,1... | collective-permute-start | bytes 786440 | tf_op jit(solution)/shard_map/ppermute | solution.py:19
  (10 other events, 67.4 us)
where the time goes:
time: 370 us; the launch traced here: 364 us
  blocking collectives  205 us (55%)
  local copies, waits for them, and re-layouts  61.7 us (17%)
  starting transfers between devices  41.6 us (11%)
  matrix products  24.8 us (7%)
  other arithmetic  18.5 us (5%)
  waiting for transfers between devices  9.38 us (3%)
    psum x5, blocking collectives, coarse_totals(): summed = lax.psum((first, second, scalars), 'member')  90.8 us
    all_gather x4, blocking collectives, coarse_totals(): lax.all_gather(summed[0], 'cluster', axis=1, tiled=True)  52.7 us
    all_gather x4, blocking collectives, coarse_totals(): lax.all_gather(summed[2], 'cluster', axis=1, tiled=True)  34.7 us
    ppermute x9, starting transfers between devices, with_halo(): before = lax.ppermute(last, axis, up)  30 us
    all_gather x2, blocking collectives, coarse_totals(): lax.all_gather(summed[1], 'cluster', axis=1, tiled=True)  27.2 us
    gather x4, local copies, waits for them, and re-layouts, per_device(): jnp.take(product, ordering, axis=1)  18.3 us
    gather x2, local copies, waits for them, and re-layouts, per_device(): local_order = jnp.take(flattened, inverse, axis=1)  16.8 us
    dot_general x2, matrix products, per_device(): jnp.dot(local_order, dual_operator, preferred_element_type=jnp.float32)  14.5 us
  transfers between devices with their start and end apart: 18, of which 4 were waited for; matrix products, arithmetic and copies ran while one was open for 6% of the time, Pallas kernels for 0%

commit v1 on v0

v1 whole, which is shorter than its diff:
```python
import functools

import jax
import jax.numpy as jnp
import numpy as np
from jax import lax
from jax.experimental import pallas as pl
from jax.experimental.pallas import tpu as pltpu
from jax.sharding import PartitionSpec as P

AXES = ("cluster", "member")
F32 = jnp.float32
BF16 = jnp.bfloat16
EXACT = lax.Precision.HIGHEST
KP = 8
TILE = 512


def dot(left, right):
    return jnp.dot(left, right, preferred_element_type=F32)


def dot_rows(left, right):
    return lax.dot_general(
        left, right, (((1,), (1,)), ((), ())), precision=EXACT, preferred_element_type=F32
    )


def dot_modes(amounts, rows):
    return lax.dot_general(
        amounts, rows, (((0,), (0,)), ((), ())), precision=EXACT, preferred_element_type=F32
    )


def two_parts(value):
    high = value.astype(BF16)
    return high, (value - high.astype(F32)).astype(BF16)


def chain_table(clusters, members):
    count = clusters * members
    ints, floats = [], []

    def side(pos):
        cluster, member = divmod(pos, members)
        other = cluster
        if member == 0:
            other = cluster - 1
        elif member == members - 1:
            other = cluster + 1
        return cluster, min(max(other, 0), clusters - 1)

    for pos in range(count):
        row, near = [pos % 2], []
        row += side(pos)
        for partner in (pos ^ 1, pos - 1 if pos % 2 == 0 else pos + 1):
            real = 0 <= partner < count
            row += side(partner if real else pos)
            near.append((0.5 if real else 1.0, float(real and partner // members == pos // members)))
        ints.append(row)
        floats.append([near[0][0], near[1][0], near[0][1], near[1][1]])
    return np.array(ints, np.int32), np.array(floats, np.float32)


def pack_kernel(modes, ints, load, basis, blocks, out_a, out_b):
    loads, _, face = load.shape
    half = blocks.shape[0] // 2
    size = blocks.shape[1]
    odd = ints[0] == 1
    row = lax.broadcasted_iota(jnp.int32, (size, size), 0)
    col = lax.broadcasted_iota(jnp.int32, (size, size), 1)
    load_0, load_1 = load[:, 0, :], load[:, 1, :]
    basis_0, basis_1 = basis[:, :face], basis[:, face:]
    low = loads + KP
    mid = size // 2
    for out, first in ((out_a, odd), (out_b, jnp.logical_not(odd))):
        out[:loads, :] = jnp.where(first, load_0, load_1)
        out[loads:low, :] = jnp.zeros((KP, face), F32)
        out[loads : loads + modes, :] = jnp.where(first, basis_0, basis_1)
        base = jnp.where(first, 0, half)
        for pair in range(half // 2):
            upper = blocks[base + 2 * pair].astype(F32)
            lower = blocks[base + 2 * pair + 1].astype(F32)
            both = jnp.where(row <= col, upper, lower)
            left = pair * size
            right = (half // 2 + pair) * size
            out[low : low + mid, left : left + size] = both[:mid]
            out[low : low + mid, right : right + size] = both[mid:]
            diagonal = jnp.sum(jnp.where(row == col, lower, 0.0), axis=0, keepdims=True)
            out[loads + modes : loads + modes + 1, left : left + size] = diagonal


def order_kernel(position_rows, position_cols, pick, place):
    rows, count = pick.shape
    here = lax.broadcasted_iota(jnp.int32, (rows, count), 1)
    pick[...] = jnp.where(position_rows[...] == here, 1.0, 0.0).astype(BF16)
    start = pl.program_id(0) * rows
    here = lax.broadcasted_iota(jnp.int32, (rows, count), 0) + start
    place[...] = jnp.where(position_cols[...] == here, 1.0, 0.0).astype(BF16)


def operator_step(step, tiles, rows, pick, operator, place, first, second, third, finish):
    @pl.when(step < tiles)
    def _():
        cols = pl.ds(pl.multiple_of(step * TILE, TILE), TILE)
        second[:, cols] = dot(first[...], pick[...]).astype(BF16)

    @pl.when((step >= tiles) & (step < 2 * tiles))
    def _():
        cols = pl.ds(pl.multiple_of((step - tiles) * TILE, TILE), TILE)
        product = dot(second[...], operator[...])
        high, low = two_parts(product[:rows] + product[rows:])
        third[:rows, cols] = high
        third[rows:, cols] = low

    @pl.when(step >= 2 * tiles)
    def _():
        product = dot(third[...], place[...])
        finish(step - 2 * tiles, product[:rows] + product[rows:])


def store_image(tile, value, tiles, image_a, image_b):
    half = tiles // 2

    @pl.when(tile < half)
    def _():
        image_a[:, pl.ds(pl.multiple_of(tile * TILE, TILE), TILE)] = value

    @pl.when(tile >= half)
    def _():
        image_b[:, pl.ds(pl.multiple_of((tile - half) * TILE, TILE), TILE)] = value


def smooth_block(value, weight, block_pair):
    rows = value.shape[0]
    high, low = two_parts(weight * value)
    left = jnp.concatenate(
        [jnp.concatenate([high, high], axis=1), jnp.concatenate([low, low], axis=1)], axis=0
    )
    product = dot(left, block_pair)
    return weight * (product[:rows] + product[rows:])


def first_kernel(
    modes, tiles,
    ints, floats, pay_a, pay_b, got_a, got_b, blocks, pick, operator, place,
    residual, smooth, coarse, pairs, image_a, image_b, terms,
    own_basis, first, second, third,
):
    step = pl.program_id(0)
    loads, slots = residual.shape
    face = slots // 2
    count = pairs.shape[0]
    half = count // 2
    size = pairs.shape[2]
    rows = loads + 4 * KP
    low_row = loads + KP
    mid = size // 2

    @pl.when(step == 0)
    def _():
        odd = ints[0] == 1
        row = lax.broadcasted_iota(jnp.int32, (size, size), 0)
        col = lax.broadcasted_iota(jnp.int32, (size, size), 1)
        real = lax.broadcasted_iota(jnp.int32, (KP, face), 0) < modes
        for side, pay, got in ((0, pay_a, got_a), (1, pay_b, got_b)):
            cols = slice(side * face, (side + 1) * face)
            residual[:, cols] = pay[:loads, :] + got[:loads, :]
            mine = jnp.where(real, pay[loads:low_row, :], 0.0)
            theirs = jnp.where(real, got[loads:low_row, :], 0.0)
            same = floats[2 + side]
            own_basis[:, cols] = mine
            coarse[:KP, cols] = mine + same * theirs
            coarse[KP : 2 * KP, cols] = (1.0 - same) * theirs
            base = jnp.where(odd, side * half, (1 - side) * half)
            for pair in range(half // 2):
                left = pair * size
                right = (half // 2 + pair) * size
                both = jnp.concatenate(
                    [
                        got[low_row : low_row + mid, left : left + size],
                        got[low_row : low_row + mid, right : right + size],
                    ],
                    axis=0,
                )
                turned = both.T
                diagonal = got[loads + modes : loads + modes + 1, left : left + size]
                upper = jnp.where(row <= col, both, turned)
                lower = jnp.where(row > col, both, jnp.where(row < col, turned, diagonal))
                for k, theirs_block in ((2 * pair, upper), (2 * pair + 1, lower)):
                    pairs[side * half + k, :size, :] = blocks[base + k]
                    pairs[side * half + k, size:, :] = theirs_block.astype(BF16)
        for block in range(count):
            cols = slice(block * size, (block + 1) * size)
            weight = floats[0] if block < half else floats[1]
            modes_here = coarse[: 2 * KP, cols]
            value = jnp.concatenate([residual[:, cols], modes_here], axis=0)
            result = smooth_block(value, weight, pairs[block])
            smooth[:, cols] = result[:loads]
            coarse[2 * KP :, cols] = result[loads:]
            high, low = two_parts(
                jnp.concatenate([result[:loads], modes_here, result[loads:]], axis=0)
            )
            first[:rows, cols] = high
            first[rows:, cols] = low
        vectors = jnp.concatenate([residual[...], smooth[...]], axis=0)
        terms[0] = dot_rows(own_basis[...], vectors)

    def finish(tile, value):
        store_image(tile, floats[4] * value, tiles, image_a, image_b)

    operator_step(
        step, tiles, rows, pick, operator, place, first, second, third, finish
    )

    @pl.when(step == 3 * tiles - 1)
    def _():
        energy = dot_rows(coarse[:, :face], image_a[...]) + dot_rows(coarse[:, face:], image_b[...])
        shared = dot_rows(own_basis[...], coarse[2 * KP :, :])
        terms[1, :, :loads] = energy[:KP, :loads]
        terms[1, :, loads:] = energy[KP : 2 * KP, :loads]
        terms[2, :, :loads] = energy[2 * KP : 3 * KP, :loads]
        terms[2, :, loads:] = energy[3 * KP :, :loads]
        for i in range(2):
            for j in range(2):
                at = (2 * i + j) * 4 * KP
                basis_rows = energy[i * KP : (i + 1) * KP]
                smooth_rows = energy[(2 + i) * KP : (3 + i) * KP]
                basis_cols = slice(loads + j * KP, loads + (j + 1) * KP)
                smooth_cols = slice(loads + (2 + j) * KP, loads + (3 + j) * KP)
                terms[3, :, at : at + KP] = basis_rows[:, basis_cols]
                terms[3, :, at + KP : at + 2 * KP] = basis_rows[:, smooth_cols]
                terms[3, :, at + 2 * KP : at + 3 * KP] = smooth_rows[:, smooth_cols]
                last = shared[:, j * KP : (j + 1) * KP] if i == 0 else jnp.zeros((KP, KP), F32)
                terms[3, :, at + 3 * KP : at + 4 * KP] = last


def coarse_solves(clusters, members, loads, terms, inverse):
    def total(c, kind):
        value = terms[c * members, kind]
        for m in range(1, members):
            value = value + terms[c * members + m, kind]
        return value

    def begin(c, kind):
        return terms[c * members, kind]

    def end(c, kind):
        return terms[c * members + members - 1, kind]

    span = 4 * KP
    lanes = terms.shape[-1]
    totals = [total(c, 0) for c in range(clusters)]
    load_side = [v[:, :loads] for v in totals]
    smooth_side = [v[:, loads:] for v in totals]

    def images(kind):
        found = []
        for c in range(clusters):
            value = total(c, kind)[:, :loads]
            if c + 1 < clusters:
                value = value + begin(c + 1, kind)[:, loads:]
            if c > 0:
                value = value + end(c - 1, kind)[:, loads:]
            found.append(value)
        return found

    centre, below, above = [], [], []
    for c in range(clusters):
        value, under, over = total(c, 3), begin(c, 3), end(c, 3)
        if c + 1 < clusters:
            value = value + pltpu.roll(begin(c + 1, 3), lanes - 3 * span, 1)
            over = over + pltpu.roll(begin(c + 1, 3), lanes - span, 1)
        if c > 0:
            value = value + pltpu.roll(end(c - 1, 3), lanes - 3 * span, 1)
            under = under + pltpu.roll(end(c - 1, 3), lanes - span, 1)
        centre.append(value)
        below.append(under)
        above.append(over)

    def block_times(block, amounts):
        value = block[:, 0:1] * amounts[0:1]
        for k in range(1, KP):
            value = value + block[:, k : k + 1] * amounts[k : k + 1]
        return value

    def times(kind, amounts):
        found = []
        for c in range(clusters):
            near, far = slice(kind * KP, (kind + 1) * KP), slice(span + kind * KP, span + (kind + 1) * KP)
            value = block_times(centre[c][:, near], amounts[c])
            if c > 0:
                value = value + block_times(below[c][:, far], amounts[c - 1])
            if c + 1 < clusters:
                value = value + block_times(above[c][:, far], amounts[c + 1])
            found.append(value)
        return found

    turned_centre = [v.T for v in centre]
    turned_below = [v.T for v in below]
    turned_above = [v.T for v in above]

    def turned_times(kind, amounts):
        found = []
        near, far = slice(kind * KP, (kind + 1) * KP), slice(span + kind * KP, span + (kind + 1) * KP)
        for c in range(clusters):
            value = block_times(turned_centre[c][near], amounts[c])
            if c > 0:
                value = value + block_times(turned_above[c - 1][far], amounts[c - 1])
            if c + 1 < clusters:
                value = value + block_times(turned_below[c + 1][far], amounts[c + 1])
            found.append(value)
        return found

    def solve(parts):
        value = jnp.dot(
            inverse[...], jnp.concatenate(parts, axis=0), precision=EXACT, preferred_element_type=F32
        )
        return [value[c * KP : (c + 1) * KP] for c in range(clusters)]

    def less(left, *others):
        found = list(left)
        for other in others:
            found = [p - q for p, q in zip(found, other)]
        return found

    load_amounts = solve(load_side)
    smooth_amounts = solve(less(smooth_side, times(3, load_amounts)))
    image_amounts = solve(less(images(1), times(1, load_amounts), times(0, smooth_amounts)))
    image_side = less(images(2), times(2, load_amounts), turned_times(1, smooth_amounts))
    smooth_image_amounts = solve(less(image_side, times(3, image_amounts)))
    return load_amounts, smooth_amounts, image_amounts, smooth_image_amounts


def second_kernel(
    clusters, members, tiles,
    ints, floats, terms, inverse, residual, smooth, coarse, pairs, image_a, image_b, got_a, got_b,
    pick, operator, place,
    search, applied, change, next_a, next_b, scalars,
    amounts, columns, first, second, third,
):
    step = pl.program_id(0)
    loads, slots = residual.shape
    face = slots // 2
    count = pairs.shape[0]
    half = count // 2
    size = pairs.shape[2]
    lane = lax.broadcasted_iota(jnp.int32, columns.shape, 1)

    def weighted(left, right):
        product = left * right
        near = jnp.sum(product[:, :face], axis=1, keepdims=True)
        far = jnp.sum(product[:, face:], axis=1, keepdims=True)
        return floats[0] * near + floats[1] * far

    @pl.when(step == 0)
    def _():
        solved = coarse_solves(clusters, members, loads, terms, inverse)
        for kind, parts in enumerate(solved):
            for c, part in enumerate(parts):
                amounts[kind, c] = part

        def local(kind, place_of):
            return [amounts[kind, ints[place_of]], amounts[kind, ints[place_of + 1]]]

        own = jnp.concatenate(local(1, 1) + local(0, 1), axis=0)
        image_own = jnp.concatenate(local(3, 1) + local(2, 1), axis=0)
        projected = residual[...] - dot_modes(own[2 * KP :], coarse[: 2 * KP, :])
        direction = smooth[...] - dot_modes(own, coarse[...])
        search[...] = direction
        for side, image, got in ((0, image_a, got_a), (1, image_b, got_b)):
            theirs = local(1, 3 + 2 * side) + local(0, 3 + 2 * side)
            mixed = jnp.concatenate([own] + theirs, axis=0)
            rows = jnp.concatenate([image[loads:, :], got[loads:, :]], axis=0)
            applied[:, side * face : (side + 1) * face] = (
                image[:loads, :] + got[:loads, :] - dot_modes(mixed, rows)
            )
        image_projected = applied[...] - dot_modes(image_own[2 * KP :], coarse[: 2 * KP, :])
        for block in range(count):
            cols = slice(block * size, (block + 1) * size)
            weight = floats[0] if block < half else floats[1]
            change[:, cols] = smooth_block(applied[:, cols], weight, pairs[block])
        changed = change[...] - dot_modes(image_own, coarse[...])
        change[...] = changed
        high, low = two_parts(changed)
        first[:loads, :] = high
        first[loads:, :] = low
        found = [
            weighted(projected, direction),
            weighted(direction, applied[...]),
            weighted(projected, changed) + weighted(image_projected, direction),
            weighted(image_projected, changed),
        ]
        value = jnp.zeros(columns.shape, F32)
        for k, column in enumerate(found):
            value = jnp.where(lane == k, column, value)
        columns[...] = value

    def finish(tile, value):
        store_image(tile, floats[4] * value, tiles, next_a, next_b)

    operator_step(
        step, tiles, loads, pick, operator, place, first, second, third, finish
    )

    @pl.when(step == 3 * tiles - 1)
    def _():
        value = columns[...]
        for k, vector in ((4, search), (5, change)):
            column = jnp.sum(vector[:, :face] * next_a[...], axis=1, keepdims=True)
            column = column + jnp.sum(vector[:, face:] * next_b[...], axis=1, keepdims=True)
            value = jnp.where(lane == k, column, value)
        turned = value.T
        scalars[...] = turned[:8, :]


def last_kernel(
    ints, scalars, residual, search, applied, change, next_a, next_b, got_a, got_b, out_m, out_r
):
    loads, slots = residual.shape
    face = slots // 2
    total = jnp.sum(scalars[...], axis=0)
    rho = total[0:1]
    gamma = total[1:2]
    alpha = rho / gamma
    rho_next = rho - alpha * total[2:3] + alpha * alpha * total[3:4]
    grow = 1.0 + rho_next / rho
    energy = grow * grow * gamma - 2.0 * grow * alpha * total[4:5] + alpha * alpha * total[5:6]
    alpha_next = rho_next / energy
    lengths = jnp.concatenate(
        [alpha + alpha_next * grow, alpha_next * alpha, jnp.zeros((6, rho.shape[1]), F32)], axis=0
    )
    turned = jnp.concatenate([lengths, jnp.zeros((120, rho.shape[1]), F32)], axis=0).T
    along, against = turned[:loads, 0:1], turned[:loads, 1:2]
    sides = []
    for side, own, got in ((0, next_a, got_a), (1, next_b, got_b)):
        cols = slice(side * face, (side + 1) * face)
        sides.append(
            (
                along * search[:, cols] - against * change[:, cols],
                residual[:, cols] - along * applied[:, cols] + against * (own[...] + got[...]),
            )
        )
    odd = ints[0] == 1
    for k, out in ((0, out_m), (1, out_r)):
        out[:, 0, :] = jnp.where(odd, sides[0][k], sides[1][k])
        out[:, 1, :] = jnp.where(odd, sides[1][k], sides[0][k])


VMEM = pl.BlockSpec(memory_space=pltpu.VMEM)
SMEM = pl.BlockSpec(memory_space=pltpu.SMEM)


def shaped(shape, dtype=F32):
    return jax.ShapeDtypeStruct(shape, dtype)


def whole(shape):
    return pl.BlockSpec(shape, lambda i: (0,) * len(shape))


def per_device(
    dual_load, dual_operator, index_map, stiffness, coarse_basis, dirichlet_blocks, coarse_inverse
):
    loads, _, face = dual_load.shape[2:]
    slots = 2 * face
    modes = coarse_basis.shape[2]
    block_count, size, _ = dirichlet_blocks.shape[2:]
    clusters, members = lax.axis_size("cluster"), lax.axis_size("member")
    devices = clusters * members
    position = lax.axis_index("cluster") * members + lax.axis_index("member")
    int_table, float_table = chain_table(clusters, members)
    ints = lax.dynamic_index_in_dim(jnp.asarray(int_table), position, 0, keepdims=False)
    floats = lax.dynamic_index_in_dim(jnp.asarray(float_table), position, 0, keepdims=False)
    floats = jnp.concatenate([floats, (1.0 / stiffness).reshape(1)])
    load = dual_load.reshape(loads, 2, face)
    basis = coarse_basis.reshape(modes, slots)
    blocks = dirichlet_blocks.reshape(block_count, size, size)

    evens = [(i, i + 1) for i in range(0, devices - 1, 2)]
    odds = [(i, i + 1) for i in range(1, devices - 1, 2)]
    evens = evens + [(j, i) for i, j in evens]
    odds = odds + [(j, i) for i, j in odds]

    def swap(side_a, side_b):
        from_b = lax.ppermute(side_b, AXES, odds)
        from_a = lax.ppermute(side_a, AXES, evens)
        return from_a, from_b

    def share(payload):
        sent = jnp.broadcast_to(payload[None], (devices,) + payload.shape)
        return lax.all_to_all(sent, AXES, 0, 0, tiled=True)

    packed = shaped((loads + KP + size // 2, face))
    pay_a, pay_b = pl.pallas_call(
        functools.partial(pack_kernel, modes),
        out_shape=(packed, packed),
        in_specs=[SMEM, VMEM, VMEM, VMEM],
        out_specs=(VMEM, VMEM),
    )(ints, load, basis, blocks)
    got_a, got_b = swap(pay_a, pay_b)

    by_face = index_map.reshape(2, face)
    flipped = jnp.where(ints[0] == 1, by_face, by_face[::-1]).reshape(slots)
    step_rows = slots // 8
    pick, place = pl.pallas_call(
        order_kernel,
        grid=(8,),
        out_shape=(shaped((slots, slots), BF16), shaped((slots, slots), BF16)),
        in_specs=[pl.BlockSpec((step_rows, 1), lambda i: (i, 0)), whole((1, slots))],
        out_specs=(
            pl.BlockSpec((step_rows, slots), lambda i: (i, 0)),
            pl.BlockSpec((step_rows, slots), lambda i: (i, 0)),
        ),
    )(flipped.reshape(slots, 1), flipped.reshape(1, slots))

    padded = jnp.pad(
        coarse_inverse.reshape(clusters, modes, clusters, modes),
        ((0, 0), (0, KP - modes), (0, 0), (0, KP - modes)),
    ).reshape(clusters * KP, clusters * KP)

    tiles = slots // TILE
    tile_specs = [
        pl.BlockSpec((slots, TILE), lambda i: (0, jnp.clip(i, 0, tiles - 1))),
        pl.BlockSpec((slots, TILE), lambda i: (0, jnp.clip(i - tiles, 0, tiles - 1))),
        pl.BlockSpec((slots, TILE), lambda i: (0, jnp.clip(i - 2 * tiles, 0, tiles - 1))),
    ]
    params = pltpu.CompilerParams(
        dimension_semantics=("arbitrary",), vmem_limit_bytes=48 * 1024 * 1024
    )
    rows = loads + 4 * KP
    pair_shape = (block_count, 2 * size, size)
    residual, smooth, coarse, pairs, image_a, image_b, terms = pl.pallas_call(
        functools.partial(first_kernel, modes, tiles),
        grid=(3 * tiles,),
        out_shape=(
            shaped((loads, slots)),
            shaped((loads, slots)),
            shaped((4 * KP, slots)),
            shaped(pair_shape, BF16),
            shaped((rows, face)),
            shaped((rows, face)),
            shaped((4, KP, 2 * loads)),
        ),
        in_specs=[SMEM, SMEM] + [whole(packed.shape)] * 4 + [whole(blocks.shape)] + tile_specs,
        out_specs=(
            whole((loads, slots)),
            whole((loads, slots)),
            whole((4 * KP, slots)),
            whole(pair_shape),
            whole((rows, face)),
            whole((rows, face)),
            whole((4, KP, 2 * loads)),
        ),
        scratch_shapes=[pltpu.VMEM((KP, slots), F32)] + [pltpu.VMEM((2 * rows, slots), BF16)] * 3,
        compiler_params=params,
    )(ints, floats, pay_a, pay_b, got_a, got_b, blocks, pick, dual_operator, place)

    got_a, got_b = swap(image_a, image_b)
    terms = share(terms)

    vector = whole((loads, slots))
    half_vector = whole((loads, face))
    search, applied, change, next_a, next_b, scalars = pl.pallas_call(
        functools.partial(second_kernel, clusters, members, tiles),
        grid=(3 * tiles,),
        out_shape=(
            shaped((loads, slots)),
            shaped((loads, slots)),
            shaped((loads, slots)),
            shaped((loads, face)),
            shaped((loads, face)),
            shaped((8, loads)),
        ),
        in_specs=[
            SMEM, SMEM, whole(terms.shape), whole(padded.shape), vector, vector,
            whole((4 * KP, slots)), whole(pair_shape),
        ]
        + [whole((rows, face))] * 4
        + tile_specs,
        out_specs=(vector, vector, vector, half_vector, half_vector, whole((8, loads))),
        scratch_shapes=[
            pltpu.VMEM((4, clusters, KP, loads), F32),
            pltpu.VMEM((loads, 128), F32),
        ]
        + [pltpu.VMEM((2 * loads, slots), BF16)] * 3,
        compiler_params=params,
    )(
        ints, floats, terms, padded, residual, smooth, coarse, pairs,
        image_a, image_b, got_a, got_b, pick, dual_operator, place,
    )

    got_a, got_b = swap(next_a, next_b)
    scalars = share(scalars)

    out_m, out_r = pl.pallas_call(
        last_kernel,
        out_shape=(shaped((loads, 2, face)), shaped((loads, 2, face))),
        in_specs=[SMEM] + [VMEM] * 9,
        out_specs=(VMEM, VMEM),
        compiler_params=pltpu.CompilerParams(vmem_limit_bytes=48 * 1024 * 1024),
    )(ints, scalars, residual, search, applied, change, next_a, next_b, got_a, got_b)
    return out_m.reshape(dual_load.shape), out_r.reshape(dual_load.shape)


def solution(mesh):
    in_specs = (
        P("cluster", "member", None, None, None),
        P(),
        P("cluster", "member", None),
        P("cluster", "member"),
        P("cluster", "member", None, None),
        P("cluster", "member", None, None, None),
        P(),
    )
    out_specs = (P("cluster", "member", None, None, None), P("cluster", "member", None, None, None))
    return jax.shard_map(
        per_device, mesh=mesh, in_specs=in_specs, out_specs=out_specs, check_vma=False
    )
```

time: 370 us -> 119 us (0.32); the launches traced: 364 us -> 117 us
  blocking collectives: 205 us -> 15.3 us
  Pallas kernels: 0 us -> 51.4 us
  local copies, waits for them, and re-layouts: 61.7 us -> 19.4 us
  starting transfers between devices: 41.6 us -> 14.5 us
  matrix products: 24.8 us -> 0 us
  other arithmetic: 18.5 us -> 2.25 us
    all_gather x10 -> x0, blocking collectives: 115 us -> none  [the longest x4 52.7 us: coarse_totals(): lax.all_gather(summed[0], 'cluster', axis=1, tiled=True)]
    psum x5 -> x0, blocking collectives: 90.8 us -> none  [coarse_totals(): summed = lax.psum((first, second, scalars), 'member')]
    pallas_call x0 -> x5, Pallas kernels: none -> 51.4 us  [the longest x1 19.8 us: per_device(): pl.pallas_call(functools.partial(second_kernel, clusters, members, tiles)...]
    ppermute x18 -> x6, starting transfers between devices: 41.6 us -> 5.14 us  [the longest x3 3.11 us: swap(): from_a = lax.ppermute(side_a, AXES, evens)]
    gather x6 -> x0, local copies, waits for them, and re-layouts: 35.1 us -> none  [the longest x4 18.3 us: per_device(): jnp.take(product, ordering, axis=1)]
    dot_general x18 -> x0, matrix products: 24.8 us -> none  [the longest x2 14.5 us: per_device(): jnp.dot(local_order, dual_operator, preferred_element_type=jnp.float32)]
    all_to_all x0 -> x1, blocking collectives: none -> 15.3 us  [share(): return lax.all_to_all(sent, AXES, 0, 0, tiled=True)]
    all_to_all x0 -> x1, waiting for transfers between devices: none -> 12.3 us  [share(): return lax.all_to_all(sent, AXES, 0, 0, tiled=True)]
  transfers between devices with their start and end apart: 18 -> 7, of which waited for: 4 -> 2; matrix products, arithmetic and copies ran while one was open for 6% -> 5% of each run, Pallas kernels for 0% -> 7%
where the time goes in v1:
time: 119 us; the launch traced here: 117 us
  Pallas kernels  51.4 us (43%)
  local copies, waits for them, and re-layouts  19.4 us (16%)
  blocking collectives  15.3 us (13%)
  starting transfers between devices  14.5 us (12%)
  waiting for transfers between devices  12.8 us (11%)
  other arithmetic  2.25 us (2%)
  between operations  1.55 us (1%)
    pallas_call x1, Pallas kernels, per_device(): pl.pallas_call(functools.partial(second_kernel, clusters, members, tiles)...  19.8 us
    pallas_call x1, Pallas kernels, per_device(): pl.pallas_call(functools.partial(first_kernel, modes, tiles), grid=(3 * t...  18.3 us
    unnamed x42, local copies, waits for them, and re-layouts  15.5 us
    all_to_all x1, blocking collectives, share(): return lax.all_to_all(sent, AXES, 0, 0, tiled=True)  15.3 us
    all_to_all x1, waiting for transfers between devices, share(): return lax.all_to_all(sent, AXES, 0, 0, tiled=True)  12.3 us
    all_to_all x1, starting transfers between devices, share(): return lax.all_to_all(sent, AXES, 0, 0, tiled=True)  9.37 us
    pallas_call x1, Pallas kernels, per_device(): pl.pallas_call(order_kernel, grid=(8,), out_shape=(shaped((slots, slots),...  8.44 us
    ppermute x3, starting transfers between devices, swap(): from_a = lax.ppermute(side_a, AXES, evens)  3.11 us
  transfers between devices with their start and end apart: 7, of which 2 were waited for; matrix products, arithmetic and copies ran while one was open for 5% of the time, Pallas kernels for 7%

profile of v1, /device:TPU:0, one launch (start us, length us, event | category | flops | bytes accessed | tf_op | source)
XLA Modules:
  0.0 117.3 jit_solution(7697980872212630687)
XLA Ops:
  0.6 1.4 %copy.17 = f32[1,1,6,2048]{3,2,1,0:T(8,128)} copy(f32[1,1,6,2048]{3,1,2,0:T(1,128)} %param.13) | data formatting | bytes 98304
  2.1 1.3 %constant_dynamic-slice_fusion = (s32[1,7]{1,0:T(1,128)S(1)}, s32[7]{0:T(128)}) fusion(s32[32,7]{1,0:T(8,128)} %constant.32.clone, s32[]{:T(128)S(6)} %select_n.14), kind=kLoop, calls=%fused_computation.4 | loop fusion | bytes 88 | tf_op jit(solution)/shard_map/jit(dynamic_index_in_dim)/dynamic_slice | solution.py:473
  3.3 2.4 %shard_map.104 = (f32[136,1024]{1,0:T(8,128)}, f32[136,1024]{1,0:T(8,128)}) custom-call(s32[7]{0:T(128)} %get-tuple-element.41.ints, f32[64,2,1024]{2,1,0:T(2,128)} %bitcast.25, f32[6,2048]{1,0:T(8,128)} %bitcast.26, bf16[16,128,128]{2,1,0:T(8,128)(2,1)} %bitcast.22), custom_call_target="tpu_custom_call" | custom-call | tf_op jit(solution)/shard_map/pallas_call | solution.py:495
  6.2 0.7 collective-permute-start.1
  7.4 1.4 %reduce.3 = s32[2048]{0:T(1024)S(1)} reduce(s32[1,1,2048]{2,1,0:T(1,128)} %param.11, s32[]{:T(128)} %broadcast.7), dimensions={0,1}, to_apply=%param.11.reduce_sub_computation.3 | reduce | bytes 16388 | tf_op args[2]
  9.1 1.4 %copy.14 = s32[1,2048]{0,1:T(8,128)} copy(s32[1,2048]{1,0:T(1,128)S(1)} %bitcast.27) | data formatting | bytes 16384
  10.5 8.4 %shard_map.105 = (bf16[2048,2048]{1,0:T(8,128)(2,1)}, bf16[2048,2048]{1,0:T(8,128)(2,1)}) custom-call(s32[2048,1]{1,0:T(8,128)} %bitcast.24, s32[1,2048]{1,0:T(1,128)} %bitcast.28), custom_call_target="tpu_custom_call" | custom-call | tf_op jit(solution)/shard_map/pallas_call | solution.py:506
  19.6 0.7 dynamic-slice_bitcast_fusion
  20.4 1.0 copy-done
  21.4 1.1 copy-done.2
  22.5 1.1 copy-done.3
  23.5 0.7 copy-done.14
  24.2 18.3 %shard_map.106 = (f32[64,2048]{1,0:T(8,128)S(1)}, f32[64,2048]{1,0:T(8,128)S(1)}, f32[32,2048]{1,0:T(8,128)S(1)}, bf16[16,256,128]{2,1,0:T(8,128)(2,1)S(1)}, f32...) custom-call(s32[7]{0:T(128)S(1)} %copy-done.14, f32[5]{0:T(128)S(1)} %pad_maximum_fusion.floats, ...), custom_call_target="tpu_custom_call" | custom-call | tf_op jit(solution)/shard_map/pallas_call | solution.py:533
  42.5 1.0 copy-done.1
  43.5 0.7 copy-done.12
  44.3 0.9 broadcast_in_dim.4
  45.2 9.4 %all-to-all-start = ((f32[32,4,8,128]{3,2,1,0:T(8,128)}), f32[32,4,8,128]{3,2,1,0:T(8,128)S(1)}, u32[]{:S(2)}, u32[]{:S(2)}) async-start(f32[32,4,8,128]{3,2,1,0:T(8,128)} %broadcast_in_dim.4), calls=%async_computation | async-start | bytes 1048576 | tf_op jit(solution)/shard_map/all_to_all | solution.py:492
  54.9 0.7 collective-permute-start.3
  56.3 0.7 copy-done.8
  57.1 0.7 copy-done.10
  57.8 12.3 %all-to-all-done.terms = f32[32,4,8,128]{3,2,1,0:T(8,128)S(1)} async-done(((f32[32,4,8,128]{3,2,1,0:T(8,128)}), f32[32,4,8,128]{3,2,1,0:T(8,128)S(1)}, u32[]{:S(2)}, u32[]{:S(2)}) %all-to-all-start) | async-done | bytes 524320 | tf_op jit(solution)/shard_map/all_to_all | solution.py:492
  70.1 1.0 copy-done.5
  71.1 1.0 copy-done.7
  72.1 1.0 copy-done.9
  73.1 1.0 copy-done.11
  74.1 0.9 copy-done.13
  75.1 19.8 %shard_map.107 = (f32[64,2048]{1,0:T(8,128)S(1)}, f32[64,2048]{1,0:T(8,128)S(1)}, f32[64,2048]{1,0:T(8,128)S(1)}, f32[64,1024]{1,0:T(8,128)S(1)}, f32[64,1024]{1,0:T(8,128)}, /*index=5*/f32[8,64]{1,0:T(8,128)S(1)}) custom-call(s32[7]{0:T(128)S(1)} %copy-done.15, f32[5]{0:T(128)S(1)} %pad_maximum_fusion.floats, f32[32,4,8,128]{3,2,1,0:T(8,128)S(1)} %all-to-all-done.terms, ...), custom_call_target="tpu_custom_call" | custom-call | tf_op jit(solution)/shard_map/pallas_call | solution.py:564
  94.9 2.3 %collective-permute-start.4 = (f32[64,1024]{1,0:T(8,128)S(1)}, f32[64,1024]{1,0:T(8,128)S(1)}, u32[]{:S(2)}, u32[]{:S(2)}) collective-permute-start(f32[64,1024]{1,0:T(8,128)S(1)} %get-tuple-element.36.next_a), channel_id=1, source_target_pairs={{0,1},{2,3},{4,5},{6,7},{8,9},{10,11},{12,13},{14,15},{16,17},{18,... | collective-permute-start | bytes 786440 | tf_op jit(solution)/shard_map/ppermute | solution.py:487
  97.2 0.7 collective-permute-start.5
  98.0 15.3 %all_to_all.10 = f32[32,1,512]{2,1,0:T(1,128)S(1)} all-to-all(f32[32,1,512]{2,1,0:T(1,128)S(1)} %reshape.55), channel_id=1, replica_groups=mesh['cluster'=4,'member'=8] {'cluster','member'}, dimensions={0} | all-to-all | bytes 131072 | tf_op jit(solution)/shard_map/all_to_all | solution.py:492
  113.9 0.8 reduce.4
  114.8 2.5 %shard_map.108 = (f32[64,2,1024]{2,1,0:T(2,128)}, f32[64,2,1024]{2,1,0:T(2,128)}) custom-call(s32[7]{0:T(128)S(1)} %copy-done.15, f32[32,8,64]{2,1,0:T(8,128)S(1)} %reshape.56.scalars, f32[64,2048]{1,0:T(8,128)S(1)} %get-tuple-element.26.residual, f32[64,2048]{1,0:T(8,128)S(1)} %get-tuple-element.33.search, f32[64,2048]{1,0:T(8,128)S(1)} %get-tuple-element.34.applied, ...), custom_call_target="tpu_custom_call" | custom-call | tf_op jit(solution)/shard_map/pallas_call | solution.py:596
  (44 shorter events, 3.2 us)
Async XLA Ops:
  5.7 14.7 %collective-permute-start = (f32[136,1024]{1,0:T(8,128)}, f32[136,1024]{1,0:T(8,128)S(1)}, u32[]{:S(2)}, u32[]{:S(2)}) collective-permute-start(f32[136,1024]{1,0:T(8,128)} %get-tuple-element.21.pay_a), channel_id=1, source_target_pairs={{0,1},{2,3},{4,5},{6,7},{8,9},{10,11},{12,13},{14,15},{16,17},{18,... | collective-permute-start | bytes 1671176 | tf_op jit(solution)/shard_map/ppermute | solution.py:487
  6.2 14.2 %collective-permute-start.1 = (f32[136,1024]{1,0:T(8,128)}, f32[136,1024]{1,0:T(8,128)S(1)}, u32[]{:S(2)}, u32[]{:S(2)}) collective-permute-start(f32[136,1024]{1,0:T(8,128)} %get-tuple-element.22.pay_b), channel_id=1, source_target_pairs={{1,2},{3,4},{5,6},{7,8},{9,10},{11,12},{13,14},{15,16},{17,18},{19... | collective-permute-start | bytes 1671176 | tf_op jit(solution)/shard_map/ppermute | solution.py:486
  9.1 1.4 %copy-start.16 = (s32[1,1,2,1024]{3,1,2,0:T(1,128)}, s32[1,1,2,1024]{3,1,2,0:T(1,128)S(1)}, u32[]{:S(2)}) copy-start(s32[1,1,2,1024]{3,1,2,0:T(1,128)S(1)} %copy.13) | copy-start | bytes 24580
  20.4 1.0 copy-start
  21.4 1.1 copy-start.2
  22.5 1.1 copy-start.3
  23.5 0.7 copy-start.14
  24.2 31.4 %copy-start.17 = (f32[24,24]{1,0:T(8,128)S(1)}, f32[24,24]{1,0:T(8,128)}, u32[]{:S(2)}) copy-start(f32[24,24]{1,0:T(8,128)} %param.15) | copy-start | bytes 6916
  24.2 45.9 %copy-start.15 = (s32[7]{0:T(128)S(1)}, s32[7]{0:T(128)}, u32[]{:S(2)}) copy-start(s32[7]{0:T(128)} %get-tuple-element.41.ints) | copy-start | bytes 88
  42.5 1.0 copy-start.1
  43.5 0.7 copy-start.12
  44.2 25.9 %copy-start.4 = (f32[96,1024]{1,0:T(8,128)}, f32[96,1024]{1,0:T(8,128)S(1)}, u32[]{:S(2)}) copy-start(f32[96,1024]{1,0:T(8,128)S(1)} %get-tuple-element.30.image_a) | copy-start | bytes 1179652
  44.3 25.9 %copy-start.6 = (f32[96,1024]{1,0:T(8,128)}, f32[96,1024]{1,0:T(8,128)S(1)}, u32[]{:S(2)}) copy-start(f32[96,1024]{1,0:T(8,128)S(1)} %get-tuple-element.31.image_b) | copy-start | bytes 1179652
  45.2 24.9 %all-to-all-start = ((f32[32,4,8,128]{3,2,1,0:T(8,128)}), f32[32,4,8,128]{3,2,1,0:T(8,128)S(1)}, u32[]{:S(2)}, u32[]{:S(2)}) async-start(f32[32,4,8,128]{3,2,1,0:T(8,128)} %broadcast_in_dim.4), calls=%async_computation | async-start | bytes 1048576 | tf_op jit(solution)/shard_map/all_to_all | solution.py:492
  54.6 1.8 %collective-permute-start.2 = (f32[96,1024]{1,0:T(8,128)S(1)}, f32[96,1024]{1,0:T(8,128)S(1)}, u32[]{:S(2)}, u32[]{:S(2)}) collective-permute-start(f32[96,1024]{1,0:T(8,128)S(1)} %get-tuple-element.30.image_a), channel_id=1, source_target_pairs={{0,1},{2,3},{4,5},{6,7},{8,9},{10,11},{12,13},{14,15},{16,17},{18,... | collective-permute-start | bytes 1179656 | tf_op jit(solution)/shard_map/ppermute | solution.py:487
  54.9 2.2 %collective-permute-start.3 = (f32[96,1024]{1,0:T(8,128)S(1)}, f32[96,1024]{1,0:T(8,128)S(1)}, u32[]{:S(2)}, u32[]{:S(2)}) collective-permute-start(f32[96,1024]{1,0:T(8,128)S(1)} %get-tuple-element.31.image_b), channel_id=1, source_target_pairs={{1,2},{3,4},{5,6},{7,8},{9,10},{11,12},{13,14},{15,16},{17,18},{19... | collective-permute-start | bytes 1179656 | tf_op jit(solution)/shard_map/ppermute | solution.py:486
  56.3 0.7 copy-start.8
  57.1 0.7 copy-start.10
  70.1 1.0 copy-start.5
  71.1 1.0 copy-start.7
  72.1 1.0 copy-start.9
  73.1 1.0 copy-start.11
  74.1 0.9 copy-start.13
  94.9 19.9 %collective-permute-start.4 = (f32[64,1024]{1,0:T(8,128)S(1)}, f32[64,1024]{1,0:T(8,128)S(1)}, u32[]{:S(2)}, u32[]{:S(2)}) collective-permute-start(f32[64,1024]{1,0:T(8,128)S(1)} %get-tuple-element.36.next_a), channel_id=1, source_target_pairs={{0,1},{2,3},{4,5},{6,7},{8,9},{10,11},{12,13},{14,15},{16,17},{18,... | collective-permute-start | bytes 786440 | tf_op jit(solution)/shard_map/ppermute | solution.py:487
  97.2 17.6 %collective-permute-start.5 = (f32[64,1024]{1,0:T(8,128)}, f32[64,1024]{1,0:T(8,128)S(1)}, u32[]{:S(2)}, u32[]{:S(2)}) collective-permute-start(f32[64,1024]{1,0:T(8,128)} %get-tuple-element.37.next_b), channel_id=1, source_target_pairs={{1,2},{3,4},{5,6},{7,8},{9,10},{11,12},{13,14},{15,16},{17,18},{19... | collective-permute-start | bytes 786440 | tf_op jit(solution)/shard_map/ppermute | solution.py:486

commit v2 on v0

v2 whole, which is shorter than its diff:
```python
import functools
from typing import NamedTuple

import jax
import jax.numpy as jnp
from jax import lax
from jax.experimental import pallas as pl
from jax.experimental.pallas import tpu as pltpu
from jax.sharding import PartitionSpec as P

AXES = ("cluster", "member")
F32 = jnp.float32
BF16 = jnp.bfloat16
EXACT = lax.Precision.HIGHEST
KP = 8
TILE = 1024


def dot(left, right):
    return jnp.dot(left, right, preferred_element_type=F32)


def dot_rows(left, right):
    return lax.dot_general(left, right, (((1,), (1,)), ((), ())), preferred_element_type=F32)


def two_parts(value):
    high = value.astype(BF16)
    return high, (value - high.astype(F32)).astype(BF16)


def stacked(value):
    return jnp.concatenate(two_parts(value), axis=0)


def folded(value, rows, cols):
    value = value[:rows] + value[rows:]
    return value[:, :cols] + value[:, cols:]


def three_rows(value):
    high, low = two_parts(value)
    return jnp.concatenate([high, low, high], axis=0)


def dot_modes(amounts, rows):
    high, low = two_parts(amounts)
    left = jnp.concatenate([high, high, low], axis=0)
    return lax.dot_general(left, rows, (((0,), (0,)), ((), ())), preferred_element_type=F32)


class Chain(NamedTuple):
    odd: jax.Array
    own: tuple
    near: tuple
    weights: tuple
    same: tuple


def chain(clusters, members):
    count = clusters * members
    position = lax.axis_index("cluster") * members + lax.axis_index("member")
    parity = lax.rem(position, 2)

    def reach(pos):
        cluster, member = lax.div(pos, members), lax.rem(pos, members)
        other = cluster + jnp.where(member == members - 1, 1, jnp.where(member == 0, -1, 0))
        return cluster, jnp.clip(other, 0, clusters - 1)

    own = reach(position)
    near, weights, same = [], [], []
    for partner in (position + 1 - 2 * parity, position - 1 + 2 * parity):
        real = (partner >= 0) & (partner < count)
        there = reach(jnp.clip(partner, 0, count - 1))
        near.append(there)
        weights.append(jnp.where(real, 0.5, 1.0))
        same.append(jnp.where(real & (there[0] == own[0]), 1.0, 0.0))
    return Chain(parity == 1, own, tuple(near), tuple(weights), tuple(same))


def pack_kernel(
    extent,
    far_load, far_basis, far_blocks,
    out_a, out_b, mine,
    load, basis, blocks, arrived,
):
    copies = [
        pltpu.make_async_copy(source, target, arrived.at[k])
        for k, (source, target) in enumerate(
            ((far_load, load), (far_blocks, blocks), (far_basis, basis))
        )
    ]
    for copy in copies:
        copy.start()
    loads, _, face = load.shape
    modes = basis.shape[0]
    half = blocks.shape[0] // 2
    size = blocks.shape[1]
    odd = chain(*extent).odd
    row = lax.broadcasted_iota(jnp.int32, (size, size), 0)
    col = lax.broadcasted_iota(jnp.int32, (size, size), 1)
    mid = size // 2
    low = loads + mid
    copies[0].wait()
    load_0, load_1 = load[:, 0, :], load[:, 1, :]
    out_a[:loads, :] = jnp.where(odd, load_0, load_1)
    out_b[:loads, :] = jnp.where(odd, load_1, load_0)
    for copy in copies[1:]:
        copy.wait()
    for side, out, first in ((0, out_a, odd), (1, out_b, jnp.logical_not(odd))):
        out[low:, :] = jnp.zeros((KP, face), F32)
        for k in range(modes):
            mode = basis[k]
            out[low + k : low + k + 1, :] = jnp.where(first, mode[:, :face], mode[:, face:])
        base = jnp.where(first, 0, half)
        for pair in range(half // 2):
            mine[side * half + 2 * pair] = blocks[base + 2 * pair]
            mine[side * half + 2 * pair + 1] = blocks[base + 2 * pair + 1]
            upper = blocks[base + 2 * pair].astype(F32)
            lower = blocks[base + 2 * pair + 1].astype(F32)
            both = jnp.where(row <= col, upper, lower)
            left = pair * size
            right = (half // 2 + pair) * size
            out[loads:low, left : left + size] = both[:mid]
            out[loads:low, right : right + size] = both[mid:]
            diagonal = jnp.sum(jnp.where(row == col, lower, 0.0), axis=0, keepdims=True)
            out[low + modes : low + modes + 1, left : left + size] = diagonal


def order_kernel(
    extent,
    far_index, far_operator, stiffness,
    pick, place, operator, softness,
    index, arrived,
):
    copies = [
        pltpu.make_async_copy(far_index, index, arrived.at[0]),
        pltpu.make_async_copy(far_operator, operator, arrived.at[1]),
    ]
    for copy in copies:
        copy.start()
    slots = pick.shape[0]
    face = slots // 2
    rows = 128
    odd = chain(*extent).odd
    lane = lax.broadcasted_iota(jnp.int32, (rows, slots), 1)
    depth = lax.broadcasted_iota(jnp.int32, (rows, slots), 0)
    one, zero = jnp.ones((), F32), jnp.zeros((), F32)
    softness[...] = 1.0 / stiffness[...]
    copies[0].wait()
    index_0, index_1 = index[:, :face], index[:, face:]
    wanted = jnp.concatenate(
        [jnp.where(odd, index_0, index_1), jnp.where(odd, index_1, index_0)], axis=1
    )
    for start in range(0, slots, rows):
        here = jnp.broadcast_to(wanted[:, start : start + rows].astype(F32), (rows, rows)).T
        target = jnp.concatenate([here] * (slots // rows), axis=1).astype(jnp.int32)
        pick[start : start + rows, :] = jnp.where(target == lane, one, zero).astype(BF16)
        place[start : start + rows, :] = jnp.where(wanted == depth + start, one, zero).astype(BF16)
    copies[1].wait()


def merge_kernel(keep, got, out):
    kinds, depth, lanes = keep.shape
    rows = got.shape[0] - depth
    for kind in range(kinds):
        value = keep[kind] + got[rows:, kind * lanes : (kind + 1) * lanes]
        out[:, kind * depth : (kind + 1) * depth, :] = jnp.broadcast_to(
            value[None], (out.shape[0], depth, lanes)
        )


def operator_apply(rows, scale, pick, operator, place, first, second, third, image_a, image_b):
    slots = first.shape[1]
    face = slots // 2

    @pl.loop(0, slots // TILE)
    def _(tile):
        cols = pl.ds(pl.multiple_of(tile * TILE, TILE), TILE)
        second[:, cols] = dot(first[...], pick[:, cols]).astype(BF16)

    @pl.loop(0, slots // TILE)
    def _(tile):
        cols = pl.ds(pl.multiple_of(tile * TILE, TILE), TILE)
        product = dot(second[...], operator[:, cols])
        high, low = two_parts(product[:rows] + product[rows:])
        third[:rows, cols] = high
        third[rows:, cols] = low

    for side, image in ((0, image_a), (1, image_b)):
        product = dot(third[...], place[:, side * face : (side + 1) * face])
        image[:rows, :] = scale * (product[:rows] + product[rows:])


def smooth_block(value, weight, block_pair):
    rows = value.shape[0]
    high, low = two_parts(weight * value)
    left = jnp.concatenate(
        [jnp.concatenate([high, high], axis=1), jnp.concatenate([low, low], axis=1)], axis=0
    )
    product = dot(left, block_pair)
    return weight * (product[:rows] + product[rows:])


def first_kernel(
    extent, modes,
    softness, pay_a, pay_b, got_a, got_b, blocks, pick, operator, place,
    residual, smooth, coarse, pairs, image_a, image_b, keep,
    first, second, third, terms,
):
    loads, slots = residual.shape
    face = slots // 2
    count = pairs.shape[0]
    half = count // 2
    size = pairs.shape[2]
    rows = loads + 4 * KP
    mid = size // 2
    low = loads + mid
    here = chain(*extent)
    odd = here.odd
    row = lax.broadcasted_iota(jnp.int32, (size, size), 0)
    col = lax.broadcasted_iota(jnp.int32, (size, size), 1)
    real = lax.broadcasted_iota(jnp.int32, (KP, face), 0) < modes
    own_basis, span = [], []
    for side, pay, got in ((0, pay_a, got_a), (1, pay_b, got_b)):
        cols = slice(side * face, (side + 1) * face)
        residual[:, cols] = pay[:loads, :] + got[:loads, :]
        mine = jnp.where(real, pay[low:, :], 0.0)
        theirs = jnp.where(real, got[low:, :], 0.0)
        same = here.same[side]
        own_basis.append(mine)
        span.append(jnp.concatenate([mine + same * theirs, (1.0 - same) * theirs], axis=0))
        for pair in range(half // 2):
            left = pair * size
            right = (half // 2 + pair) * size
            both = jnp.concatenate(
                [got[loads:low, left : left + size], got[loads:low, right : right + size]], axis=0
            )
            turned = both.T
            diagonal = got[low + modes : low + modes + 1, left : left + size]
            upper = jnp.where(row <= col, both, turned)
            lower = jnp.where(row > col, both, jnp.where(row < col, turned, diagonal))
            for k, theirs_block in ((2 * pair, upper), (2 * pair + 1, lower)):
                pairs[side * half + k, :size, :] = blocks[side * half + k]
                pairs[side * half + k, size:, :] = theirs_block.astype(BF16)
    for block in range(count):
        side, k = divmod(block, half)
        cols = slice(block * size, (block + 1) * size)
        modes_here = span[side][:, k * size : (k + 1) * size]
        value = jnp.concatenate([residual[:, cols], modes_here], axis=0)
        result = smooth_block(value, here.weights[side], pairs[block])
        smooth[:, cols] = result[:loads]
        high, low = two_parts(jnp.concatenate([result[:loads], modes_here, result[loads:]], axis=0))
        first[:rows, cols] = high
        first[rows:, cols] = low
        coarse[: 4 * KP, cols] = high[loads:]
        coarse[4 * KP : 8 * KP, cols] = low[loads:]
        coarse[8 * KP :, cols] = high[loads:]

    operator_apply(
        rows, softness[...], pick, operator, place, first, second, third, image_a, image_b
    )

    basis = stacked(jnp.concatenate(own_basis, axis=1))
    load_side = folded(dot_rows(basis, stacked(residual[...])), KP, loads)
    smooth_side = folded(dot_rows(basis, first[...]), KP, rows)
    shared = smooth_side[:, loads + 2 * KP :]
    energy = jnp.zeros((8 * KP, 2 * rows), F32)
    for side, image in ((0, image_a), (1, image_b)):
        cols = slice(side * face, (side + 1) * face)
        energy = energy + dot_rows(coarse[: 8 * KP, cols], stacked(image[:rows, :]))
    energy = folded(energy, 4 * KP, rows)
    terms[0, :, :loads] = load_side
    terms[0, :, loads:] = smooth_side[:, :loads]
    terms[1, :, :loads] = energy[:KP, :loads]
    terms[1, :, loads:] = energy[KP : 2 * KP, :loads]
    terms[2, :, :loads] = energy[2 * KP : 3 * KP, :loads]
    terms[2, :, loads:] = energy[3 * KP :, :loads]
    for i in range(2):
        for j in range(2):
            at = (2 * i + j) * 4 * KP
            basis_rows = energy[i * KP : (i + 1) * KP]
            smooth_rows = energy[(2 + i) * KP : (3 + i) * KP]
            basis_cols = slice(loads + j * KP, loads + (j + 1) * KP)
            smooth_cols = slice(loads + (2 + j) * KP, loads + (3 + j) * KP)
            terms[3, :, at : at + KP] = basis_rows[:, basis_cols]
            terms[3, :, at + KP : at + 2 * KP] = basis_rows[:, smooth_cols]
            terms[3, :, at + 2 * KP : at + 3 * KP] = smooth_rows[:, smooth_cols]
            last = shared[:, j * KP : (j + 1) * KP] if i == 0 else jnp.zeros((KP, KP), F32)
            terms[3, :, at + 3 * KP : at + 4 * KP] = last
    keep[...] = jnp.where(odd, terms[2:], terms[:2])
    image_a[rows:, :] = jnp.zeros((KP, face), F32)
    for kind in range(2):
        image_a[rows:, kind * 2 * loads : (kind + 1) * 2 * loads] = jnp.where(
            odd, terms[kind], terms[2 + kind]
        )


def coarse_solves(clusters, members, loads, odd, terms, other_terms, inverse):
    def pick_kind(kind, mine, theirs):
        return jnp.where(odd, theirs, mine) if kind < 2 else jnp.where(odd, mine, theirs)

    def rows_of(kind):
        return slice(kind % 2 * KP, kind % 2 * KP + KP)

    def total(c, kind):
        pairs = members // 2
        found = [ref[c * pairs, rows_of(kind)] for ref in (terms, other_terms)]
        for m in range(1, pairs):
            found = [
                v + ref[c * pairs + m, rows_of(kind)]
                for v, ref in zip(found, (terms, other_terms))
            ]
        return pick_kind(kind, *found)

    def one(pair, kind):
        return pick_kind(kind, terms[pair, rows_of(kind)], other_terms[pair, rows_of(kind)])

    def begin(c, kind):
        return one(c * members // 2, kind)

    def end(c, kind):
        return one((c + 1) * members // 2 - 1, kind)

    span = 4 * KP
    lanes = terms.shape[-1]
    totals = [total(c, 0) for c in range(clusters)]
    load_side = [v[:, :loads] for v in totals]
    smooth_side = [v[:, loads:] for v in totals]

    def images(kind):
        found = []
        for c in range(clusters):
            value = total(c, kind)[:, :loads]
            if c + 1 < clusters:
                value = value + begin(c + 1, kind)[:, loads:]
            if c > 0:
                value = value + end(c - 1, kind)[:, loads:]
            found.append(value)
        return found

    centre, below, above = [], [], []
    for c in range(clusters):
        value, under, over = total(c, 3), begin(c, 3), end(c, 3)
        if c + 1 < clusters:
            value = value + pltpu.roll(begin(c + 1, 3), lanes - 3 * span, 1)
            over = over + pltpu.roll(begin(c + 1, 3), lanes - span, 1)
        if c > 0:
            value = value + pltpu.roll(end(c - 1, 3), lanes - 3 * span, 1)
            under = under + pltpu.roll(end(c - 1, 3), lanes - span, 1)
        centre.append(value)
        below.append(under)
        above.append(over)

    def block_times(block, amounts):
        value = block[:, 0:1] * amounts[0:1]
        for k in range(1, KP):
            value = value + block[:, k : k + 1] * amounts[k : k + 1]
        return value

    def times(kind, amounts):
        found = []
        for c in range(clusters):
            near, far = slice(kind * KP, (kind + 1) * KP), slice(span + kind * KP, span + (kind + 1) * KP)
            value = block_times(centre[c][:, near], amounts[c])
            if c > 0:
                value = value + block_times(below[c][:, far], amounts[c - 1])
            if c + 1 < clusters:
                value = value + block_times(above[c][:, far], amounts[c + 1])
            found.append(value)
        return found

    turned_centre = [v.T for v in centre]
    turned_below = [v.T for v in below]
    turned_above = [v.T for v in above]

    def turned_times(kind, amounts):
        found = []
        near, far = slice(kind * KP, (kind + 1) * KP), slice(span + kind * KP, span + (kind + 1) * KP)
        for c in range(clusters):
            value = block_times(turned_centre[c][near], amounts[c])
            if c > 0:
                value = value + block_times(turned_above[c - 1][far], amounts[c - 1])
            if c + 1 < clusters:
                value = value + block_times(turned_below[c + 1][far], amounts[c + 1])
            found.append(value)
        return found

    modes = inverse.shape[0] // clusters
    row = lax.broadcasted_iota(jnp.int32, (clusters * KP, clusters * modes), 0)
    col = lax.broadcasted_iota(jnp.int32, (clusters * KP, clusters * modes), 1)
    mode = row % KP
    spread = jnp.where((mode < modes) & (col == row // KP * modes + mode), 1.0, 0.0)
    padded = jnp.dot(spread, inverse[...], precision=EXACT, preferred_element_type=F32)
    padded = lax.dot_general(
        padded, spread, (((1,), (1,)), ((), ())), precision=EXACT, preferred_element_type=F32
    )

    def solve(parts):
        value = jnp.dot(
            padded, jnp.concatenate(parts, axis=0), precision=EXACT, preferred_element_type=F32
        )
        return [value[c * KP : (c + 1) * KP] for c in range(clusters)]

    def less(left, *others):
        found = list(left)
        for other in others:
            found = [p - q for p, q in zip(found, other)]
        return found

    load_amounts = solve(load_side)
    smooth_amounts = solve(less(smooth_side, times(3, load_amounts)))
    image_amounts = solve(less(images(1), times(1, load_amounts), times(0, smooth_amounts)))
    image_side = less(images(2), times(2, load_amounts), turned_times(1, smooth_amounts))
    smooth_image_amounts = solve(less(image_side, times(3, image_amounts)))
    return load_amounts, smooth_amounts, image_amounts, smooth_image_amounts


def second_kernel(
    extent,
    softness, terms, other_terms, inverse, residual, smooth, coarse, pairs, image_a, image_b, got_a, got_b,
    pick, operator, place,
    search, applied, change, next_a, next_b, scalars,
    amounts, first, second, third,
):
    loads, slots = residual.shape
    face = slots // 2
    count = pairs.shape[0]
    half = count // 2
    size = pairs.shape[2]
    clusters, members = extent
    here = chain(*extent)

    def weighted(left, right):
        product = left * right
        near = jnp.sum(product[:, :face], axis=1, keepdims=True)
        far = jnp.sum(product[:, face:], axis=1, keepdims=True)
        return here.weights[0] * near + here.weights[1] * far

    solved = coarse_solves(clusters, members, loads, here.odd, terms, other_terms, inverse)
    for kind, parts in enumerate(solved):
        for c, part in enumerate(parts):
            amounts[kind, c] = part

    def local(kind, reached):
        return [amounts[kind, c] for c in reached]

    none = [jnp.zeros((2 * KP, loads), F32)]
    own = jnp.concatenate(local(1, here.own) + local(0, here.own), axis=0)
    image_own = jnp.concatenate(local(3, here.own) + local(2, here.own), axis=0)
    own_basis = jnp.concatenate(local(0, here.own) + none, axis=0)
    image_own_basis = jnp.concatenate(local(2, here.own) + none, axis=0)
    projected = residual[...] - dot_modes(own_basis, coarse[...])
    direction = smooth[...] - dot_modes(own, coarse[...])
    search[...] = direction
    for side, image, got in ((0, image_a, got_a), (1, image_b, got_b)):
        theirs = local(1, here.near[side]) + local(0, here.near[side])
        mixed = jnp.concatenate([own] + theirs, axis=0)
        rows = slice(loads, loads + 4 * KP)
        rows = three_rows(jnp.concatenate([image[rows, :], got[rows, :]], axis=0))
        applied[:, side * face : (side + 1) * face] = (
            image[:loads, :] + got[:loads, :] - dot_modes(mixed, rows)
        )
    image_projected = applied[...] - dot_modes(image_own_basis, coarse[...])
    for block in range(count):
        cols = slice(block * size, (block + 1) * size)
        weight = here.weights[block // half]
        change[:, cols] = smooth_block(applied[:, cols], weight, pairs[block])
    changed = change[...] - dot_modes(image_own, coarse[...])
    change[...] = changed
    high, low = two_parts(changed)
    first[:loads, :] = high
    first[loads:, :] = low
    found = [
        weighted(projected, direction),
        weighted(direction, applied[...]),
        weighted(projected, changed) + weighted(image_projected, direction),
        weighted(image_projected, changed),
    ]

    operator_apply(
        loads, softness[...], pick, operator, place, first, second, third, next_a, next_b
    )

    for vector in (search, change):
        column = jnp.sum(vector[:, :face] * next_a[...], axis=1, keepdims=True)
        column = column + jnp.sum(vector[:, face:] * next_b[...], axis=1, keepdims=True)
        found.append(column)
    lane = lax.broadcasted_iota(jnp.int32, (loads, 128), 1)
    value = jnp.zeros(lane.shape, F32)
    for k, column in enumerate(found):
        value = jnp.where(lane == k, column, value)
    turned = value.T
    scalars[:, :loads] = turned[:4, :]
    scalars[:, loads:] = turned[4:8, :]


def last_kernel(
    extent, scalars, residual, search, applied, change, next_a, next_b, got_a, got_b, out_m, out_r
):
    loads, slots = residual.shape
    face = slots // 2
    total = jnp.sum(scalars[...], axis=0)
    total = jnp.concatenate([total[:, :loads], total[:, loads:]], axis=0)
    rho = total[0:1]
    gamma = total[1:2]
    alpha = rho / gamma
    rho_next = rho - alpha * total[2:3] + alpha * alpha * total[3:4]
    grow = 1.0 + rho_next / rho
    energy = grow * grow * gamma - 2.0 * grow * alpha * total[4:5] + alpha * alpha * total[5:6]
    alpha_next = rho_next / energy
    lengths = jnp.concatenate(
        [alpha + alpha_next * grow, alpha_next * alpha, jnp.zeros((6, rho.shape[1]), F32)], axis=0
    )
    turned = jnp.concatenate([lengths, jnp.zeros((120, rho.shape[1]), F32)], axis=0).T
    along, against = turned[:loads, 0:1], turned[:loads, 1:2]
    sides = []
    for side, own, got in ((0, next_a, got_a), (1, next_b, got_b)):
        cols = slice(side * face, (side + 1) * face)
        sides.append(
            (
                along * search[:, cols] - against * change[:, cols],
                residual[:, cols] - along * applied[:, cols] + against * (own[...] + got[...]),
            )
        )
    odd = chain(*extent).odd
    for k, out in ((0, out_m), (1, out_r)):
        out[:, 0, :] = jnp.where(odd, sides[0][k], sides[1][k])
        out[:, 1, :] = jnp.where(odd, sides[1][k], sides[0][k])


VMEM = pl.BlockSpec(memory_space=pltpu.VMEM)
HBM = pl.BlockSpec(memory_space=pltpu.HBM)


def shaped(shape, dtype=F32):
    return jax.ShapeDtypeStruct(shape, dtype)


def in_hbm(value):
    return pltpu.with_memory_space_constraint(value, pltpu.HBM)


def per_device(
    dual_load, dual_operator, index_map, stiffness, coarse_basis, dirichlet_blocks, coarse_inverse
):
    loads, _, face = dual_load.shape[2:]
    slots = 2 * face
    modes = coarse_basis.shape[2]
    block_count, size, _ = dirichlet_blocks.shape[2:]
    clusters, members = lax.axis_size("cluster"), lax.axis_size("member")
    devices = clusters * members
    extent = clusters, members
    load = dual_load.reshape(loads, 2, face)
    basis = coarse_basis.reshape(modes, 1, slots)
    blocks = dirichlet_blocks.reshape(block_count, size, size)

    evens = [(i, i + 1) for i in range(0, devices - 1, 2)]
    odds = [(i, i + 1) for i in range(1, devices - 1, 2)]
    evens = evens + [(j, i) for i, j in evens]
    odds = odds + [(j, i) for i, j in odds]

    def swap(side_a, side_b):
        from_b = lax.ppermute(side_b, AXES, odds)
        from_a = lax.ppermute(side_a, AXES, evens)
        return from_a, from_b

    def share(copies, groups=None):
        return lax.all_to_all(copies, AXES, 0, 0, axis_index_groups=groups, tiled=True)

    def params(mebibytes):
        return pltpu.CompilerParams(vmem_limit_bytes=mebibytes * 1024 * 1024)

    half_vector = shaped((loads, face))
    vector = shaped((loads, slots))
    packed = shaped((loads + size // 2 + KP, face))
    pay_a, pay_b, mine = pl.pallas_call(
        functools.partial(pack_kernel, extent),
        out_shape=(packed, packed, shaped(blocks.shape, BF16)),
        in_specs=[HBM] * 3,
        out_specs=(VMEM,) * 3,
        scratch_shapes=[
            pltpu.VMEM(load.shape, F32),
            pltpu.VMEM(basis.shape, F32),
            pltpu.VMEM(blocks.shape, BF16),
            pltpu.SemaphoreType.DMA((3,)),
        ],
        compiler_params=params(8),
    )(*[in_hbm(v) for v in (load, basis, blocks)])
    got_a, got_b = swap(pay_a, pay_b)

    ordering = shaped((slots, slots), BF16)
    pick, place, operator, softness = pl.pallas_call(
        functools.partial(order_kernel, extent),
        out_shape=(ordering, ordering, ordering, shaped((1, 1))),
        in_specs=[HBM, HBM, VMEM],
        out_specs=(VMEM,) * 4,
        scratch_shapes=[pltpu.VMEM((1, slots), jnp.int32), pltpu.SemaphoreType.DMA((2,))],
        compiler_params=params(8),
    )(in_hbm(index_map.reshape(1, slots)), in_hbm(dual_operator), stiffness)
    pick, operator, place = [
        pltpu.with_memory_space_constraint(v, pltpu.VMEM) for v in (pick, operator, place)
    ]

    rows = loads + 4 * KP
    residual, smooth, coarse, pairs, image_a, image_b, keep = pl.pallas_call(
        functools.partial(first_kernel, extent, modes),
        out_shape=(
            vector,
            vector,
            shaped((12 * KP, slots), BF16),
            shaped((block_count, 2 * size, size), BF16),
            shaped((rows + KP, face)),
            shaped((rows, face)),
            shaped((2, KP, 2 * loads)),
        ),
        in_specs=[VMEM] * 9,
        out_specs=(VMEM,) * 7,
        scratch_shapes=[pltpu.VMEM((2 * rows, slots), BF16)] * 3
        + [pltpu.VMEM((4, KP, 2 * loads), F32)],
        compiler_params=params(20),
    )(softness, pay_a, pay_b, got_a, got_b, mine, pick, operator, place)

    got_a, got_b = swap(image_a, image_b)
    terms = pl.pallas_call(
        merge_kernel,
        out_shape=shaped((devices // 2, 2 * KP, 2 * loads)),
        in_specs=[VMEM] * 2,
        out_specs=VMEM,
        compiler_params=params(8),
    )(keep, got_a)
    terms = share(terms, [list(range(k, devices, 2)) for k in range(2)])
    other_terms = lax.ppermute(terms, AXES, evens)

    search, applied, change, next_a, next_b, scalars = pl.pallas_call(
        functools.partial(second_kernel, extent),
        out_shape=(vector, vector, vector, half_vector, half_vector, shaped((4, 2 * loads))),
        in_specs=[VMEM] * 15,
        out_specs=(VMEM,) * 6,
        scratch_shapes=[pltpu.VMEM((4, clusters, KP, loads), F32)]
        + [pltpu.VMEM((2 * loads, slots), BF16)] * 3,
        compiler_params=params(20),
    )(
        softness, terms, other_terms, coarse_inverse, residual, smooth, coarse, pairs,
        image_a, image_b, got_a, got_b, pick, operator, place,
    )

    got_a, got_b = swap(next_a, next_b)
    scalars = share(jnp.broadcast_to(scalars[None], (devices,) + scalars.shape))

    out_m, out_r = pl.pallas_call(
        functools.partial(last_kernel, extent),
        out_shape=(shaped((loads, 2, face)), shaped((loads, 2, face))),
        in_specs=[VMEM] * 9,
        out_specs=(VMEM, VMEM),
        compiler_params=params(20),
    )(scalars, residual, search, applied, change, next_a, next_b, got_a, got_b)
    return out_m.reshape(dual_load.shape), out_r.reshape(dual_load.shape)


def solution(mesh):
    in_specs = (
        P("cluster", "member", None, None, None),
        P(),
        P("cluster", "member", None),
        P("cluster", "member"),
        P("cluster", "member", None, None),
        P("cluster", "member", None, None, None),
        P(),
    )
    out_specs = (P("cluster", "member", None, None, None), P("cluster", "member", None, None, None))
    return jax.shard_map(
        per_device, mesh=mesh, in_specs=in_specs, out_specs=out_specs, check_vma=False
    )
```

time: 370 us -> 74.6 us (0.20); the launches traced: 364 us -> 74.3 us
  blocking collectives: 205 us -> 30.6 us
  local copies, waits for them, and re-layouts: 61.7 us -> 6.61 us
  starting transfers between devices: 41.6 us -> 9.99 us
  matrix products: 24.8 us -> 0 us
  Pallas kernels: 0 us -> 23.7 us
  other arithmetic: 18.5 us -> 0 us
  waiting for transfers between devices: 9.38 us -> 2.07 us
    all_gather x10 -> x0, blocking collectives: 115 us -> none  [the longest x4 52.7 us: coarse_totals(): lax.all_gather(summed[0], 'cluster', axis=1, tiled=True)]
    psum x5 -> x0, blocking collectives: 90.8 us -> none  [coarse_totals(): summed = lax.psum((first, second, scalars), 'member')]
    gather x6 -> x0, local copies, waits for them, and re-layouts: 35.1 us -> none  [the longest x4 18.3 us: per_device(): jnp.take(product, ordering, axis=1)]
    ppermute x18 -> x7, starting transfers between devices: 41.6 us -> 9.99 us  [the longest x3 7.96 us: swap(): from_a = lax.ppermute(side_a, AXES, evens)]
    all_to_all x0 -> x2, blocking collectives: none -> 30.6 us  [share(): lax.all_to_all(copies, AXES, 0, 0, axis_index_groups=groups, tiled=True)]
    dot_general x18 -> x0, matrix products: 24.8 us -> none  [the longest x2 14.5 us: per_device(): jnp.dot(local_order, dual_operator, preferred_element_type=jnp.float32)]
    pallas_call x0 -> x6, Pallas kernels: none -> 23.7 us  [the longest x1 7.95 us: per_device(): pl.pallas_call(functools.partial(first_kernel, extent, modes), out_shape=...]
    scatter x1 -> x0, local copies, waits for them, and re-layouts: 8.74 us -> none  [per_device(): inverse = jnp.zeros((slot_count,), jnp.int32).at[ordering].set(jnp.arange...]
  transfers between devices with their start and end apart: 18 -> 7, of which waited for: 4 -> 2; matrix products, arithmetic and copies ran while one was open for 6% -> 0% of each run, Pallas kernels for 0% -> 7%
where the time goes in v2:
time: 74.6 us; the launch traced here: 74.3 us
  blocking collectives  30.6 us (41%)
  Pallas kernels  23.7 us (32%)
  starting transfers between devices  9.99 us (13%)
  local copies, waits for them, and re-layouts  6.61 us (9%)
  waiting for transfers between devices  2.07 us (3%)
  between operations  1.36 us (2%)
    all_to_all x2, blocking collectives, share(): lax.all_to_all(copies, AXES, 0, 0, axis_index_groups=groups, tiled=True)  30.6 us
    ppermute x3, starting transfers between devices, swap(): from_a = lax.ppermute(side_a, AXES, evens)  7.96 us
    pallas_call x1, Pallas kernels, per_device(): pl.pallas_call(functools.partial(first_kernel, extent, modes), out_shape=...  7.95 us
    pallas_call x1, Pallas kernels, per_device(): pl.pallas_call(functools.partial(second_kernel, extent), out_shape=(vecto...  7.63 us
    unnamed x6, local copies, waits for them, and re-layouts  6.6 us
    pallas_call x1, Pallas kernels, per_device(): pl.pallas_call(functools.partial(order_kernel, extent), out_shape=(orderi...  5.15 us
    ppermute x3, starting transfers between devices, swap(): from_b = lax.ppermute(side_b, AXES, odds)  2.02 us
    pallas_call x1, Pallas kernels, per_device(): pl.pallas_call(functools.partial(last_kernel, extent), out_shape=(shaped(...  1.61 us
  transfers between devices with their start and end apart: 7, of which 2 were waited for; matrix products, arithmetic and copies ran while one was open for 0% of the time, Pallas kernels for 7%

profile of v2, /device:TPU:0, one launch (start us, length us, event | category | flops | bytes accessed | tf_op | source)
XLA Modules:
  0.0 74.3 jit_solution(15931460641409531302)
XLA Ops:
  0.6 1.4 %shard_map.87 = (f32[136,1024]{1,0:T(8,128)S(1)}, f32[136,1024]{1,0:T(8,128)S(1)}, bf16[16,128,128]{2,1,0:T(8,128)(2,1)S(1)}) custom-call(f32[64,2,1024]{2,1,0:T(2,128)} %bitcast.6, f32[6,1,2048]{2,1,0:T(1,128)} %bitcast.8, bf16[16,128,128]{2,1,0:T(8,128)(2,1)} %bitcast.7), custom_call_target="tpu_custom_call" | custom-call | tf_op jit(solution)/shard_map/pallas_call | solution.py:577
  2.0 0.5 collective-permute-start
  2.5 0.7 collective-permute-start.1
  3.9 5.1 %shard_map.86 = (bf16[2048,2048]{1,0:T(8,128)(2,1)S(1)}, bf16[2048,2048]{1,0:T(8,128)(2,1)S(1)}, bf16[2048,2048]{1,0:T(8,128)(2,1)S(1)}, f32[1,1]{1,0:T(1,128)}) custom-call(s32[1,2048]{1,0:T(1,128)} %bitcast.9, bf16[2048,2048]{1,0:T(8,128)(2,1)} %far_operator.1, f32[1,1]{1,0:T(1,128)S(6)} %copy.9.stiffness), custom_call_target="tpu_custom_call" | custom-call | tf_op jit(solution)/shard_map/pallas_call | solution.py:593
  9.0 0.0 copy-start
  9.0 3.2 %copy-done = bf16[2048,2048]{1,0:T(8,128)(2,1)} copy-done((bf16[2048,2048]{1,0:T(8,128)(2,1)}, bf16[2048,2048]{1,0:T(8,128)(2,1)S(1)}, u32[]{:S(2)}) %copy-start) | copy-done | bytes 8388632
  12.3 0.0 collective-permute-done.got_a
  12.3 0.0 collective-permute-done.1.got_b
  12.3 0.0 copy-start.1
  12.3 3.4 %copy-done.1 = bf16[2048,2048]{1,0:T(8,128)(2,1)S(1)} copy-done((bf16[2048,2048]{1,0:T(8,128)(2,1)S(1)}, bf16[2048,2048]{1,0:T(8,128)(2,1)}, u32[]{:S(2)}) %copy-start.1) | copy-done | bytes 8388632
  15.6 0.0 copy-start.2
  15.6 7.9 %shard_map.88 = (f32[64,2048]{1,0:T(8,128)S(1)}, f32[64,2048]{1,0:T(8,128)S(1)}, bf16[96,2048]{1,0:T(8,128)(2,1)S(1)}, bf16[16,256,128]{2,1,0:T(8,128)(2,1)S(1)}...) custom-call(f32[1,1]{1,0:T(1,128)} %get-tuple-element.24.softness, ...), custom_call_target="tpu_custom_call" | custom-call | tf_op jit(solution)/shard_map/pallas_call | solution.py:606
  23.6 7.3 %collective-permute-start.2 = (f32[104,1024]{1,0:T(8,128)S(1)}, f32[104,1024]{1,0:T(8,128)S(1)}, u32[]{:S(2)}, u32[]{:S(2)}) collective-permute-start(f32[104,1024]{1,0:T(8,128)S(1)} %get-tuple-element.32.image_a), channel_id=1, source_target_pairs={{0,1},{2,3},{4,5},{6,7},{8,9},{10,11},{12,13},{14,15},{16,17},{18,... | collective-permute-start | bytes 1277960 | tf_op jit(solution)/shard_map/ppermute | solution.py:565
  30.9 0.7 collective-permute-start.4
  31.6 0.7 collective-permute-done.2.got.got_a
  32.3 17.1 %all_to_all.10.terms = f32[16,16,128]{2,1,0:T(8,128)S(1)} all-to-all(f32[16,16,128]{2,1,0:T(8,128)S(1)} %shard_map.89), channel_id=1, replica_groups={{0,2,4,6,8,10,12,14,16,18,20,22,24,26,28,30},{1,3,5,7,9,11,13,15,17,19,..., dimensions={0} | all-to-all | bytes 262144 | tf_op jit(solution)/shard_map/all_to_all | solution.py:569
  49.4 0.0 collective-permute-start.3
  49.4 0.0 collective-permute-done.4.got_b
  49.4 1.3 %collective-permute-done.3.other_terms = f32[16,16,128]{2,1,0:T(8,128)S(1)} collective-permute-done((f32[16,16,128]{2,1,0:T(8,128)S(1)}, f32[16,16,128]{2,1,0:T(8,128)S(1)}, u32[]{:S(2)}, u32[]{:S(2)}) %collective-permute-start.3) | collective-permute-done | bytes 131104 | tf_op jit(solution)/shard_map/ppermute | solution.py:633
  50.8 0.0 copy-done.2
  50.8 7.6 %shard_map.90 = (f32[64,2048]{1,0:T(8,128)S(1)}, f32[64,2048]{1,0:T(8,128)S(1)}, f32[64,2048]{1,0:T(8,128)S(1)}, f32[64,1024]{1,0:T(8,128)S(1)}, f32[64,1024]{1,0:T(8,128)S(1)}, /*index=5*/f32[4,128]{1,0:T(4,128)S(1)}) custom-call(f32[1,1]{1,0:T(1,128)} %get-tuple-element.24.softness, f32[16,16,128]{2,1,0:T(8,128)S(1)} %all_to_all.10.terms, ...), custom_call_target="tpu_custom_call" | custom-call | tf_op jit(solution)/shard_map/pallas_call | solution.py:635
  58.4 0.2 collective-permute-start.5
  58.6 0.7 collective-permute-start.6
  59.2 13.5 %all_to_all.11.scalars = f32[32,4,128]{2,1,0:T(4,128)S(1)} all-to-all(f32[32,4,128]{2,1,0:T(4,128)S(1)} %broadcast_in_dim.2), channel_id=1, replica_groups=mesh['cluster'=4,'member'=8] {'cluster','member'}, dimensions={0} | all-to-all | bytes 131072 | tf_op jit(solution)/shard_map/all_to_all | solution.py:569
  72.7 0.0 collective-permute-done.5.got_a
  72.7 0.0 collective-permute-done.6.got_b
  72.7 1.6 %shard_map.91 = (f32[64,2,1024]{2,1,0:T(2,128)}, f32[64,2,1024]{2,1,0:T(2,128)}) custom-call(f32[32,4,128]{2,1,0:T(4,128)S(1)} %all_to_all.11.scalars, f32[64,2048]{1,0:T(8,128)S(1)} %get-tuple-element.33.residual, f32[64,2048]{1,0:T(8,128)S(1)} %get-tuple-element.39.search, f32[64,2048]{1,0:T(8,128)S(1)} %get-tuple-element.40.applied, ...), custom_call_target="tpu_custom_call" | custom-call | tf_op jit(solution)/shard_map/pallas_call | solution.py:651
  (2 shorter events, 0.0 us)
Async XLA Ops:
  2.0 10.2 %collective-permute-start = (f32[136,1024]{1,0:T(8,128)S(1)}, f32[136,1024]{1,0:T(8,128)S(1)}, u32[]{:S(2)}, u32[]{:S(2)}) collective-permute-start(f32[136,1024]{1,0:T(8,128)S(1)} %get-tuple-element.25.pay_a), channel_id=1, source_target_pairs={{0,1},{2,3},{4,5},{6,7},{8,9},{10,11},{12,13},{14,15},{16,17},{18,... | collective-permute-start | bytes 1671176 | tf_op jit(solution)/shard_map/ppermute | solution.py:565
  2.5 9.7 %collective-permute-start.1 = (f32[136,1024]{1,0:T(8,128)S(1)}, f32[136,1024]{1,0:T(8,128)S(1)}, u32[]{:S(2)}, u32[]{:S(2)}) collective-permute-start(f32[136,1024]{1,0:T(8,128)S(1)} %get-tuple-element.26.pay_b), channel_id=1, source_target_pairs={{1,2},{3,4},{5,6},{7,8},{9,10},{11,12},{13,14},{15,16},{17,18},{19... | collective-permute-start | bytes 1671176 | tf_op jit(solution)/shard_map/ppermute | solution.py:564
  9.0 3.2 %copy-start = (bf16[2048,2048]{1,0:T(8,128)(2,1)}, bf16[2048,2048]{1,0:T(8,128)(2,1)S(1)}, u32[]{:S(2)}) copy-start(bf16[2048,2048]{1,0:T(8,128)(2,1)S(1)} %get-tuple-element.30.place) | copy-start | bytes 25165828
  12.3 3.4 %copy-start.1 = (bf16[2048,2048]{1,0:T(8,128)(2,1)S(1)}, bf16[2048,2048]{1,0:T(8,128)(2,1)}, u32[]{:S(2)}) copy-start(bf16[2048,2048]{1,0:T(8,128)(2,1)} %copy-done) | copy-start | bytes 25165828
  15.6 35.1 %copy-start.2 = (f32[24,24]{1,0:T(8,128)S(1)}, f32[24,24]{1,0:T(8,128)}, u32[]{:S(2)}) copy-start(f32[24,24]{1,0:T(8,128)} %inverse.1) | copy-start | bytes 6916
  23.6 8.7 %collective-permute-start.2 = (f32[104,1024]{1,0:T(8,128)S(1)}, f32[104,1024]{1,0:T(8,128)S(1)}, u32[]{:S(2)}, u32[]{:S(2)}) collective-permute-start(f32[104,1024]{1,0:T(8,128)S(1)} %get-tuple-element.32.image_a), channel_id=1, source_target_pairs={{0,1},{2,3},{4,5},{6,7},{8,9},{10,11},{12,13},{14,15},{16,17},{18,... | collective-permute-start | bytes 1277960 | tf_op jit(solution)/shard_map/ppermute | solution.py:565
  30.9 18.5 %collective-permute-start.4 = (f32[96,1024]{1,0:T(8,128)S(1)}, f32[96,1024]{1,0:T(8,128)S(1)}, u32[]{:S(2)}, u32[]{:S(2)}) collective-permute-start(f32[96,1024]{1,0:T(8,128)S(1)} %get-tuple-element.37.image_b), channel_id=1, source_target_pairs={{1,2},{3,4},{5,6},{7,8},{9,10},{11,12},{13,14},{15,16},{17,18},{19... | collective-permute-start | bytes 1179656 | tf_op jit(solution)/shard_map/ppermute | solution.py:564
  49.4 1.3 %collective-permute-start.3 = (f32[16,16,128]{2,1,0:T(8,128)S(1)}, f32[16,16,128]{2,1,0:T(8,128)S(1)}, u32[]{:S(2)}, u32[]{:S(2)}) collective-permute-start(f32[16,16,128]{2,1,0:T(8,128)S(1)} %all_to_all.10.terms), channel_id=1, source_target_pairs={{0,1},{2,3},{4,5},{6,7},{8,9},{10,11},{12,13},{14,15},{16,17},{18,... | collective-permute-start | bytes 393224 | tf_op jit(solution)/shard_map/ppermute | solution.py:633
  58.4 14.3 %collective-permute-start.5 = (f32[64,1024]{1,0:T(8,128)S(1)}, f32[64,1024]{1,0:T(8,128)S(1)}, u32[]{:S(2)}, u32[]{:S(2)}) collective-permute-start(f32[64,1024]{1,0:T(8,128)S(1)} %get-tuple-element.42.next_a), channel_id=1, source_target_pairs={{0,1},{2,3},{4,5},{6,7},{8,9},{10,11},{12,13},{14,15},{16,17},{18,... | collective-permute-start | bytes 786440 | tf_op jit(solution)/shard_map/ppermute | solution.py:565
  58.6 14.2 %collective-permute-start.6 = (f32[64,1024]{1,0:T(8,128)S(1)}, f32[64,1024]{1,0:T(8,128)S(1)}, u32[]{:S(2)}, u32[]{:S(2)}) collective-permute-start(f32[64,1024]{1,0:T(8,128)S(1)} %get-tuple-element.43.next_b), channel_id=1, source_target_pairs={{1,2},{3,4},{5,6},{7,8},{9,10},{11,12},{13,14},{15,16},{17,18},{19... | collective-permute-start | bytes 786440 | tf_op jit(solution)/shard_map/ppermute | solution.py:564

commit v3 on v2

--- a/solution.py
+++ b/solution.py
@@ -78,58 +78,59 @@
     return Chain(parity == 1, own, tuple(near), tuple(weights), tuple(same))
 
 
+def pack_side(first, load, basis, blocks, out, mine):
+    loads, _, face = load.shape
+    modes = basis.shape[0]
+    half = blocks.shape[0] // 2
+    size = blocks.shape[1]
+    row = lax.broadcasted_iota(jnp.int32, (size, size), 0)
+    col = lax.broadcasted_iota(jnp.int32, (size, size), 1)
+    mid = size // 2
+    low = mid + KP
+    out[mid:low, :] = jnp.zeros((KP, face), F32)
+    for k in range(modes):
+        mode = basis[k]
+        out[mid + k : mid + k + 1, :] = jnp.where(first, mode[:, :face], mode[:, face:])
+    base = jnp.where(first, 0, half)
+    for pair in range(half // 2):
+        one, two = blocks[base + 2 * pair], blocks[base + 2 * pair + 1]
+        mine[2 * pair] = one
+        mine[2 * pair + 1] = two
+        upper, lower = one.astype(F32), two.astype(F32)
+        both = jnp.where(row <= col, upper, lower)
+        left = pair * size
+        right = (half // 2 + pair) * size
+        out[:mid, left : left + size] = both[:mid]
+        out[:mid, right : right + size] = both[mid:]
+        diagonal = jnp.sum(jnp.where(row == col, lower, 0.0), axis=0, keepdims=True)
+        out[mid + modes : mid + modes + 1, left : left + size] = diagonal
+    out[low:, :] = jnp.where(first, load[:, 0, :], load[:, 1, :])
+
+
 def pack_kernel(
     extent,
     far_load, far_basis, far_blocks,
-    out_a, out_b, mine,
+    out_a, out_b, mine_a, mine_b,
     load, basis, blocks, arrived,
 ):
     copies = [
         pltpu.make_async_copy(source, target, arrived.at[k])
         for k, (source, target) in enumerate(
-            ((far_load, load), (far_blocks, blocks), (far_basis, basis))
+            ((far_blocks, blocks), (far_load, load), (far_basis, basis))
         )
     ]
     for copy in copies:
         copy.start()
-    loads, _, face = load.shape
-    modes = basis.shape[0]
-    half = blocks.shape[0] // 2
-    size = blocks.shape[1]
+    for copy in copies:
+        copy.wait()
     odd = chain(*extent).odd
-    row = lax.broadcasted_iota(jnp.int32, (size, size), 0)
-    col = lax.broadcasted_iota(jnp.int32, (size, size), 1)
-    mid = size // 2
-    low = loads + mid
-    copies[0].wait()
-    load_0, load_1 = load[:, 0, :], load[:, 1, :]
-    out_a[:loads, :] = jnp.where(odd, load_0, load_1)
-    out_b[:loads, :] = jnp.where(odd, load_1, load_0)
-    for copy in copies[1:]:
-        copy.wait()
-    for side, out, first in ((0, out_a, odd), (1, out_b, jnp.logical_not(odd))):
-        out[low:, :] = jnp.zeros((KP, face), F32)
-        for k in range(modes):
-            mode = basis[k]
-            out[low + k : low + k + 1, :] = jnp.where(first, mode[:, :face], mode[:, face:])
-        base = jnp.where(first, 0, half)
-        for pair in range(half // 2):
-            mine[side * half + 2 * pair] = blocks[base + 2 * pair]
-            mine[side * half + 2 * pair + 1] = blocks[base + 2 * pair + 1]
-            upper = blocks[base + 2 * pair].astype(F32)
-            lower = blocks[base + 2 * pair + 1].astype(F32)
-            both = jnp.where(row <= col, upper, lower)
-            left = pair * size
-            right = (half // 2 + pair) * size
-            out[loads:low, left : left + size] = both[:mid]
-            out[loads:low, right : right + size] = both[mid:]
-            diagonal = jnp.sum(jnp.where(row == col, lower, 0.0), axis=0, keepdims=True)
-            out[low + modes : low + modes + 1, left : left + size] = diagonal
+    pack_side(jnp.logical_not(odd), load, basis, blocks, out_b, mine_b)
+    pack_side(odd, load, basis, blocks, out_a, mine_a)
 
 
 def order_kernel(
     extent,
-    far_index, far_operator, stiffness,
+    far_index, stiffness, far_operator,
     pick, place, operator, softness,
     index, arrived,
 ):
@@ -143,20 +144,22 @@
     face = slots // 2
     rows = 128
     odd = chain(*extent).odd
-    lane = lax.broadcasted_iota(jnp.int32, (rows, slots), 1)
-    depth = lax.broadcasted_iota(jnp.int32, (rows, slots), 0)
-    one, zero = jnp.ones((), F32), jnp.zeros((), F32)
     softness[...] = 1.0 / stiffness[...]
     copies[0].wait()
+    lane = lax.broadcasted_iota(jnp.int32, (rows, slots), 1).astype(jnp.int16)
+    depth = lax.broadcasted_iota(jnp.int32, (rows, slots), 0).astype(jnp.int16)
+    one, zero = jnp.ones((), BF16), jnp.zeros((), BF16)
     index_0, index_1 = index[:, :face], index[:, face:]
     wanted = jnp.concatenate(
         [jnp.where(odd, index_0, index_1), jnp.where(odd, index_1, index_0)], axis=1
     )
+    every = jnp.broadcast_to(wanted, (rows, slots)).astype(jnp.int16)
     for start in range(0, slots, rows):
         here = jnp.broadcast_to(wanted[:, start : start + rows].astype(F32), (rows, rows)).T
-        target = jnp.concatenate([here] * (slots // rows), axis=1).astype(jnp.int32)
-        pick[start : start + rows, :] = jnp.where(target == lane, one, zero).astype(BF16)
-        place[start : start + rows, :] = jnp.where(wanted == depth + start, one, zero).astype(BF16)
+        here = here.astype(jnp.int32).astype(jnp.int16)
+        target = jnp.concatenate([here] * (slots // rows), axis=1)
+        pick[start : start + rows, :] = jnp.where(target == lane, one, zero)
+        place[start : start + rows, :] = jnp.where(every - jnp.int16(start) == depth, one, zero)
     copies[1].wait()
 
 
@@ -170,14 +173,9 @@
         )
 
 
-def operator_apply(rows, scale, pick, operator, place, first, second, third, image_a, image_b):
-    slots = first.shape[1]
+def apply_rest(rows, scale, operator, place, second, third, image_a, image_b):
+    slots = second.shape[1]
     face = slots // 2
-
-    @pl.loop(0, slots // TILE)
-    def _(tile):
-        cols = pl.ds(pl.multiple_of(tile * TILE, TILE), TILE)
-        second[:, cols] = dot(first[...], pick[:, cols]).astype(BF16)
 
     @pl.loop(0, slots // TILE)
     def _(tile):
@@ -202,68 +200,108 @@
     return weight * (product[:rows] + product[rows:])
 
 
+def side_part(
+    modes, at, weight, same, pay, got, blocks, residual, smooth, coarse, own_basis, pairs, first
+):
+    half, size, _ = blocks.shape
+    face = half * size
+    loads = pay.shape[0] - size // 2 - KP
+    rows = loads + 4 * KP
+    mid = size // 2
+    low = mid + KP
+    cols = slice(at, at + face)
+    row = lax.broadcasted_iota(jnp.int32, (size, size), 0)
+    col = lax.broadcasted_iota(jnp.int32, (size, size), 1)
+    real = lax.broadcasted_iota(jnp.int32, (KP, face), 0) < modes
+    mine = jnp.where(real, pay[mid:low, :], 0.0)
+    theirs = jnp.where(real, got[mid:low, :], 0.0)
+    own_basis[:, cols] = stacked(mine)
+    span = jnp.concatenate([mine + same * theirs, (1.0 - same) * theirs], axis=0)
+    for pair in range(half // 2):
+        left = pair * size
+        right = (half // 2 + pair) * size
+        both = jnp.concatenate(
+            [got[:mid, left : left + size], got[:mid, right : right + size]], axis=0
+        )
+        turned = both.T
+        diagonal = got[mid + modes : mid + modes + 1, left : left + size]
+        upper = jnp.where(row <= col, both, turned)
+        lower = jnp.where(row > col, both, jnp.where(row < col, turned, diagonal))
+        for k, theirs_block in ((2 * pair, upper), (2 * pair + 1, lower)):
+            block_pair = jnp.concatenate([blocks[k], theirs_block.astype(BF16)], axis=0)
+            pairs[k] = block_pair
+            there = slice(k * size, (k + 1) * size)
+            cols = slice(at + k * size, at + (k + 1) * size)
+            value = pay[low:, there] + got[low:, there]
+            modes_here = span[:, there]
+            result = smooth_block(
+                jnp.concatenate([value, modes_here], axis=0), weight, block_pair
+            )
+            residual[:, cols] = value
+            smooth[:, cols] = result[:loads]
+            high, low_part = two_parts(
+                jnp.concatenate([result[:loads], modes_here, result[loads:]], axis=0)
+            )
+            first[:rows, cols] = high
+            first[rows:, cols] = low_part
+            coarse[: 4 * KP, cols] = high[loads:]
+            coarse[4 * KP : 8 * KP, cols] = low_part[loads:]
+            coarse[8 * KP :, cols] = high[loads:]
+
+
+def near_kernel(
+    extent, modes,
+    pay, got, blocks, pick,
+    residual, smooth, coarse, own_basis, pairs, first, second,
+):
+    here = chain(*extent)
+    side_part(
+        modes, 0, here.weights[0], here.same[0], pay, got, blocks,
+        residual, smooth, coarse, own_basis, pairs, first,
+    )
+    slots = second.shape[1]
+    face = first.shape[1]
+
+    @pl.loop(0, slots // TILE)
+    def _(tile):
+        cols = pl.ds(pl.multiple_of(tile * TILE, TILE), TILE)
+        second[:, cols] = dot(first[...], pick[:face, cols]).astype(BF16)
+
+
 def first_kernel(
     extent, modes,
-    softness, pay_a, pay_b, got_a, got_b, blocks, pick, operator, place,
+    softness, pay, got, blocks,
+    residual_a, smooth_a, coarse_a, own_basis_a, first_a, second_a,
+    pick, operator, place,
     residual, smooth, coarse, pairs, image_a, image_b, keep,
-    first, second, third, terms,
+    own_basis, first, second, third, terms,
 ):
     loads, slots = residual.shape
     face = slots // 2
-    count = pairs.shape[0]
-    half = count // 2
-    size = pairs.shape[2]
     rows = loads + 4 * KP
-    mid = size // 2
-    low = loads + mid
     here = chain(*extent)
-    odd = here.odd
-    row = lax.broadcasted_iota(jnp.int32, (size, size), 0)
-    col = lax.broadcasted_iota(jnp.int32, (size, size), 1)
-    real = lax.broadcasted_iota(jnp.int32, (KP, face), 0) < modes
-    own_basis, span = [], []
-    for side, pay, got in ((0, pay_a, got_a), (1, pay_b, got_b)):
-        cols = slice(side * face, (side + 1) * face)
-        residual[:, cols] = pay[:loads, :] + got[:loads, :]
-        mine = jnp.where(real, pay[low:, :], 0.0)
-        theirs = jnp.where(real, got[low:, :], 0.0)
-        same = here.same[side]
-        own_basis.append(mine)
-        span.append(jnp.concatenate([mine + same * theirs, (1.0 - same) * theirs], axis=0))
-        for pair in range(half // 2):
-            left = pair * size
-            right = (half // 2 + pair) * size
-            both = jnp.concatenate(
-                [got[loads:low, left : left + size], got[loads:low, right : right + size]], axis=0
-            )
-            turned = both.T
-            diagonal = got[low + modes : low + modes + 1, left : left + size]
-            upper = jnp.where(row <= col, both, turned)
-            lower = jnp.where(row > col, both, jnp.where(row < col, turned, diagonal))
-            for k, theirs_block in ((2 * pair, upper), (2 * pair + 1, lower)):
-                pairs[side * half + k, :size, :] = blocks[side * half + k]
-                pairs[side * half + k, size:, :] = theirs_block.astype(BF16)
-    for block in range(count):
-        side, k = divmod(block, half)
-        cols = slice(block * size, (block + 1) * size)
-        modes_here = span[side][:, k * size : (k + 1) * size]
-        value = jnp.concatenate([residual[:, cols], modes_here], axis=0)
-        result = smooth_block(value, here.weights[side], pairs[block])
-        smooth[:, cols] = result[:loads]
-        high, low = two_parts(jnp.concatenate([result[:loads], modes_here, result[loads:]], axis=0))
-        first[:rows, cols] = high
-        first[rows:, cols] = low
-        coarse[: 4 * KP, cols] = high[loads:]
-        coarse[4 * KP : 8 * KP, cols] = low[loads:]
-        coarse[8 * KP :, cols] = high[loads:]
-
-    operator_apply(
-        rows, softness[...], pick, operator, place, first, second, third, image_a, image_b
-    )
-
-    basis = stacked(jnp.concatenate(own_basis, axis=1))
-    load_side = folded(dot_rows(basis, stacked(residual[...])), KP, loads)
-    smooth_side = folded(dot_rows(basis, first[...]), KP, rows)
+    side_part(
+        modes, face, here.weights[1], here.same[1], pay, got, blocks,
+        residual, smooth, coarse, own_basis, pairs, first,
+    )
+
+    @pl.loop(0, slots // TILE)
+    def _(tile):
+        cols = pl.ds(pl.multiple_of(tile * TILE, TILE), TILE)
+        product = dot(first[:, face:], pick[face:, cols]) + second_a[:, cols].astype(F32)
+        second[:, cols] = product.astype(BF16)
+
+    for whole, part in (
+        (residual, residual_a), (smooth, smooth_a), (coarse, coarse_a),
+        (own_basis, own_basis_a), (first, first_a),
+    ):
+        whole[:, :face] = part[...]
+    apply_rest(rows, softness[...], operator, place, second, third, image_a, image_b)
+
+    vectors = jnp.concatenate([stacked(residual[...]), first[...]], axis=0)
+    sides = dot_rows(own_basis[...], vectors)
+    load_side = folded(sides[:, : 2 * loads], KP, loads)
+    smooth_side = folded(sides[:, 2 * loads :], KP, rows)
     shared = smooth_side[:, loads + 2 * KP :]
     energy = jnp.zeros((8 * KP, 2 * rows), F32)
     for side, image in ((0, image_a), (1, image_b)):
@@ -288,11 +326,11 @@
             terms[3, :, at + 2 * KP : at + 3 * KP] = smooth_rows[:, smooth_cols]
             last = shared[:, j * KP : (j + 1) * KP] if i == 0 else jnp.zeros((KP, KP), F32)
             terms[3, :, at + 3 * KP : at + 4 * KP] = last
-    keep[...] = jnp.where(odd, terms[2:], terms[:2])
+    keep[...] = jnp.where(here.odd, terms[2:], terms[:2])
     image_a[rows:, :] = jnp.zeros((KP, face), F32)
     for kind in range(2):
         image_a[rows:, kind * 2 * loads : (kind + 1) * 2 * loads] = jnp.where(
-            odd, terms[kind], terms[2 + kind]
+            here.odd, terms[kind], terms[2 + kind]
         )
 
 
@@ -418,16 +456,15 @@
 
 def second_kernel(
     extent,
-    softness, terms, other_terms, inverse, residual, smooth, coarse, pairs, image_a, image_b, got_a, got_b,
+    softness, terms, other_terms, inverse, residual, smooth, coarse, pairs_a, pairs_b,
+    image_a, image_b, got_a, got_b,
     pick, operator, place,
     search, applied, change, next_a, next_b, scalars,
     amounts, first, second, third,
 ):
     loads, slots = residual.shape
     face = slots // 2
-    count = pairs.shape[0]
-    half = count // 2
-    size = pairs.shape[2]
+    half, _, size = pairs_a.shape
     clusters, members = extent
     here = chain(*extent)
 
@@ -462,10 +499,10 @@
             image[:loads, :] + got[:loads, :] - dot_modes(mixed, rows)
         )
     image_projected = applied[...] - dot_modes(image_own_basis, coarse[...])
-    for block in range(count):
-        cols = slice(block * size, (block + 1) * size)
-        weight = here.weights[block // half]
-        change[:, cols] = smooth_block(applied[:, cols], weight, pairs[block])
+    for side, pairs in ((0, pairs_a), (1, pairs_b)):
+        for k in range(half):
+            cols = slice(side * face + k * size, side * face + (k + 1) * size)
+            change[:, cols] = smooth_block(applied[:, cols], here.weights[side], pairs[k])
     changed = change[...] - dot_modes(image_own, coarse[...])
     change[...] = changed
     high, low = two_parts(changed)
@@ -478,9 +515,12 @@
         weighted(image_projected, changed),
     ]
 
-    operator_apply(
-        loads, softness[...], pick, operator, place, first, second, third, next_a, next_b
-    )
+    @pl.loop(0, slots // TILE)
+    def _(tile):
+        cols = pl.ds(pl.multiple_of(tile * TILE, TILE), TILE)
+        second[:, cols] = dot(first[...], pick[:, cols]).astype(BF16)
+
+    apply_rest(loads, softness[...], operator, place, second, third, next_a, next_b)
 
     for vector in (search, change):
         column = jnp.sum(vector[:, :face] * next_a[...], axis=1, keepdims=True)
@@ -573,12 +613,14 @@
 
     half_vector = shaped((loads, face))
     vector = shaped((loads, slots))
-    packed = shaped((loads + size // 2 + KP, face))
-    pay_a, pay_b, mine = pl.pallas_call(
+    half = block_count // 2
+    packed = shaped((size // 2 + KP + loads, face))
+    side_blocks = shaped((half, size, size), BF16)
+    pay_a, pay_b, mine_a, mine_b = pl.pallas_call(
         functools.partial(pack_kernel, extent),
-        out_shape=(packed, packed, shaped(blocks.shape, BF16)),
+        out_shape=(packed, packed, side_blocks, side_blocks),
         in_specs=[HBM] * 3,
-        out_specs=(VMEM,) * 3,
+        out_specs=(VMEM,) * 4,
         scratch_shapes=[
             pltpu.VMEM(load.shape, F32),
             pltpu.VMEM(basis.shape, F32),
@@ -593,33 +635,53 @@
     pick, place, operator, softness = pl.pallas_call(
         functools.partial(order_kernel, extent),
         out_shape=(ordering, ordering, ordering, shaped((1, 1))),
-        in_specs=[HBM, HBM, VMEM],
+        in_specs=[HBM, VMEM, HBM],
         out_specs=(VMEM,) * 4,
         scratch_shapes=[pltpu.VMEM((1, slots), jnp.int32), pltpu.SemaphoreType.DMA((2,))],
         compiler_params=params(8),
-    )(in_hbm(index_map.reshape(1, slots)), in_hbm(dual_operator), stiffness)
+    )(in_hbm(index_map.reshape(1, slots)), stiffness, in_hbm(dual_operator))
     pick, operator, place = [
         pltpu.with_memory_space_constraint(v, pltpu.VMEM) for v in (pick, operator, place)
     ]
 
     rows = loads + 4 * KP
-    residual, smooth, coarse, pairs, image_a, image_b, keep = pl.pallas_call(
+    side_pairs = shaped((half, 2 * size, size), BF16)
+    residual_a, smooth_a, coarse_a, own_basis_a, pairs_a, first_a, second_a = pl.pallas_call(
+        functools.partial(near_kernel, extent, modes),
+        out_shape=(
+            half_vector,
+            half_vector,
+            shaped((12 * KP, face), BF16),
+            shaped((2 * KP, face), BF16),
+            side_pairs,
+            shaped((2 * rows, face), BF16),
+            shaped((2 * rows, slots), BF16),
+        ),
+        in_specs=[VMEM] * 4,
+        out_specs=(VMEM,) * 7,
+        compiler_params=params(8),
+    )(pay_a, got_a, mine_a, pick)
+    residual, smooth, coarse, pairs_b, image_a, image_b, keep = pl.pallas_call(
         functools.partial(first_kernel, extent, modes),
         out_shape=(
             vector,
             vector,
             shaped((12 * KP, slots), BF16),
-            shaped((block_count, 2 * size, size), BF16),
+            side_pairs,
             shaped((rows + KP, face)),
             shaped((rows, face)),
             shaped((2, KP, 2 * loads)),
         ),
-        in_specs=[VMEM] * 9,
+        in_specs=[VMEM] * 13,
         out_specs=(VMEM,) * 7,
-        scratch_shapes=[pltpu.VMEM((2 * rows, slots), BF16)] * 3
+        scratch_shapes=[pltpu.VMEM((2 * KP, slots), BF16)]
+        + [pltpu.VMEM((2 * rows, slots), BF16)] * 3
         + [pltpu.VMEM((4, KP, 2 * loads), F32)],
-        compiler_params=params(20),
-    )(softness, pay_a, pay_b, got_a, got_b, mine, pick, operator, place)
+        compiler_params=params(12),
+    )(
+        softness, pay_b, got_b, mine_b, residual_a, smooth_a, coarse_a, own_basis_a, first_a,
+        second_a, pick, operator, place,
+    )
 
     got_a, got_b = swap(image_a, image_b)
     terms = pl.pallas_call(
@@ -635,13 +697,13 @@
     search, applied, change, next_a, next_b, scalars = pl.pallas_call(
         functools.partial(second_kernel, extent),
         out_shape=(vector, vector, vector, half_vector, half_vector, shaped((4, 2 * loads))),
-        in_specs=[VMEM] * 15,
+        in_specs=[VMEM] * 16,
         out_specs=(VMEM,) * 6,
         scratch_shapes=[pltpu.VMEM((4, clusters, KP, loads), F32)]
         + [pltpu.VMEM((2 * loads, slots), BF16)] * 3,
-        compiler_params=params(20),
+        compiler_params=params(12),
     )(
-        softness, terms, other_terms, coarse_inverse, residual, smooth, coarse, pairs,
+        softness, terms, other_terms, coarse_inverse, residual, smooth, coarse, pairs_a, pairs_b,
         image_a, image_b, got_a, got_b, pick, operator, place,
     )
 
@@ -653,7 +715,7 @@
         out_shape=(shaped((loads, 2, face)), shaped((loads, 2, face))),
         in_specs=[VMEM] * 9,
         out_specs=(VMEM, VMEM),
-        compiler_params=params(20),
+        compiler_params=params(12),
     )(scalars, residual, search, applied, change, next_a, next_b, got_a, got_b)
     return out_m.reshape(dual_load.shape), out_r.reshape(dual_load.shape)
 

time: 74.6 us -> 70.6 us (0.946)
  local copies, waits for them, and re-layouts: 6.61 us -> 0.02 us
  starting transfers between devices: 9.99 us -> 12.7 us
    unnamed x6 -> x2, local copies, waits for them, and re-layouts: 6.6 us -> 0.01 us
    ppermute x3, starting transfers between devices: 7.96 us -> 10.7 us  [swap(): from_a = lax.ppermute(side_a, AXES, evens)]
    pallas_call x0 -> x1, Pallas kernels: none -> 1.69 us  [per_device(): pl.pallas_call(functools.partial(near_kernel, extent, modes), out_shape=(...]
    pallas_call x1, Pallas kernels: 5.15 us -> 3.93 us  [per_device(): pl.pallas_call(functools.partial(order_kernel, extent), out_shape=(orderi...]
    pallas_call x1, Pallas kernels: 7.95 us -> 7 us  [per_device(): pl.pallas_call(functools.partial(first_kernel, extent, modes), out_shape=...]
  transfers between devices with their start and end apart: 7 -> 7, of which waited for: 2 -> 2; matrix products, arithmetic and copies ran while one was open for 0% -> 0% of each run, Pallas kernels for 7% -> 8%
where the time goes in v3:
time: 70.6 us; the launch traced here: 70.3 us
  blocking collectives  30.6 us (43%)
  Pallas kernels  23.5 us (33%)
  starting transfers between devices  12.7 us (18%)
  waiting for transfers between devices  2.07 us (3%)
  between operations  1.37 us (2%)
    all_to_all x2, blocking collectives, share(): lax.all_to_all(copies, AXES, 0, 0, axis_index_groups=groups, tiled=True)  30.6 us
    ppermute x3, starting transfers between devices, swap(): from_a = lax.ppermute(side_a, AXES, evens)  10.7 us
    pallas_call x1, Pallas kernels, per_device(): pl.pallas_call(functools.partial(second_kernel, extent), out_shape=(vecto...  7.69 us
    pallas_call x1, Pallas kernels, per_device(): pl.pallas_call(functools.partial(first_kernel, extent, modes), out_shape=...  7 us
    pallas_call x1, Pallas kernels, per_device(): pl.pallas_call(functools.partial(order_kernel, extent), out_shape=(orderi...  3.93 us
    ppermute x3, starting transfers between devices, swap(): from_b = lax.ppermute(side_b, AXES, odds)  2.02 us
    pallas_call x1, Pallas kernels, per_device(): pl.pallas_call(functools.partial(near_kernel, extent, modes), out_shape=(...  1.69 us
    pallas_call x1, Pallas kernels, per_device(): pl.pallas_call(functools.partial(last_kernel, extent), out_shape=(shaped(...  1.63 us
  transfers between devices with their start and end apart: 7, of which 2 were waited for; matrix products, arithmetic and copies ran while one was open for 0% of the time, Pallas kernels for 8%

profile of v3, /device:TPU:0, one launch (start us, length us, event | category | flops | bytes accessed | tf_op | source)
XLA Modules:
  0.0 70.3 jit_solution(4304786800999207699)
XLA Ops:
  0.6 1.6 %shard_map.87 = (f32[136,1024]{1,0:T(8,128)S(1)}, f32[136,1024]{1,0:T(8,128)S(1)}, bf16[8,128,128]{2,1,0:T(8,128)(2,1)S(1)}, bf16[8,128,128]{2,1,0:T(8,128)(2,1)S(1)}) custom-call(f32[64,2,1024]{2,1,0:T(2,128)} %bitcast.6, f32[6,1,2048]{2,1,0:T(1,128)} %bitcast.8, bf16[16,128,128]{2,1,0:T(8,128)(2,1)} %bitcast.7), custom_call_target="tpu_custom_call" | custom-call | tf_op jit(solution)/shard_map/pallas_call | solution.py:619
  2.2 0.5 collective-permute-start.1
  2.7 0.7 collective-permute-start
  4.1 3.9 %shard_map.86 = (bf16[2048,2048]{1,0:T(8,128)(2,1)S(1)}, bf16[2048,2048]{1,0:T(8,128)(2,1)S(1)}, bf16[2048,2048]{1,0:T(8,128)(2,1)S(1)}, f32[1,1]{1,0:T(1,128)}) custom-call(s32[1,2048]{1,0:T(1,128)} %bitcast.9, f32[1,1]{1,0:T(1,128)S(6)} %copy.9.stiffness, bf16[2048,2048]{1,0:T(8,128)(2,1)} %far_operator.1), custom_call_target="tpu_custom_call" | custom-call | tf_op jit(solution)/shard_map/pallas_call | solution.py:635
  8.0 0.0 collective-permute-done.1.got
  8.0 1.7 %shard_map.88 = (f32[64,1024]{1,0:T(8,128)S(1)}, f32[64,1024]{1,0:T(8,128)S(1)}, bf16[96,1024]{1,0:T(8,128)(2,1)S(1)}, bf16[16,1024]{1,0:T(8,128)(2,1)S(1)}, bf1...) custom-call(f32[136,1024]{1,0:T(8,128)S(1)} %get-tuple-element.35.pay, ...), custom_call_target="tpu_custom_call" | custom-call | tf_op jit(solution)/shard_map/pallas_call | solution.py:649
  9.7 0.0 collective-permute-done.got
  9.7 0.0 copy-start
  9.7 7.0 %shard_map.89 = (f32[64,2048]{1,0:T(8,128)S(1)}, f32[64,2048]{1,0:T(8,128)S(1)}, bf16[96,2048]{1,0:T(8,128)(2,1)S(1)}, bf16[8,256,128]{2,1,0:T(8,128)(2,1)S(1)},...) custom-call(f32[1,1]{1,0:T(1,128)} %get-tuple-element.32.softness, ...), custom_call_target="tpu_custom_call" | custom-call | tf_op jit(solution)/shard_map/pallas_call | solution.py:664
  16.7 10.0 %collective-permute-start.2 = (f32[104,1024]{1,0:T(8,128)S(1)}, f32[104,1024]{1,0:T(8,128)S(1)}, u32[]{:S(2)}, u32[]{:S(2)}) collective-permute-start(f32[104,1024]{1,0:T(8,128)S(1)} %get-tuple-element.47.image_a), channel_id=1, source_target_pairs={{0,1},{2,3},{4,5},{6,7},{8,9},{10,11},{12,13},{14,15},{16,17},{18,... | collective-permute-start | bytes 1277960 | tf_op jit(solution)/shard_map/ppermute | solution.py:605
  26.8 0.7 collective-permute-start.4
  27.4 0.7 %collective-permute-done.2.got.got_a = f32[104,1024]{1,0:T(8,128)S(1)} collective-permute-done((f32[104,1024]{1,0:T(8,128)S(1)}, f32[104,1024]{1,0:T(8,128)S(1)}, u32[]{:S(2)}, u32[]{:S(2)}) %collective-permute-start.2) | collective-permute-done | bytes 426016 | tf_op jit(solution)/shard_map/ppermute | solution.py:605
  28.2 17.1 %all_to_all.10.terms = f32[16,16,128]{2,1,0:T(8,128)S(1)} all-to-all(f32[16,16,128]{2,1,0:T(8,128)S(1)} %shard_map.90), channel_id=1, replica_groups={{0,2,4,6,8,10,12,14,16,18,20,22,24,26,28,30},{1,3,5,7,9,11,13,15,17,19,..., dimensions={0} | all-to-all | bytes 262144 | tf_op jit(solution)/shard_map/all_to_all | solution.py:609
  45.3 0.0 collective-permute-start.3
  45.3 0.0 collective-permute-done.4.got_b
  45.3 1.3 %collective-permute-done.3.other_terms = f32[16,16,128]{2,1,0:T(8,128)S(1)} collective-permute-done((f32[16,16,128]{2,1,0:T(8,128)S(1)}, f32[16,16,128]{2,1,0:T(8,128)S(1)}, u32[]{:S(2)}, u32[]{:S(2)}) %collective-permute-start.3) | collective-permute-done | bytes 131104 | tf_op jit(solution)/shard_map/ppermute | solution.py:695
  46.6 0.0 copy-done
  46.6 7.7 %shard_map.91 = (f32[64,2048]{1,0:T(8,128)S(1)}, f32[64,2048]{1,0:T(8,128)S(1)}, f32[64,2048]{1,0:T(8,128)S(1)}, f32[64,1024]{1,0:T(8,128)S(1)}, f32[64,1024]{1,0:T(8,128)S(1)}, /*index=5*/f32[4,128]{1,0:T(4,128)S(1)}) custom-call(f32[1,1]{1,0:T(1,128)} %get-tuple-element.32.softness, f32[16,16,128]{2,1,0:T(8,128)S(1)} %all_to_all.10.terms, ...), custom_call_target="tpu_custom_call" | custom-call | tf_op jit(solution)/shard_map/pallas_call | solution.py:697
  54.3 0.2 collective-permute-start.5
  54.5 0.7 collective-permute-start.6
  55.2 13.4 %all_to_all.11.scalars = f32[32,4,128]{2,1,0:T(4,128)S(1)} all-to-all(f32[32,4,128]{2,1,0:T(4,128)S(1)} %broadcast_in_dim.2), channel_id=1, replica_groups=mesh['cluster'=4,'member'=8] {'cluster','member'}, dimensions={0} | all-to-all | bytes 131072 | tf_op jit(solution)/shard_map/all_to_all | solution.py:609
  68.6 0.0 collective-permute-done.5.got_a
  68.6 0.0 collective-permute-done.6.got_b
  68.6 1.6 %shard_map.92 = (f32[64,2,1024]{2,1,0:T(2,128)}, f32[64,2,1024]{2,1,0:T(2,128)}) custom-call(f32[32,4,128]{2,1,0:T(4,128)S(1)} %all_to_all.11.scalars, f32[64,2048]{1,0:T(8,128)S(1)} %get-tuple-element.48.residual, f32[64,2048]{1,0:T(8,128)S(1)} %get-tuple-element.55.search, f32[64,2048]{1,0:T(8,128)S(1)} %get-tuple-element.56.applied, ...), custom_call_target="tpu_custom_call" | custom-call | tf_op jit(solution)/shard_map/pallas_call | solution.py:713
  (2 shorter events, 0.0 us)
Async XLA Ops:
  2.2 5.8 %collective-permute-start.1 = (f32[136,1024]{1,0:T(8,128)S(1)}, f32[136,1024]{1,0:T(8,128)S(1)}, u32[]{:S(2)}, u32[]{:S(2)}) collective-permute-start(f32[136,1024]{1,0:T(8,128)S(1)} %get-tuple-element.35.pay), channel_id=1, source_target_pairs={{0,1},{2,3},{4,5},{6,7},{8,9},{10,11},{12,13},{14,15},{16,17},{18,... | collective-permute-start | bytes 1671176 | tf_op jit(solution)/shard_map/ppermute | solution.py:605
  2.7 7.0 %collective-permute-start = (f32[136,1024]{1,0:T(8,128)S(1)}, f32[136,1024]{1,0:T(8,128)S(1)}, u32[]{:S(2)}, u32[]{:S(2)}) collective-permute-start(f32[136,1024]{1,0:T(8,128)S(1)} %get-tuple-element.33.pay), channel_id=1, source_target_pairs={{1,2},{3,4},{5,6},{7,8},{9,10},{11,12},{13,14},{15,16},{17,18},{19... | collective-permute-start | bytes 1671176 | tf_op jit(solution)/shard_map/ppermute | solution.py:604
  9.7 36.9 %copy-start = (f32[24,24]{1,0:T(8,128)S(1)}, f32[24,24]{1,0:T(8,128)}, u32[]{:S(2)}) copy-start(f32[24,24]{1,0:T(8,128)} %inverse.1) | copy-start | bytes 6916
  16.7 11.4 %collective-permute-start.2 = (f32[104,1024]{1,0:T(8,128)S(1)}, f32[104,1024]{1,0:T(8,128)S(1)}, u32[]{:S(2)}, u32[]{:S(2)}) collective-permute-start(f32[104,1024]{1,0:T(8,128)S(1)} %get-tuple-element.47.image_a), channel_id=1, source_target_pairs={{0,1},{2,3},{4,5},{6,7},{8,9},{10,11},{12,13},{14,15},{16,17},{18,... | collective-permute-start | bytes 1277960 | tf_op jit(solution)/shard_map/ppermute | solution.py:605
  26.8 18.5 %collective-permute-start.4 = (f32[96,1024]{1,0:T(8,128)S(1)}, f32[96,1024]{1,0:T(8,128)S(1)}, u32[]{:S(2)}, u32[]{:S(2)}) collective-permute-start(f32[96,1024]{1,0:T(8,128)S(1)} %get-tuple-element.53.image_b), channel_id=1, source_target_pairs={{1,2},{3,4},{5,6},{7,8},{9,10},{11,12},{13,14},{15,16},{17,18},{19... | collective-permute-start | bytes 1179656 | tf_op jit(solution)/shard_map/ppermute | solution.py:604
  45.3 1.3 %collective-permute-start.3 = (f32[16,16,128]{2,1,0:T(8,128)S(1)}, f32[16,16,128]{2,1,0:T(8,128)S(1)}, u32[]{:S(2)}, u32[]{:S(2)}) collective-permute-start(f32[16,16,128]{2,1,0:T(8,128)S(1)} %all_to_all.10.terms), channel_id=1, source_target_pairs={{0,1},{2,3},{4,5},{6,7},{8,9},{10,11},{12,13},{14,15},{16,17},{18,... | collective-permute-start | bytes 393224 | tf_op jit(solution)/shard_map/ppermute | solution.py:695
  54.3 14.3 %collective-permute-start.5 = (f32[64,1024]{1,0:T(8,128)S(1)}, f32[64,1024]{1,0:T(8,128)S(1)}, u32[]{:S(2)}, u32[]{:S(2)}) collective-permute-start(f32[64,1024]{1,0:T(8,128)S(1)} %get-tuple-element.58.next_a), channel_id=1, source_target_pairs={{0,1},{2,3},{4,5},{6,7},{8,9},{10,11},{12,13},{14,15},{16,17},{18,... | collective-permute-start | bytes 786440 | tf_op jit(solution)/shard_map/ppermute | solution.py:605
  54.5 14.1 %collective-permute-start.6 = (f32[64,1024]{1,0:T(8,128)S(1)}, f32[64,1024]{1,0:T(8,128)S(1)}, u32[]{:S(2)}, u32[]{:S(2)}) collective-permute-start(f32[64,1024]{1,0:T(8,128)S(1)} %get-tuple-element.59.next_b), channel_id=1, source_target_pairs={{1,2},{3,4},{5,6},{7,8},{9,10},{11,12},{13,14},{15,16},{17,18},{19... | collective-permute-start | bytes 786440 | tf_op jit(solution)/shard_map/ppermute | solution.py:604

commit v4 on v3

--- a/solution.py
+++ b/solution.py
@@ -12,6 +12,7 @@
 F32 = jnp.float32
 BF16 = jnp.bfloat16
 EXACT = lax.Precision.HIGHEST
+SLICE = 4
 KP = 8
 TILE = 1024
 
@@ -166,11 +167,25 @@
 def merge_kernel(keep, got, out):
     kinds, depth, lanes = keep.shape
     rows = got.shape[0] - depth
-    for kind in range(kinds):
-        value = keep[kind] + got[rows:, kind * lanes : (kind + 1) * lanes]
-        out[:, kind * depth : (kind + 1) * depth, :] = jnp.broadcast_to(
-            value[None], (out.shape[0], depth, lanes)
-        )
+    modes = out.shape[1] * SLICE // kinds
+    values = [keep[k] + got[rows:, k * lanes : (k + 1) * lanes] for k in range(kinds)]
+    value = jnp.concatenate([v[:modes] for v in values], axis=0)
+    for part in range(out.shape[1]):
+        piece = value[part * SLICE : (part + 1) * SLICE]
+        out[:, part] = jnp.broadcast_to(piece[None], (out.shape[0],) + piece.shape)
+
+
+def fold_kernel(clusters, members, terms, out):
+    for c in range(clusters):
+        for parity in range(2):
+            for part in range(terms.shape[1]):
+                begin = terms[c * members + parity, part]
+                end = terms[(c + 1) * members - 2 + parity, part]
+                value = begin
+                for m in range(2, members, 2):
+                    value = value + terms[c * members + m + parity, part]
+                for k, result in enumerate((value, begin, end)):
+                    out[(c * 2 + parity) * 3 + k, part * SLICE : (part + 1) * SLICE] = result
 
 
 def apply_rest(rows, scale, operator, place, second, third, image_a, image_b):
@@ -334,31 +349,22 @@
         )
 
 
-def coarse_solves(clusters, members, loads, odd, terms, other_terms, inverse):
-    def pick_kind(kind, mine, theirs):
-        return jnp.where(odd, theirs, mine) if kind < 2 else jnp.where(odd, mine, theirs)
-
-    def rows_of(kind):
-        return slice(kind % 2 * KP, kind % 2 * KP + KP)
+def coarse_solves(clusters, loads, terms, inverse):
+    modes = inverse.shape[0] // clusters
+
+    def one_kind(c, kind, which):
+        value = terms[(c * 2 + kind // 2) * 3 + which]
+        value = value[kind % 2 * modes : (kind % 2 + 1) * modes]
+        return jnp.concatenate([value, jnp.zeros((KP - modes, value.shape[1]), F32)], axis=0)
 
     def total(c, kind):
-        pairs = members // 2
-        found = [ref[c * pairs, rows_of(kind)] for ref in (terms, other_terms)]
-        for m in range(1, pairs):
-            found = [
-                v + ref[c * pairs + m, rows_of(kind)]
-                for v, ref in zip(found, (terms, other_terms))
-            ]
-        return pick_kind(kind, *found)
-
-    def one(pair, kind):
-        return pick_kind(kind, terms[pair, rows_of(kind)], other_terms[pair, rows_of(kind)])
+        return one_kind(c, kind, 0)
 
     def begin(c, kind):
-        return one(c * members // 2, kind)
+        return one_kind(c, kind, 1)
 
     def end(c, kind):
-        return one((c + 1) * members // 2 - 1, kind)
+        return one_kind(c, kind, 2)
 
     span = 4 * KP
     lanes = terms.shape[-1]
@@ -424,7 +430,6 @@
             found.append(value)
         return found
 
-    modes = inverse.shape[0] // clusters
     row = lax.broadcasted_iota(jnp.int32, (clusters * KP, clusters * modes), 0)
     col = lax.broadcasted_iota(jnp.int32, (clusters * KP, clusters * modes), 1)
     mode = row % KP
@@ -456,7 +461,7 @@
 
 def second_kernel(
     extent,
-    softness, terms, other_terms, inverse, residual, smooth, coarse, pairs_a, pairs_b,
+    softness, terms, inverse, residual, smooth, coarse, pairs_a, pairs_b,
     image_a, image_b, got_a, got_b,
     pick, operator, place,
     search, applied, change, next_a, next_b, scalars,
@@ -465,7 +470,7 @@
     loads, slots = residual.shape
     face = slots // 2
     half, _, size = pairs_a.shape
-    clusters, members = extent
+    clusters, _ = extent
     here = chain(*extent)
 
     def weighted(left, right):
@@ -474,7 +479,7 @@
         far = jnp.sum(product[:, face:], axis=1, keepdims=True)
         return here.weights[0] * near + here.weights[1] * far
 
-    solved = coarse_solves(clusters, members, loads, here.odd, terms, other_terms, inverse)
+    solved = coarse_solves(clusters, loads, terms, inverse)
     for kind, parts in enumerate(solved):
         for c, part in enumerate(parts):
             amounts[kind, c] = part
@@ -605,8 +610,9 @@
         from_a = lax.ppermute(side_a, AXES, evens)
         return from_a, from_b
 
-    def share(copies, groups=None):
-        return lax.all_to_all(copies, AXES, 0, 0, axis_index_groups=groups, tiled=True)
+    def share(copies):
+        parts = copies.reshape((-1,) + copies.shape[2:])
+        return lax.all_to_all(parts, AXES, 0, 0, tiled=True).reshape(copies.shape)
 
     def params(mebibytes):
         return pltpu.CompilerParams(vmem_limit_bytes=mebibytes * 1024 * 1024)
@@ -686,29 +692,35 @@
     got_a, got_b = swap(image_a, image_b)
     terms = pl.pallas_call(
         merge_kernel,
-        out_shape=shaped((devices // 2, 2 * KP, 2 * loads)),
+        out_shape=shaped((devices, 2 * modes // SLICE, SLICE, 2 * loads)),
         in_specs=[VMEM] * 2,
         out_specs=VMEM,
         compiler_params=params(8),
     )(keep, got_a)
-    terms = share(terms, [list(range(k, devices, 2)) for k in range(2)])
-    other_terms = lax.ppermute(terms, AXES, evens)
+    terms = pl.pallas_call(
+        functools.partial(fold_kernel, clusters, members),
+        out_shape=shaped((clusters * 6, 2 * modes, 2 * loads)),
+        in_specs=[VMEM],
+        out_specs=VMEM,
+        compiler_params=params(8),
+    )(share(terms))
 
     search, applied, change, next_a, next_b, scalars = pl.pallas_call(
         functools.partial(second_kernel, extent),
         out_shape=(vector, vector, vector, half_vector, half_vector, shaped((4, 2 * loads))),
-        in_specs=[VMEM] * 16,
+        in_specs=[VMEM] * 15,
         out_specs=(VMEM,) * 6,
         scratch_shapes=[pltpu.VMEM((4, clusters, KP, loads), F32)]
         + [pltpu.VMEM((2 * loads, slots), BF16)] * 3,
         compiler_params=params(12),
     )(
-        softness, terms, other_terms, coarse_inverse, residual, smooth, coarse, pairs_a, pairs_b,
+        softness, terms, coarse_inverse, residual, smooth, coarse, pairs_a, pairs_b,
         image_a, image_b, got_a, got_b, pick, operator, place,
     )
 
     got_a, got_b = swap(next_a, next_b)
-    scalars = share(jnp.broadcast_to(scalars[None], (devices,) + scalars.shape))
+    scalars = share(jnp.broadcast_to(scalars[None, None], (devices, 1) + scalars.shape))
+    scalars = scalars.reshape(devices, 4, 2 * loads)
 
     out_m, out_r = pl.pallas_call(
         functools.partial(last_kernel, extent),

time: 70.6 us -> 69.9 us (0.990)
  waiting for transfers between devices: 2.07 us -> 0.73 us
    ppermute x1 -> x0, waiting for transfers between devices: 1.34 us -> none  [per_device(): other_terms = lax.ppermute(terms, AXES, evens)]
  transfers between devices with their start and end apart: 7 -> 6, of which waited for: 2 -> 1; matrix products, arithmetic and copies ran while one was open for 0% -> 0% of each run, Pallas kernels for 8% -> 8%
where the time goes in v4:
time: 69.9 us; the launch traced here: 69.6 us
  blocking collectives  30.8 us (44%)
  Pallas kernels  23.6 us (34%)
  starting transfers between devices  13.2 us (19%)
  between operations  1.39 us (2%)
  waiting for transfers between devices  0.73 us (1%)
    all_to_all x2, blocking collectives, share(): return lax.all_to_all(parts, AXES, 0, 0, tiled=True).reshape(copies.shape)  30.8 us
    ppermute x3, starting transfers between devices, swap(): from_a = lax.ppermute(side_a, AXES, evens)  11.1 us
    pallas_call x1, Pallas kernels, per_device(): pl.pallas_call(functools.partial(second_kernel, extent), out_shape=(vecto...  7.67 us
    pallas_call x1, Pallas kernels, per_device(): pl.pallas_call(functools.partial(first_kernel, extent, modes), out_shape=...  7.01 us
    pallas_call x1, Pallas kernels, per_device(): pl.pallas_call(functools.partial(order_kernel, extent), out_shape=(orderi...  3.93 us
    ppermute x3, starting transfers between devices, swap(): from_b = lax.ppermute(side_b, AXES, odds)  2.02 us
    pallas_call x1, Pallas kernels, per_device(): pl.pallas_call(functools.partial(near_kernel, extent, modes), out_shape=(...  1.7 us
    pallas_call x1, Pallas kernels, per_device(): pl.pallas_call(functools.partial(last_kernel, extent), out_shape=(shaped(...  1.63 us
  transfers between devices with their start and end apart: 6, of which 1 were waited for; matrix products, arithmetic and copies ran while one was open for 0% of the time, Pallas kernels for 8%

profile of v4, /device:TPU:0, one launch (start us, length us, event | category | flops | bytes accessed | tf_op | source)
XLA Modules:
  0.0 69.6 jit_solution(1091990977864479717)
XLA Ops:
  0.6 1.6 %shard_map.87 = (f32[136,1024]{1,0:T(8,128)S(1)}, f32[136,1024]{1,0:T(8,128)S(1)}, bf16[8,128,128]{2,1,0:T(8,128)(2,1)S(1)}, bf16[8,128,128]{2,1,0:T(8,128)(2,1)S(1)}) custom-call(f32[64,2,1024]{2,1,0:T(2,128)} %bitcast.10, f32[6,1,2048]{2,1,0:T(1,128)} %bitcast.12, bf16[16,128,128]{2,1,0:T(8,128)(2,1)} %bitcast.11), custom_call_target="tpu_custom_call" | custom-call | tf_op jit(solution)/shard_map/pallas_call | solution.py:625
  2.2 0.5 collective-permute-start.1
  2.7 0.7 collective-permute-start
  4.1 3.9 %shard_map.86 = (bf16[2048,2048]{1,0:T(8,128)(2,1)S(1)}, bf16[2048,2048]{1,0:T(8,128)(2,1)S(1)}, bf16[2048,2048]{1,0:T(8,128)(2,1)S(1)}, f32[1,1]{1,0:T(1,128)}) custom-call(s32[1,2048]{1,0:T(1,128)} %bitcast.13, f32[1,1]{1,0:T(1,128)S(6)} %copy.9.stiffness, bf16[2048,2048]{1,0:T(8,128)(2,1)} %far_operator.1), custom_call_target="tpu_custom_call" | custom-call | tf_op jit(solution)/shard_map/pallas_call | solution.py:641
  8.0 0.0 collective-permute-done.1.got
  8.0 1.7 %shard_map.88 = (f32[64,1024]{1,0:T(8,128)S(1)}, f32[64,1024]{1,0:T(8,128)S(1)}, bf16[96,1024]{1,0:T(8,128)(2,1)S(1)}, bf16[16,1024]{1,0:T(8,128)(2,1)S(1)}, bf1...) custom-call(f32[136,1024]{1,0:T(8,128)S(1)} %get-tuple-element.35.pay, ...), custom_call_target="tpu_custom_call" | custom-call | tf_op jit(solution)/shard_map/pallas_call | solution.py:655
  9.7 0.0 collective-permute-done.got
  9.7 0.0 copy-start
  9.7 7.0 %shard_map.89 = (f32[64,2048]{1,0:T(8,128)S(1)}, f32[64,2048]{1,0:T(8,128)S(1)}, bf16[96,2048]{1,0:T(8,128)(2,1)S(1)}, bf16[8,256,128]{2,1,0:T(8,128)(2,1)S(1)},...) custom-call(f32[1,1]{1,0:T(1,128)} %get-tuple-element.32.softness, ...), custom_call_target="tpu_custom_call" | custom-call | tf_op jit(solution)/shard_map/pallas_call | solution.py:670
  16.7 10.0 %collective-permute-start.2 = (f32[104,1024]{1,0:T(8,128)S(1)}, f32[104,1024]{1,0:T(8,128)S(1)}, u32[]{:S(2)}, u32[]{:S(2)}) collective-permute-start(f32[104,1024]{1,0:T(8,128)S(1)} %get-tuple-element.47.image_a), channel_id=1, source_target_pairs={{0,1},{2,3},{4,5},{6,7},{8,9},{10,11},{12,13},{14,15},{16,17},{18,... | collective-permute-start | bytes 1277960 | tf_op jit(solution)/shard_map/ppermute | solution.py:610
  26.8 0.7 collective-permute-start.3
  27.4 0.7 %collective-permute-done.2.got.got_a = f32[104,1024]{1,0:T(8,128)S(1)} collective-permute-done((f32[104,1024]{1,0:T(8,128)S(1)}, f32[104,1024]{1,0:T(8,128)S(1)}, u32[]{:S(2)}, u32[]{:S(2)}) %collective-permute-start.2) | collective-permute-done | bytes 426016 | tf_op jit(solution)/shard_map/ppermute | solution.py:610
  28.2 17.2 %all_to_all.10 = f32[96,4,128]{2,1,0:T(4,128)S(1)} all-to-all(f32[96,4,128]{2,1,0:T(4,128)S(1)} %bitcast.8), channel_id=1, replica_groups=mesh['cluster'=4,'member'=8] {'cluster','member'}, dimensions={0} | all-to-all | bytes 393216 | tf_op jit(solution)/shard_map/all_to_all | solution.py:615
  45.4 0.0 collective-permute-done.3.got_b
  45.4 0.0 copy-done
  45.4 7.7 %shard_map.92 = (f32[64,2048]{1,0:T(8,128)S(1)}, f32[64,2048]{1,0:T(8,128)S(1)}, f32[64,2048]{1,0:T(8,128)S(1)}, f32[64,1024]{1,0:T(8,128)S(1)}, f32[64,1024]{1,0:T(8,128)S(1)}, /*index=5*/f32[4,128]{1,0:T(4,128)S(1)}) custom-call(f32[1,1]{1,0:T(1,128)} %get-tuple-element.32.softness, f32[24,12,128]{2,1,0:T(8,128)S(1)} %shard_map.91.terms, ...), custom_call_target="tpu_custom_call" | custom-call | tf_op jit(solution)/shard_map/pallas_call | solution.py:708
  53.1 0.6 collective-permute-start.4
  53.7 0.7 collective-permute-start.5
  54.4 13.6 %all_to_all.11.scalars = f32[32,4,128]{2,1,0:T(4,128)S(1)} all-to-all(f32[32,4,128]{2,1,0:T(4,128)S(1)} %reshape.40), channel_id=1, replica_groups=mesh['cluster'=4,'member'=8] {'cluster','member'}, dimensions={0} | all-to-all | bytes 131072 | tf_op jit(solution)/shard_map/all_to_all | solution.py:615
  68.0 0.0 collective-permute-done.4.got_a
  68.0 0.0 collective-permute-done.5.got_b
  68.0 1.6 %shard_map.93 = (f32[64,2,1024]{2,1,0:T(2,128)}, f32[64,2,1024]{2,1,0:T(2,128)}) custom-call(f32[32,4,128]{2,1,0:T(4,128)S(1)} %all_to_all.11.scalars, f32[64,2048]{1,0:T(8,128)S(1)} %get-tuple-element.48.residual, f32[64,2048]{1,0:T(8,128)S(1)} %get-tuple-element.55.search, f32[64,2048]{1,0:T(8,128)S(1)} %get-tuple-element.56.applied, ...), custom_call_target="tpu_custom_call" | custom-call | tf_op jit(solution)/shard_map/pallas_call | solution.py:725
  (3 shorter events, 0.1 us)
Async XLA Ops:
  2.2 5.8 %collective-permute-start.1 = (f32[136,1024]{1,0:T(8,128)S(1)}, f32[136,1024]{1,0:T(8,128)S(1)}, u32[]{:S(2)}, u32[]{:S(2)}) collective-permute-start(f32[136,1024]{1,0:T(8,128)S(1)} %get-tuple-element.35.pay), channel_id=1, source_target_pairs={{0,1},{2,3},{4,5},{6,7},{8,9},{10,11},{12,13},{14,15},{16,17},{18,... | collective-permute-start | bytes 1671176 | tf_op jit(solution)/shard_map/ppermute | solution.py:610
  2.7 7.0 %collective-permute-start = (f32[136,1024]{1,0:T(8,128)S(1)}, f32[136,1024]{1,0:T(8,128)S(1)}, u32[]{:S(2)}, u32[]{:S(2)}) collective-permute-start(f32[136,1024]{1,0:T(8,128)S(1)} %get-tuple-element.33.pay), channel_id=1, source_target_pairs={{1,2},{3,4},{5,6},{7,8},{9,10},{11,12},{13,14},{15,16},{17,18},{19... | collective-permute-start | bytes 1671176 | tf_op jit(solution)/shard_map/ppermute | solution.py:609
  9.7 35.7 %copy-start = (f32[24,24]{1,0:T(8,128)S(1)}, f32[24,24]{1,0:T(8,128)}, u32[]{:S(2)}) copy-start(f32[24,24]{1,0:T(8,128)} %inverse.1) | copy-start | bytes 6916
  16.7 11.4 %collective-permute-start.2 = (f32[104,1024]{1,0:T(8,128)S(1)}, f32[104,1024]{1,0:T(8,128)S(1)}, u32[]{:S(2)}, u32[]{:S(2)}) collective-permute-start(f32[104,1024]{1,0:T(8,128)S(1)} %get-tuple-element.47.image_a), channel_id=1, source_target_pairs={{0,1},{2,3},{4,5},{6,7},{8,9},{10,11},{12,13},{14,15},{16,17},{18,... | collective-permute-start | bytes 1277960 | tf_op jit(solution)/shard_map/ppermute | solution.py:610
  26.8 18.7 %collective-permute-start.3 = (f32[96,1024]{1,0:T(8,128)S(1)}, f32[96,1024]{1,0:T(8,128)S(1)}, u32[]{:S(2)}, u32[]{:S(2)}) collective-permute-start(f32[96,1024]{1,0:T(8,128)S(1)} %get-tuple-element.53.image_b), channel_id=1, source_target_pairs={{1,2},{3,4},{5,6},{7,8},{9,10},{11,12},{13,14},{15,16},{17,18},{19... | collective-permute-start | bytes 1179656 | tf_op jit(solution)/shard_map/ppermute | solution.py:609
  53.1 14.8 %collective-permute-start.4 = (f32[64,1024]{1,0:T(8,128)S(1)}, f32[64,1024]{1,0:T(8,128)S(1)}, u32[]{:S(2)}, u32[]{:S(2)}) collective-permute-start(f32[64,1024]{1,0:T(8,128)S(1)} %get-tuple-element.58.next_a), channel_id=1, source_target_pairs={{0,1},{2,3},{4,5},{6,7},{8,9},{10,11},{12,13},{14,15},{16,17},{18,... | collective-permute-start | bytes 786440 | tf_op jit(solution)/shard_map/ppermute | solution.py:610
  53.7 14.3 %collective-permute-start.5 = (f32[64,1024]{1,0:T(8,128)S(1)}, f32[64,1024]{1,0:T(8,128)S(1)}, u32[]{:S(2)}, u32[]{:S(2)}) collective-permute-start(f32[64,1024]{1,0:T(8,128)S(1)} %get-tuple-element.59.next_b), channel_id=1, source_target_pairs={{1,2},{3,4},{5,6},{7,8},{9,10},{11,12},{13,14},{15,16},{17,18},{19... | collective-permute-start | bytes 786440 | tf_op jit(solution)/shard_map/ppermute | solution.py:609

commit v5 on v4

--- a/solution.py
+++ b/solution.py
@@ -14,7 +14,6 @@
 EXACT = lax.Precision.HIGHEST
 SLICE = 4
 KP = 8
-TILE = 1024
 
 
 def dot(left, right):
@@ -192,17 +191,15 @@
     slots = second.shape[1]
     face = slots // 2
 
-    @pl.loop(0, slots // TILE)
-    def _(tile):
-        cols = pl.ds(pl.multiple_of(tile * TILE, TILE), TILE)
-        product = dot(second[...], operator[:, cols])
-        high, low = two_parts(product[:rows] + product[rows:])
-        third[:rows, cols] = high
-        third[rows:, cols] = low
-
-    for side, image in ((0, image_a), (1, image_b)):
-        product = dot(third[...], place[:, side * face : (side + 1) * face])
-        image[:rows, :] = scale * (product[:rows] + product[rows:])
+    product = dot(second[...], operator[...])
+    high, low = two_parts(product[:rows] + product[rows:])
+    third[:rows, :] = high
+    third[rows:, :] = low
+
+    product = dot(third[...], place[...])
+    product = scale * (product[:rows] + product[rows:])
+    image_a[:rows, :] = product[:, :face]
+    image_b[:rows, :] = product[:, face:]
 
 
 def smooth_block(value, weight, block_pair):
@@ -274,13 +271,9 @@
         modes, 0, here.weights[0], here.same[0], pay, got, blocks,
         residual, smooth, coarse, own_basis, pairs, first,
     )
-    slots = second.shape[1]
     face = first.shape[1]
 
-    @pl.loop(0, slots // TILE)
-    def _(tile):
-        cols = pl.ds(pl.multiple_of(tile * TILE, TILE), TILE)
-        second[:, cols] = dot(first[...], pick[:face, cols]).astype(BF16)
+    second[...] = dot(first[...], pick[:face, :]).astype(BF16)
 
 
 def first_kernel(
@@ -300,11 +293,8 @@
         residual, smooth, coarse, own_basis, pairs, first,
     )
 
-    @pl.loop(0, slots // TILE)
-    def _(tile):
-        cols = pl.ds(pl.multiple_of(tile * TILE, TILE), TILE)
-        product = dot(first[:, face:], pick[face:, cols]) + second_a[:, cols].astype(F32)
-        second[:, cols] = product.astype(BF16)
+    product = dot(first[:, face:], pick[face:, :]) + second_a[...].astype(F32)
+    second[...] = product.astype(BF16)
 
     for whole, part in (
         (residual, residual_a), (smooth, smooth_a), (coarse, coarse_a),
@@ -520,10 +510,7 @@
         weighted(image_projected, changed),
     ]
 
-    @pl.loop(0, slots // TILE)
-    def _(tile):
-        cols = pl.ds(pl.multiple_of(tile * TILE, TILE), TILE)
-        second[:, cols] = dot(first[...], pick[:, cols]).astype(BF16)
+    second[...] = dot(first[...], pick[...]).astype(BF16)
 
     apply_rest(loads, softness[...], operator, place, second, third, next_a, next_b)
 

time: 69.9 us -> 67.9 us (0.971)
  Pallas kernels: 23.6 us -> 21.2 us
    pallas_call x1, Pallas kernels: 7.01 us -> 6.01 us  [per_device(): pl.pallas_call(functools.partial(first_kernel, extent, modes), out_shape=...]
    pallas_call x1, Pallas kernels: 7.67 us -> 6.73 us  [per_device(): pl.pallas_call(functools.partial(second_kernel, extent), out_shape=(vecto...]
where the time goes in v5:
time: 67.9 us; the launch traced here: 67.6 us
  blocking collectives  30.8 us (45%)
  Pallas kernels  21.2 us (31%)
  starting transfers between devices  13.5 us (20%)
  between operations  1.39 us (2%)
  waiting for transfers between devices  0.73 us (1%)
    all_to_all x2, blocking collectives, share(): return lax.all_to_all(parts, AXES, 0, 0, tiled=True).reshape(copies.shape)  30.8 us
    ppermute x3, starting transfers between devices, swap(): from_a = lax.ppermute(side_a, AXES, evens)  11.5 us
    pallas_call x1, Pallas kernels, per_device(): pl.pallas_call(functools.partial(second_kernel, extent), out_shape=(vecto...  6.73 us
    pallas_call x1, Pallas kernels, per_device(): pl.pallas_call(functools.partial(first_kernel, extent, modes), out_shape=...  6.01 us
    pallas_call x1, Pallas kernels, per_device(): pl.pallas_call(functools.partial(order_kernel, extent), out_shape=(orderi...  3.93 us
    ppermute x3, starting transfers between devices, swap(): from_b = lax.ppermute(side_b, AXES, odds)  2.02 us
    pallas_call x1, Pallas kernels, per_device(): pl.pallas_call(functools.partial(last_kernel, extent), out_shape=(shaped(...  1.63 us
    pallas_call x1, Pallas kernels, per_device(): pl.pallas_call(functools.partial(pack_kernel, extent), out_shape=(packed,...  1.56 us
  transfers between devices with their start and end apart: 6, of which 1 were waited for; matrix products, arithmetic and copies ran while one was open for 0% of the time, Pallas kernels for 8%

profile of v5, /device:TPU:0, one launch (start us, length us, event | category | flops | bytes accessed | tf_op | source)
XLA Modules:
  0.0 67.6 jit_solution(5562472080380051283)
XLA Ops:
  0.6 1.6 %shard_map.87 = (f32[136,1024]{1,0:T(8,128)S(1)}, f32[136,1024]{1,0:T(8,128)S(1)}, bf16[8,128,128]{2,1,0:T(8,128)(2,1)S(1)}, bf16[8,128,128]{2,1,0:T(8,128)(2,1)S(1)}) custom-call(f32[64,2,1024]{2,1,0:T(2,128)} %bitcast.10, f32[6,1,2048]{2,1,0:T(1,128)} %bitcast.12, bf16[16,128,128]{2,1,0:T(8,128)(2,1)} %bitcast.11), custom_call_target="tpu_custom_call" | custom-call | tf_op jit(solution)/shard_map/pallas_call | solution.py:612
  2.2 0.5 collective-permute-start.1
  2.7 0.7 %collective-permute-start = (f32[136,1024]{1,0:T(8,128)S(1)}, f32[136,1024]{1,0:T(8,128)S(1)}, u32[]{:S(2)}, u32[]{:S(2)}) collective-permute-start(f32[136,1024]{1,0:T(8,128)S(1)} %get-tuple-element.33.pay), channel_id=1, source_target_pairs={{1,2},{3,4},{5,6},{7,8},{9,10},{11,12},{13,14},{15,16},{17,18},{19... | collective-permute-start | bytes 1671176 | tf_op jit(solution)/shard_map/ppermute | solution.py:596
  4.1 3.9 %shard_map.86 = (bf16[2048,2048]{1,0:T(8,128)(2,1)S(1)}, bf16[2048,2048]{1,0:T(8,128)(2,1)S(1)}, bf16[2048,2048]{1,0:T(8,128)(2,1)S(1)}, f32[1,1]{1,0:T(1,128)}) custom-call(s32[1,2048]{1,0:T(1,128)} %bitcast.13, f32[1,1]{1,0:T(1,128)S(6)} %copy.9.stiffness, bf16[2048,2048]{1,0:T(8,128)(2,1)} %far_operator.1), custom_call_target="tpu_custom_call" | custom-call | tf_op jit(solution)/shard_map/pallas_call | solution.py:628
  8.0 0.0 collective-permute-done.1.got
  8.0 1.3 %shard_map.88 = (f32[64,1024]{1,0:T(8,128)S(1)}, f32[64,1024]{1,0:T(8,128)S(1)}, bf16[96,1024]{1,0:T(8,128)(2,1)S(1)}, bf16[16,1024]{1,0:T(8,128)(2,1)S(1)}, bf1...) custom-call(f32[136,1024]{1,0:T(8,128)S(1)} %get-tuple-element.35.pay, ...), custom_call_target="tpu_custom_call" | custom-call | tf_op jit(solution)/shard_map/pallas_call | solution.py:642
  9.3 0.0 collective-permute-done.got
  9.3 0.0 copy-start
  9.4 6.0 %shard_map.89 = (f32[64,2048]{1,0:T(8,128)S(1)}, f32[64,2048]{1,0:T(8,128)S(1)}, bf16[96,2048]{1,0:T(8,128)(2,1)S(1)}, bf16[8,256,128]{2,1,0:T(8,128)(2,1)S(1)},...) custom-call(f32[1,1]{1,0:T(1,128)} %get-tuple-element.32.softness, ...), custom_call_target="tpu_custom_call" | custom-call | tf_op jit(solution)/shard_map/pallas_call | solution.py:657
  15.4 10.4 %collective-permute-start.2 = (f32[104,1024]{1,0:T(8,128)S(1)}, f32[104,1024]{1,0:T(8,128)S(1)}, u32[]{:S(2)}, u32[]{:S(2)}) collective-permute-start(f32[104,1024]{1,0:T(8,128)S(1)} %get-tuple-element.47.image_a), channel_id=1, source_target_pairs={{0,1},{2,3},{4,5},{6,7},{8,9},{10,11},{12,13},{14,15},{16,17},{18,... | collective-permute-start | bytes 1277960 | tf_op jit(solution)/shard_map/ppermute | solution.py:597
  25.8 0.7 collective-permute-start.3
  26.4 0.7 %collective-permute-done.2.got.got_a = f32[104,1024]{1,0:T(8,128)S(1)} collective-permute-done((f32[104,1024]{1,0:T(8,128)S(1)}, f32[104,1024]{1,0:T(8,128)S(1)}, u32[]{:S(2)}, u32[]{:S(2)}) %collective-permute-start.2) | collective-permute-done | bytes 426016 | tf_op jit(solution)/shard_map/ppermute | solution.py:597
  27.2 17.2 %all_to_all.10 = f32[96,4,128]{2,1,0:T(4,128)S(1)} all-to-all(f32[96,4,128]{2,1,0:T(4,128)S(1)} %bitcast.8), channel_id=1, replica_groups=mesh['cluster'=4,'member'=8] {'cluster','member'}, dimensions={0} | all-to-all | bytes 393216 | tf_op jit(solution)/shard_map/all_to_all | solution.py:602
  44.4 0.0 collective-permute-done.3.got_b
  44.4 0.0 copy-done
  44.4 6.7 %shard_map.92 = (f32[64,2048]{1,0:T(8,128)S(1)}, f32[64,2048]{1,0:T(8,128)S(1)}, f32[64,2048]{1,0:T(8,128)S(1)}, f32[64,1024]{1,0:T(8,128)S(1)}, f32[64,1024]{1,0:T(8,128)S(1)}, /*index=5*/f32[4,128]{1,0:T(4,128)S(1)}) custom-call(f32[1,1]{1,0:T(1,128)} %get-tuple-element.32.softness, f32[24,12,128]{2,1,0:T(8,128)S(1)} %shard_map.91.terms, ...), custom_call_target="tpu_custom_call" | custom-call | tf_op jit(solution)/shard_map/pallas_call | solution.py:695
  51.2 0.6 collective-permute-start.4
  51.8 0.7 collective-permute-start.5
  52.4 13.6 %all_to_all.11.scalars = f32[32,4,128]{2,1,0:T(4,128)S(1)} all-to-all(f32[32,4,128]{2,1,0:T(4,128)S(1)} %reshape.40), channel_id=1, replica_groups=mesh['cluster'=4,'member'=8] {'cluster','member'}, dimensions={0} | all-to-all | bytes 131072 | tf_op jit(solution)/shard_map/all_to_all | solution.py:602
  66.0 0.0 collective-permute-done.4.got_a
  66.0 0.0 collective-permute-done.5.got_b
  66.0 1.6 %shard_map.93 = (f32[64,2,1024]{2,1,0:T(2,128)}, f32[64,2,1024]{2,1,0:T(2,128)}) custom-call(f32[32,4,128]{2,1,0:T(4,128)S(1)} %all_to_all.11.scalars, f32[64,2048]{1,0:T(8,128)S(1)} %get-tuple-element.48.residual, f32[64,2048]{1,0:T(8,128)S(1)} %get-tuple-element.55.search, f32[64,2048]{1,0:T(8,128)S(1)} %get-tuple-element.56.applied, ...), custom_call_target="tpu_custom_call" | custom-call | tf_op jit(solution)/shard_map/pallas_call | solution.py:712
  (3 shorter events, 0.1 us)
Async XLA Ops:
  2.2 5.8 %collective-permute-start.1 = (f32[136,1024]{1,0:T(8,128)S(1)}, f32[136,1024]{1,0:T(8,128)S(1)}, u32[]{:S(2)}, u32[]{:S(2)}) collective-permute-start(f32[136,1024]{1,0:T(8,128)S(1)} %get-tuple-element.35.pay), channel_id=1, source_target_pairs={{0,1},{2,3},{4,5},{6,7},{8,9},{10,11},{12,13},{14,15},{16,17},{18,... | collective-permute-start | bytes 1671176 | tf_op jit(solution)/shard_map/ppermute | solution.py:597
  2.7 6.6 %collective-permute-start = (f32[136,1024]{1,0:T(8,128)S(1)}, f32[136,1024]{1,0:T(8,128)S(1)}, u32[]{:S(2)}, u32[]{:S(2)}) collective-permute-start(f32[136,1024]{1,0:T(8,128)S(1)} %get-tuple-element.33.pay), channel_id=1, source_target_pairs={{1,2},{3,4},{5,6},{7,8},{9,10},{11,12},{13,14},{15,16},{17,18},{19... | collective-permute-start | bytes 1671176 | tf_op jit(solution)/shard_map/ppermute | solution.py:596
  9.3 35.1 %copy-start = (f32[24,24]{1,0:T(8,128)S(1)}, f32[24,24]{1,0:T(8,128)}, u32[]{:S(2)}) copy-start(f32[24,24]{1,0:T(8,128)} %inverse.1) | copy-start | bytes 6916
  15.4 11.8 %collective-permute-start.2 = (f32[104,1024]{1,0:T(8,128)S(1)}, f32[104,1024]{1,0:T(8,128)S(1)}, u32[]{:S(2)}, u32[]{:S(2)}) collective-permute-start(f32[104,1024]{1,0:T(8,128)S(1)} %get-tuple-element.47.image_a), channel_id=1, source_target_pairs={{0,1},{2,3},{4,5},{6,7},{8,9},{10,11},{12,13},{14,15},{16,17},{18,... | collective-permute-start | bytes 1277960 | tf_op jit(solution)/shard_map/ppermute | solution.py:597
  25.8 18.7 %collective-permute-start.3 = (f32[96,1024]{1,0:T(8,128)S(1)}, f32[96,1024]{1,0:T(8,128)S(1)}, u32[]{:S(2)}, u32[]{:S(2)}) collective-permute-start(f32[96,1024]{1,0:T(8,128)S(1)} %get-tuple-element.53.image_b), channel_id=1, source_target_pairs={{1,2},{3,4},{5,6},{7,8},{9,10},{11,12},{13,14},{15,16},{17,18},{19... | collective-permute-start | bytes 1179656 | tf_op jit(solution)/shard_map/ppermute | solution.py:596
  51.2 14.8 %collective-permute-start.4 = (f32[64,1024]{1,0:T(8,128)S(1)}, f32[64,1024]{1,0:T(8,128)S(1)}, u32[]{:S(2)}, u32[]{:S(2)}) collective-permute-start(f32[64,1024]{1,0:T(8,128)S(1)} %get-tuple-element.58.next_a), channel_id=1, source_target_pairs={{0,1},{2,3},{4,5},{6,7},{8,9},{10,11},{12,13},{14,15},{16,17},{18,... | collective-permute-start | bytes 786440 | tf_op jit(solution)/shard_map/ppermute | solution.py:597
  51.8 14.3 %collective-permute-start.5 = (f32[64,1024]{1,0:T(8,128)S(1)}, f32[64,1024]{1,0:T(8,128)S(1)}, u32[]{:S(2)}, u32[]{:S(2)}) collective-permute-start(f32[64,1024]{1,0:T(8,128)S(1)} %get-tuple-element.59.next_b), channel_id=1, source_target_pairs={{1,2},{3,4},{5,6},{7,8},{9,10},{11,12},{13,14},{15,16},{17,18},{19... | collective-permute-start | bytes 786440 | tf_op jit(solution)/shard_map/ppermute | solution.py:596

commit v6 on v5

--- a/solution.py
+++ b/solution.py
@@ -631,6 +631,7 @@
         in_specs=[HBM, VMEM, HBM],
         out_specs=(VMEM,) * 4,
         scratch_shapes=[pltpu.VMEM((1, slots), jnp.int32), pltpu.SemaphoreType.DMA((2,))],
+        cost_estimate=pl.CostEstimate(flops=10**11, transcendentals=0, bytes_accessed=10**8),
         compiler_params=params(8),
     )(in_hbm(index_map.reshape(1, slots)), stiffness, in_hbm(dual_operator))
     pick, operator, place = [

time: 67.9 us -> 67 us (0.987)
  blocking collectives: 30.8 us -> 29.9 us
    all_to_all x2, blocking collectives: 30.8 us -> 29.9 us  [share(): return lax.all_to_all(parts, AXES, 0, 0, tiled=True).reshape(copies.shape)]
where the time goes in v6:
time: 67 us; the launch traced here: 66.7 us
  blocking collectives  29.9 us (45%)
  Pallas kernels  21.2 us (32%)
  starting transfers between devices  13.4 us (20%)
  between operations  1.39 us (2%)
  waiting for transfers between devices  0.73 us (1%)
    all_to_all x2, blocking collectives, share(): return lax.all_to_all(parts, AXES, 0, 0, tiled=True).reshape(copies.shape)  29.9 us
    ppermute x3, starting transfers between devices, swap(): from_a = lax.ppermute(side_a, AXES, evens)  11.4 us
    pallas_call x1, Pallas kernels, per_device(): pl.pallas_call(functools.partial(second_kernel, extent), out_shape=(vecto...  6.73 us
    pallas_call x1, Pallas kernels, per_device(): pl.pallas_call(functools.partial(first_kernel, extent, modes), out_shape=...  6.01 us
    pallas_call x1, Pallas kernels, per_device(): pl.pallas_call(functools.partial(order_kernel, extent), out_shape=(orderi...  3.93 us
    ppermute x3, starting transfers between devices, swap(): from_b = lax.ppermute(side_b, AXES, odds)  2.04 us
    pallas_call x1, Pallas kernels, per_device(): pl.pallas_call(functools.partial(last_kernel, extent), out_shape=(shaped(...  1.63 us
    pallas_call x1, Pallas kernels, per_device(): pl.pallas_call(functools.partial(pack_kernel, extent), out_shape=(packed,...  1.56 us
  transfers between devices with their start and end apart: 6, of which 1 were waited for; matrix products, arithmetic and copies ran while one was open for 0% of the time, Pallas kernels for 8%

profile of v6, /device:TPU:0, one launch (start us, length us, event | category | flops | bytes accessed | tf_op | source)
XLA Modules:
  0.0 66.7 jit_solution(5017764539822499460)
XLA Ops:
  0.6 1.6 %shard_map.87 = (f32[136,1024]{1,0:T(8,128)S(1)}, f32[136,1024]{1,0:T(8,128)S(1)}, bf16[8,128,128]{2,1,0:T(8,128)(2,1)S(1)}, bf16[8,128,128]{2,1,0:T(8,128)(2,1)S(1)}) custom-call(f32[64,2,1024]{2,1,0:T(2,128)} %bitcast.10, f32[6,1,2048]{2,1,0:T(1,128)} %bitcast.12, bf16[16,128,128]{2,1,0:T(8,128)(2,1)} %bitcast.11), custom_call_target="tpu_custom_call" | custom-call | tf_op jit(solution)/shard_map/pallas_call | solution.py:612
  2.2 0.7 %collective-permute-start = (f32[136,1024]{1,0:T(8,128)S(1)}, f32[136,1024]{1,0:T(8,128)S(1)}, u32[]{:S(2)}, u32[]{:S(2)}) collective-permute-start(f32[136,1024]{1,0:T(8,128)S(1)} %get-tuple-element.33.pay), channel_id=1, source_target_pairs={{1,2},{3,4},{5,6},{7,8},{9,10},{11,12},{13,14},{15,16},{17,18},{19... | collective-permute-start | bytes 1671176 | tf_op jit(solution)/shard_map/ppermute | solution.py:596
  2.9 4.3 %collective-permute-start.1 = (f32[136,1024]{1,0:T(8,128)S(1)}, f32[136,1024]{1,0:T(8,128)S(1)}, u32[]{:S(2)}, u32[]{:S(2)}) collective-permute-start(f32[136,1024]{1,0:T(8,128)S(1)} %get-tuple-element.35.pay), channel_id=1, source_target_pairs={{0,1},{2,3},{4,5},{6,7},{8,9},{10,11},{12,13},{14,15},{16,17},{18,... | collective-permute-start | bytes 1671176 | tf_op jit(solution)/shard_map/ppermute | solution.py:597
  7.9 3.9 %shard_map.86 = (bf16[2048,2048]{1,0:T(8,128)(2,1)S(1)}, bf16[2048,2048]{1,0:T(8,128)(2,1)S(1)}, bf16[2048,2048]{1,0:T(8,128)(2,1)S(1)}, f32[1,1]{1,0:T(1,128)}) custom-call(s32[1,2048]{1,0:T(1,128)} %bitcast.15, f32[1,1]{1,0:T(1,128)S(6)} %copy.9.stiffness, bf16[2048,2048]{1,0:T(8,128)(2,1)} %far_operator.1), custom_call_target="tpu_custom_call" | custom-call | flops 99999997952 | bytes 100000000 | tf_op jit(solution)/shard_map/pallas_call | solution.py:628
  11.8 0.0 collective-permute-done.1.got
  11.8 1.3 %shard_map.88 = (f32[64,1024]{1,0:T(8,128)S(1)}, f32[64,1024]{1,0:T(8,128)S(1)}, bf16[96,1024]{1,0:T(8,128)(2,1)S(1)}, bf16[16,1024]{1,0:T(8,128)(2,1)S(1)}, bf1...) custom-call(f32[136,1024]{1,0:T(8,128)S(1)} %get-tuple-element.35.pay, ...), custom_call_target="tpu_custom_call" | custom-call | tf_op jit(solution)/shard_map/pallas_call | solution.py:643
  13.2 0.0 collective-permute-done.got
  13.2 0.0 copy-start
  13.2 6.0 %shard_map.89 = (f32[64,2048]{1,0:T(8,128)S(1)}, f32[64,2048]{1,0:T(8,128)S(1)}, bf16[96,2048]{1,0:T(8,128)(2,1)S(1)}, bf16[8,256,128]{2,1,0:T(8,128)(2,1)S(1)},...) custom-call(f32[1,1]{1,0:T(1,128)} %get-tuple-element.32.softness, ...), custom_call_target="tpu_custom_call" | custom-call | tf_op jit(solution)/shard_map/pallas_call | solution.py:658
  19.2 6.5 %collective-permute-start.2 = (f32[104,1024]{1,0:T(8,128)S(1)}, f32[104,1024]{1,0:T(8,128)S(1)}, u32[]{:S(2)}, u32[]{:S(2)}) collective-permute-start(f32[104,1024]{1,0:T(8,128)S(1)} %get-tuple-element.47.image_a), channel_id=1, source_target_pairs={{0,1},{2,3},{4,5},{6,7},{8,9},{10,11},{12,13},{14,15},{16,17},{18,... | collective-permute-start | bytes 1277960 | tf_op jit(solution)/shard_map/ppermute | solution.py:597
  25.7 0.7 %collective-permute-start.3 = (f32[96,1024]{1,0:T(8,128)S(1)}, f32[96,1024]{1,0:T(8,128)S(1)}, u32[]{:S(2)}, u32[]{:S(2)}) collective-permute-start(f32[96,1024]{1,0:T(8,128)S(1)} %get-tuple-element.53.image_b), channel_id=1, source_target_pairs={{1,2},{3,4},{5,6},{7,8},{9,10},{11,12},{13,14},{15,16},{17,18},{19... | collective-permute-start | bytes 1179656 | tf_op jit(solution)/shard_map/ppermute | solution.py:596
  26.4 0.7 %collective-permute-done.2.got.got_a = f32[104,1024]{1,0:T(8,128)S(1)} collective-permute-done((f32[104,1024]{1,0:T(8,128)S(1)}, f32[104,1024]{1,0:T(8,128)S(1)}, u32[]{:S(2)}, u32[]{:S(2)}) %collective-permute-start.2) | collective-permute-done | bytes 426016 | tf_op jit(solution)/shard_map/ppermute | solution.py:597
  27.1 16.8 %all_to_all.10 = f32[96,4,128]{2,1,0:T(4,128)S(1)} all-to-all(f32[96,4,128]{2,1,0:T(4,128)S(1)} %bitcast.8), channel_id=1, replica_groups=mesh['cluster'=4,'member'=8] {'cluster','member'}, dimensions={0} | all-to-all | bytes 393216 | tf_op jit(solution)/shard_map/all_to_all | solution.py:602
  43.9 0.0 collective-permute-done.3.got_b
  43.9 0.0 copy-done
  43.9 6.7 %shard_map.92 = (f32[64,2048]{1,0:T(8,128)S(1)}, f32[64,2048]{1,0:T(8,128)S(1)}, f32[64,2048]{1,0:T(8,128)S(1)}, f32[64,1024]{1,0:T(8,128)S(1)}, f32[64,1024]{1,0:T(8,128)S(1)}, /*index=5*/f32[4,128]{1,0:T(4,128)S(1)}) custom-call(f32[1,1]{1,0:T(1,128)} %get-tuple-element.32.softness, f32[24,12,128]{2,1,0:T(8,128)S(1)} %shard_map.91.terms, ...), custom_call_target="tpu_custom_call" | custom-call | tf_op jit(solution)/shard_map/pallas_call | solution.py:696
  50.7 0.6 collective-permute-start.4
  51.3 0.7 collective-permute-start.5
  51.9 13.2 %all_to_all.11.scalars = f32[32,4,128]{2,1,0:T(4,128)S(1)} all-to-all(f32[32,4,128]{2,1,0:T(4,128)S(1)} %reshape.40), channel_id=1, replica_groups=mesh['cluster'=4,'member'=8] {'cluster','member'}, dimensions={0} | all-to-all | bytes 131072 | tf_op jit(solution)/shard_map/all_to_all | solution.py:602
  65.1 0.0 collective-permute-done.4.got_a
  65.1 0.0 collective-permute-done.5.got_b
  65.1 1.6 %shard_map.93 = (f32[64,2,1024]{2,1,0:T(2,128)}, f32[64,2,1024]{2,1,0:T(2,128)}) custom-call(f32[32,4,128]{2,1,0:T(4,128)S(1)} %all_to_all.11.scalars, f32[64,2048]{1,0:T(8,128)S(1)} %get-tuple-element.48.residual, f32[64,2048]{1,0:T(8,128)S(1)} %get-tuple-element.55.search, f32[64,2048]{1,0:T(8,128)S(1)} %get-tuple-element.56.applied, ...), custom_call_target="tpu_custom_call" | custom-call | tf_op jit(solution)/shard_map/pallas_call | solution.py:713
  (3 shorter events, 0.1 us)
Async XLA Ops:
  2.2 11.0 %collective-permute-start = (f32[136,1024]{1,0:T(8,128)S(1)}, f32[136,1024]{1,0:T(8,128)S(1)}, u32[]{:S(2)}, u32[]{:S(2)}) collective-permute-start(f32[136,1024]{1,0:T(8,128)S(1)} %get-tuple-element.33.pay), channel_id=1, source_target_pairs={{1,2},{3,4},{5,6},{7,8},{9,10},{11,12},{13,14},{15,16},{17,18},{19... | collective-permute-start | bytes 1671176 | tf_op jit(solution)/shard_map/ppermute | solution.py:596
  2.9 8.9 %collective-permute-start.1 = (f32[136,1024]{1,0:T(8,128)S(1)}, f32[136,1024]{1,0:T(8,128)S(1)}, u32[]{:S(2)}, u32[]{:S(2)}) collective-permute-start(f32[136,1024]{1,0:T(8,128)S(1)} %get-tuple-element.35.pay), channel_id=1, source_target_pairs={{0,1},{2,3},{4,5},{6,7},{8,9},{10,11},{12,13},{14,15},{16,17},{18,... | collective-permute-start | bytes 1671176 | tf_op jit(solution)/shard_map/ppermute | solution.py:597
  13.2 30.7 %copy-start = (f32[24,24]{1,0:T(8,128)S(1)}, f32[24,24]{1,0:T(8,128)}, u32[]{:S(2)}) copy-start(f32[24,24]{1,0:T(8,128)} %inverse.1) | copy-start | bytes 6916
  19.2 7.9 %collective-permute-start.2 = (f32[104,1024]{1,0:T(8,128)S(1)}, f32[104,1024]{1,0:T(8,128)S(1)}, u32[]{:S(2)}, u32[]{:S(2)}) collective-permute-start(f32[104,1024]{1,0:T(8,128)S(1)} %get-tuple-element.47.image_a), channel_id=1, source_target_pairs={{0,1},{2,3},{4,5},{6,7},{8,9},{10,11},{12,13},{14,15},{16,17},{18,... | collective-permute-start | bytes 1277960 | tf_op jit(solution)/shard_map/ppermute | solution.py:597
  25.7 18.2 %collective-permute-start.3 = (f32[96,1024]{1,0:T(8,128)S(1)}, f32[96,1024]{1,0:T(8,128)S(1)}, u32[]{:S(2)}, u32[]{:S(2)}) collective-permute-start(f32[96,1024]{1,0:T(8,128)S(1)} %get-tuple-element.53.image_b), channel_id=1, source_target_pairs={{1,2},{3,4},{5,6},{7,8},{9,10},{11,12},{13,14},{15,16},{17,18},{19... | collective-permute-start | bytes 1179656 | tf_op jit(solution)/shard_map/ppermute | solution.py:596
  50.7 14.5 %collective-permute-start.4 = (f32[64,1024]{1,0:T(8,128)S(1)}, f32[64,1024]{1,0:T(8,128)S(1)}, u32[]{:S(2)}, u32[]{:S(2)}) collective-permute-start(f32[64,1024]{1,0:T(8,128)S(1)} %get-tuple-element.58.next_a), channel_id=1, source_target_pairs={{0,1},{2,3},{4,5},{6,7},{8,9},{10,11},{12,13},{14,15},{16,17},{18,... | collective-permute-start | bytes 786440 | tf_op jit(solution)/shard_map/ppermute | solution.py:597
  51.3 13.9 %collective-permute-start.5 = (f32[64,1024]{1,0:T(8,128)S(1)}, f32[64,1024]{1,0:T(8,128)S(1)}, u32[]{:S(2)}, u32[]{:S(2)}) collective-permute-start(f32[64,1024]{1,0:T(8,128)S(1)} %get-tuple-element.59.next_b), channel_id=1, source_target_pairs={{1,2},{3,4},{5,6},{7,8},{9,10},{11,12},{13,14},{15,16},{17,18},{19... | collective-permute-start | bytes 786440 | tf_op jit(solution)/shard_map/ppermute | solution.py:596

commit v7 on v6

--- a/solution.py
+++ b/solution.py
@@ -78,8 +78,8 @@
     return Chain(parity == 1, own, tuple(near), tuple(weights), tuple(same))
 
 
-def pack_side(first, load, basis, blocks, out, mine):
-    loads, _, face = load.shape
+def pack_side(first, basis, blocks, out):
+    face = basis.shape[2] // 2
     modes = basis.shape[0]
     half = blocks.shape[0] // 2
     size = blocks.shape[1]
@@ -94,8 +94,6 @@
     base = jnp.where(first, 0, half)
     for pair in range(half // 2):
         one, two = blocks[base + 2 * pair], blocks[base + 2 * pair + 1]
-        mine[2 * pair] = one
-        mine[2 * pair + 1] = two
         upper, lower = one.astype(F32), two.astype(F32)
         both = jnp.where(row <= col, upper, lower)
         left = pair * size
@@ -104,28 +102,32 @@
         out[:mid, right : right + size] = both[mid:]
         diagonal = jnp.sum(jnp.where(row == col, lower, 0.0), axis=0, keepdims=True)
         out[mid + modes : mid + modes + 1, left : left + size] = diagonal
-    out[low:, :] = jnp.where(first, load[:, 0, :], load[:, 1, :])
 
 
 def pack_kernel(
     extent,
     far_load, far_basis, far_blocks,
-    out_a, out_b, mine_a, mine_b,
-    load, basis, blocks, arrived,
+    out_a, out_b, blocks,
+    load, basis, arrived,
 ):
     copies = [
         pltpu.make_async_copy(source, target, arrived.at[k])
         for k, (source, target) in enumerate(
-            ((far_blocks, blocks), (far_load, load), (far_basis, basis))
+            ((far_blocks, blocks), (far_basis, basis), (far_load, load))
         )
     ]
     for copy in copies:
         copy.start()
-    for copy in copies:
+    for copy in copies[:2]:
         copy.wait()
     odd = chain(*extent).odd
-    pack_side(jnp.logical_not(odd), load, basis, blocks, out_b, mine_b)
-    pack_side(odd, load, basis, blocks, out_a, mine_a)
+    pack_side(jnp.logical_not(odd), basis, blocks, out_b)
+    pack_side(odd, basis, blocks, out_a)
+    copies[2].wait()
+    low = blocks.shape[1] // 2 + KP
+    load_0, load_1 = load[:, 0, :], load[:, 1, :]
+    out_b[low:, :] = jnp.where(odd, load_1, load_0)
+    out_a[low:, :] = jnp.where(odd, load_0, load_1)
 
 
 def order_kernel(
@@ -213,9 +215,9 @@
 
 
 def side_part(
-    modes, at, weight, same, pay, got, blocks, residual, smooth, coarse, own_basis, pairs, first
+    modes, at, weight, same, base, pay, got, blocks, residual, smooth, coarse, own_basis, pairs, first
 ):
-    half, size, _ = blocks.shape
+    half, size = blocks.shape[0] // 2, blocks.shape[1]
     face = half * size
     loads = pay.shape[0] - size // 2 - KP
     rows = loads + 4 * KP
@@ -240,7 +242,7 @@
         upper = jnp.where(row <= col, both, turned)
         lower = jnp.where(row > col, both, jnp.where(row < col, turned, diagonal))
         for k, theirs_block in ((2 * pair, upper), (2 * pair + 1, lower)):
-            block_pair = jnp.concatenate([blocks[k], theirs_block.astype(BF16)], axis=0)
+            block_pair = jnp.concatenate([blocks[base + k], theirs_block.astype(BF16)], axis=0)
             pairs[k] = block_pair
             there = slice(k * size, (k + 1) * size)
             cols = slice(at + k * size, at + (k + 1) * size)
@@ -267,8 +269,9 @@
     residual, smooth, coarse, own_basis, pairs, first, second,
 ):
     here = chain(*extent)
+    base = jnp.where(here.odd, 0, blocks.shape[0] // 2)
     side_part(
-        modes, 0, here.weights[0], here.same[0], pay, got, blocks,
+        modes, 0, here.weights[0], here.same[0], base, pay, got, blocks,
         residual, smooth, coarse, own_basis, pairs, first,
     )
     face = first.shape[1]
@@ -288,8 +291,9 @@
     face = slots // 2
     rows = loads + 4 * KP
     here = chain(*extent)
+    base = jnp.where(here.odd, blocks.shape[0] // 2, 0)
     side_part(
-        modes, face, here.weights[1], here.same[1], pay, got, blocks,
+        modes, face, here.weights[1], here.same[1], base, pay, got, blocks,
         residual, smooth, coarse, own_basis, pairs, first,
     )
 
@@ -608,16 +612,14 @@
     vector = shaped((loads, slots))
     half = block_count // 2
     packed = shaped((size // 2 + KP + loads, face))
-    side_blocks = shaped((half, size, size), BF16)
-    pay_a, pay_b, mine_a, mine_b = pl.pallas_call(
+    pay_a, pay_b, own_blocks = pl.pallas_call(
         functools.partial(pack_kernel, extent),
-        out_shape=(packed, packed, side_blocks, side_blocks),
+        out_shape=(packed, packed, shaped(blocks.shape, BF16)),
         in_specs=[HBM] * 3,
-        out_specs=(VMEM,) * 4,
+        out_specs=(VMEM,) * 3,
         scratch_shapes=[
             pltpu.VMEM(load.shape, F32),
             pltpu.VMEM(basis.shape, F32),
-            pltpu.VMEM(blocks.shape, BF16),
             pltpu.SemaphoreType.DMA((3,)),
         ],
         compiler_params=params(8),
@@ -654,7 +656,7 @@
         in_specs=[VMEM] * 4,
         out_specs=(VMEM,) * 7,
         compiler_params=params(8),
-    )(pay_a, got_a, mine_a, pick)
+    )(pay_a, got_a, own_blocks, pick)
     residual, smooth, coarse, pairs_b, image_a, image_b, keep = pl.pallas_call(
         functools.partial(first_kernel, extent, modes),
         out_shape=(
@@ -673,7 +675,7 @@
         + [pltpu.VMEM((4, KP, 2 * loads), F32)],
         compiler_params=params(12),
     )(
-        softness, pay_b, got_b, mine_b, residual_a, smooth_a, coarse_a, own_basis_a, first_a,
+        softness, pay_b, got_b, own_blocks, residual_a, smooth_a, coarse_a, own_basis_a, first_a,
         second_a, pick, operator, place,
     )
 

time: 67 us -> 66.8 us (level)
  no operation moved by 1% of the time
where the time goes in v7:
time: 66.8 us; the launch traced here: 66.5 us
  blocking collectives  29.9 us (45%)
  Pallas kernels  21 us (31%)
  starting transfers between devices  13.5 us (20%)
  between operations  1.39 us (2%)
  waiting for transfers between devices  0.73 us (1%)
    all_to_all x2, blocking collectives, share(): return lax.all_to_all(parts, AXES, 0, 0, tiled=True).reshape(copies.shape)  29.9 us
    ppermute x3, starting transfers between devices, swap(): from_a = lax.ppermute(side_a, AXES, evens)  11.4 us
    pallas_call x1, Pallas kernels, per_device(): pl.pallas_call(functools.partial(second_kernel, extent), out_shape=(vecto...  6.72 us
    pallas_call x1, Pallas kernels, per_device(): pl.pallas_call(functools.partial(first_kernel, extent, modes), out_shape=...  6.02 us
    pallas_call x1, Pallas kernels, per_device(): pl.pallas_call(functools.partial(order_kernel, extent), out_shape=(orderi...  3.93 us
    ppermute x3, starting transfers between devices, swap(): from_b = lax.ppermute(side_b, AXES, odds)  2.04 us
    pallas_call x1, Pallas kernels, per_device(): pl.pallas_call(functools.partial(last_kernel, extent), out_shape=(shaped(...  1.63 us
    pallas_call x1, Pallas kernels, per_device(): pl.pallas_call(functools.partial(pack_kernel, extent), out_shape=(packed,...  1.36 us
  transfers between devices with their start and end apart: 6, of which 1 were waited for; matrix products, arithmetic and copies ran while one was open for 0% of the time, Pallas kernels for 8%

profile of v7, /device:TPU:0, one launch (start us, length us, event | category | flops | bytes accessed | tf_op | source)
XLA Modules:
  0.0 66.5 jit_solution(14912820928327184366)
XLA Ops:
  0.6 1.4 %shard_map.87 = (f32[136,1024]{1,0:T(8,128)S(1)}, f32[136,1024]{1,0:T(8,128)S(1)}, bf16[16,128,128]{2,1,0:T(8,128)(2,1)S(1)}) custom-call(f32[64,2,1024]{2,1,0:T(2,128)} %bitcast.10, f32[6,1,2048]{2,1,0:T(1,128)} %bitcast.12, bf16[16,128,128]{2,1,0:T(8,128)(2,1)} %bitcast.11), custom_call_target="tpu_custom_call" | custom-call | tf_op jit(solution)/shard_map/pallas_call | solution.py:615
  2.0 0.7 %collective-permute-start = (f32[136,1024]{1,0:T(8,128)S(1)}, f32[136,1024]{1,0:T(8,128)S(1)}, u32[]{:S(2)}, u32[]{:S(2)}) collective-permute-start(f32[136,1024]{1,0:T(8,128)S(1)} %get-tuple-element.32.pay), channel_id=1, source_target_pairs={{1,2},{3,4},{5,6},{7,8},{9,10},{11,12},{13,14},{15,16},{17,18},{19... | collective-permute-start | bytes 1671176 | tf_op jit(solution)/shard_map/ppermute | solution.py:600
  2.7 4.3 %collective-permute-start.1 = (f32[136,1024]{1,0:T(8,128)S(1)}, f32[136,1024]{1,0:T(8,128)S(1)}, u32[]{:S(2)}, u32[]{:S(2)}) collective-permute-start(f32[136,1024]{1,0:T(8,128)S(1)} %get-tuple-element.34.pay), channel_id=1, source_target_pairs={{0,1},{2,3},{4,5},{6,7},{8,9},{10,11},{12,13},{14,15},{16,17},{18,... | collective-permute-start | bytes 1671176 | tf_op jit(solution)/shard_map/ppermute | solution.py:601
  7.7 3.9 %shard_map.86 = (bf16[2048,2048]{1,0:T(8,128)(2,1)S(1)}, bf16[2048,2048]{1,0:T(8,128)(2,1)S(1)}, bf16[2048,2048]{1,0:T(8,128)(2,1)S(1)}, f32[1,1]{1,0:T(1,128)}) custom-call(s32[1,2048]{1,0:T(1,128)} %bitcast.15, f32[1,1]{1,0:T(1,128)S(6)} %copy.9.stiffness, bf16[2048,2048]{1,0:T(8,128)(2,1)} %far_operator.1), custom_call_target="tpu_custom_call" | custom-call | flops 99999997952 | bytes 100000000 | tf_op jit(solution)/shard_map/pallas_call | solution.py:630
  11.6 0.0 collective-permute-done.1.got
  11.6 1.3 %shard_map.88 = (f32[64,1024]{1,0:T(8,128)S(1)}, f32[64,1024]{1,0:T(8,128)S(1)}, bf16[96,1024]{1,0:T(8,128)(2,1)S(1)}, bf16[16,1024]{1,0:T(8,128)(2,1)S(1)}, bf1...) custom-call(f32[136,1024]{1,0:T(8,128)S(1)} %get-tuple-element.34.pay, ...), custom_call_target="tpu_custom_call" | custom-call | tf_op jit(solution)/shard_map/pallas_call | solution.py:645
  12.9 0.0 collective-permute-done.got
  12.9 0.0 copy-start
  13.0 6.0 %shard_map.89 = (f32[64,2048]{1,0:T(8,128)S(1)}, f32[64,2048]{1,0:T(8,128)S(1)}, bf16[96,2048]{1,0:T(8,128)(2,1)S(1)}, bf16[8,256,128]{2,1,0:T(8,128)(2,1)S(1)},...) custom-call(f32[1,1]{1,0:T(1,128)} %get-tuple-element.31.softness, ...), custom_call_target="tpu_custom_call" | custom-call | tf_op jit(solution)/shard_map/pallas_call | solution.py:660
  19.0 6.5 %collective-permute-start.2 = (f32[104,1024]{1,0:T(8,128)S(1)}, f32[104,1024]{1,0:T(8,128)S(1)}, u32[]{:S(2)}, u32[]{:S(2)}) collective-permute-start(f32[104,1024]{1,0:T(8,128)S(1)} %get-tuple-element.45.image_a), channel_id=1, source_target_pairs={{0,1},{2,3},{4,5},{6,7},{8,9},{10,11},{12,13},{14,15},{16,17},{18,... | collective-permute-start | bytes 1277960 | tf_op jit(solution)/shard_map/ppermute | solution.py:601
  25.5 0.7 %collective-permute-start.3 = (f32[96,1024]{1,0:T(8,128)S(1)}, f32[96,1024]{1,0:T(8,128)S(1)}, u32[]{:S(2)}, u32[]{:S(2)}) collective-permute-start(f32[96,1024]{1,0:T(8,128)S(1)} %get-tuple-element.51.image_b), channel_id=1, source_target_pairs={{1,2},{3,4},{5,6},{7,8},{9,10},{11,12},{13,14},{15,16},{17,18},{19... | collective-permute-start | bytes 1179656 | tf_op jit(solution)/shard_map/ppermute | solution.py:600
  26.2 0.7 %collective-permute-done.2.got.got_a = f32[104,1024]{1,0:T(8,128)S(1)} collective-permute-done((f32[104,1024]{1,0:T(8,128)S(1)}, f32[104,1024]{1,0:T(8,128)S(1)}, u32[]{:S(2)}, u32[]{:S(2)}) %collective-permute-start.2) | collective-permute-done | bytes 426016 | tf_op jit(solution)/shard_map/ppermute | solution.py:601
  26.9 16.8 %all_to_all.10 = f32[96,4,128]{2,1,0:T(4,128)S(1)} all-to-all(f32[96,4,128]{2,1,0:T(4,128)S(1)} %bitcast.8), channel_id=1, replica_groups=mesh['cluster'=4,'member'=8] {'cluster','member'}, dimensions={0} | all-to-all | bytes 393216 | tf_op jit(solution)/shard_map/all_to_all | solution.py:606
  43.7 0.0 collective-permute-done.3.got_b
  43.7 0.0 copy-done
  43.7 6.7 %shard_map.92 = (f32[64,2048]{1,0:T(8,128)S(1)}, f32[64,2048]{1,0:T(8,128)S(1)}, f32[64,2048]{1,0:T(8,128)S(1)}, f32[64,1024]{1,0:T(8,128)S(1)}, f32[64,1024]{1,0:T(8,128)S(1)}, /*index=5*/f32[4,128]{1,0:T(4,128)S(1)}) custom-call(f32[1,1]{1,0:T(1,128)} %get-tuple-element.31.softness, f32[24,12,128]{2,1,0:T(8,128)S(1)} %shard_map.91.terms, ...), custom_call_target="tpu_custom_call" | custom-call | tf_op jit(solution)/shard_map/pallas_call | solution.py:698
  50.4 0.6 collective-permute-start.4
  51.1 0.7 collective-permute-start.5
  51.8 13.1 %all_to_all.11.scalars = f32[32,4,128]{2,1,0:T(4,128)S(1)} all-to-all(f32[32,4,128]{2,1,0:T(4,128)S(1)} %reshape.40), channel_id=1, replica_groups=mesh['cluster'=4,'member'=8] {'cluster','member'}, dimensions={0} | all-to-all | bytes 131072 | tf_op jit(solution)/shard_map/all_to_all | solution.py:606
  64.9 0.0 collective-permute-done.4.got_a
  64.9 0.0 collective-permute-done.5.got_b
  64.9 1.6 %shard_map.93 = (f32[64,2,1024]{2,1,0:T(2,128)}, f32[64,2,1024]{2,1,0:T(2,128)}) custom-call(f32[32,4,128]{2,1,0:T(4,128)S(1)} %all_to_all.11.scalars, f32[64,2048]{1,0:T(8,128)S(1)} %get-tuple-element.46.residual, f32[64,2048]{1,0:T(8,128)S(1)} %get-tuple-element.53.search, f32[64,2048]{1,0:T(8,128)S(1)} %get-tuple-element.54.applied, ...), custom_call_target="tpu_custom_call" | custom-call | tf_op jit(solution)/shard_map/pallas_call | solution.py:715
  (3 shorter events, 0.1 us)
Async XLA Ops:
  2.0 10.9 %collective-permute-start = (f32[136,1024]{1,0:T(8,128)S(1)}, f32[136,1024]{1,0:T(8,128)S(1)}, u32[]{:S(2)}, u32[]{:S(2)}) collective-permute-start(f32[136,1024]{1,0:T(8,128)S(1)} %get-tuple-element.32.pay), channel_id=1, source_target_pairs={{1,2},{3,4},{5,6},{7,8},{9,10},{11,12},{13,14},{15,16},{17,18},{19... | collective-permute-start | bytes 1671176 | tf_op jit(solution)/shard_map/ppermute | solution.py:600
  2.7 8.9 %collective-permute-start.1 = (f32[136,1024]{1,0:T(8,128)S(1)}, f32[136,1024]{1,0:T(8,128)S(1)}, u32[]{:S(2)}, u32[]{:S(2)}) collective-permute-start(f32[136,1024]{1,0:T(8,128)S(1)} %get-tuple-element.34.pay), channel_id=1, source_target_pairs={{0,1},{2,3},{4,5},{6,7},{8,9},{10,11},{12,13},{14,15},{16,17},{18,... | collective-permute-start | bytes 1671176 | tf_op jit(solution)/shard_map/ppermute | solution.py:601
  12.9 30.8 %copy-start = (f32[24,24]{1,0:T(8,128)S(1)}, f32[24,24]{1,0:T(8,128)}, u32[]{:S(2)}) copy-start(f32[24,24]{1,0:T(8,128)} %inverse.1) | copy-start | bytes 6916
  19.0 7.9 %collective-permute-start.2 = (f32[104,1024]{1,0:T(8,128)S(1)}, f32[104,1024]{1,0:T(8,128)S(1)}, u32[]{:S(2)}, u32[]{:S(2)}) collective-permute-start(f32[104,1024]{1,0:T(8,128)S(1)} %get-tuple-element.45.image_a), channel_id=1, source_target_pairs={{0,1},{2,3},{4,5},{6,7},{8,9},{10,11},{12,13},{14,15},{16,17},{18,... | collective-permute-start | bytes 1277960 | tf_op jit(solution)/shard_map/ppermute | solution.py:601
  25.5 18.2 %collective-permute-start.3 = (f32[96,1024]{1,0:T(8,128)S(1)}, f32[96,1024]{1,0:T(8,128)S(1)}, u32[]{:S(2)}, u32[]{:S(2)}) collective-permute-start(f32[96,1024]{1,0:T(8,128)S(1)} %get-tuple-element.51.image_b), channel_id=1, source_target_pairs={{1,2},{3,4},{5,6},{7,8},{9,10},{11,12},{13,14},{15,16},{17,18},{19... | collective-permute-start | bytes 1179656 | tf_op jit(solution)/shard_map/ppermute | solution.py:600
  50.4 14.5 %collective-permute-start.4 = (f32[64,1024]{1,0:T(8,128)S(1)}, f32[64,1024]{1,0:T(8,128)S(1)}, u32[]{:S(2)}, u32[]{:S(2)}) collective-permute-start(f32[64,1024]{1,0:T(8,128)S(1)} %get-tuple-element.56.next_a), channel_id=1, source_target_pairs={{0,1},{2,3},{4,5},{6,7},{8,9},{10,11},{12,13},{14,15},{16,17},{18,... | collective-permute-start | bytes 786440 | tf_op jit(solution)/shard_map/ppermute | solution.py:601
  51.1 13.8 %collective-permute-start.5 = (f32[64,1024]{1,0:T(8,128)S(1)}, f32[64,1024]{1,0:T(8,128)S(1)}, u32[]{:S(2)}, u32[]{:S(2)}) collective-permute-start(f32[64,1024]{1,0:T(8,128)S(1)} %get-tuple-element.57.next_b), channel_id=1, source_target_pairs={{1,2},{3,4},{5,6},{7,8},{9,10},{11,12},{13,14},{15,16},{17,18},{19... | collective-permute-start | bytes 786440 | tf_op jit(solution)/shard_map/ppermute | solution.py:600

commit v8 on v7

--- a/solution.py
+++ b/solution.py
@@ -202,6 +202,7 @@
     product = scale * (product[:rows] + product[rows:])
     image_a[:rows, :] = product[:, :face]
     image_b[:rows, :] = product[:, face:]
+    return product
 
 
 def smooth_block(value, weight, block_pair):
@@ -305,18 +306,16 @@
         (own_basis, own_basis_a), (first, first_a),
     ):
         whole[:, :face] = part[...]
-    apply_rest(rows, softness[...], operator, place, second, third, image_a, image_b)
+    images = apply_rest(
+        rows, softness[...], operator, place, second, third, image_a, image_b
+    )
 
     vectors = jnp.concatenate([stacked(residual[...]), first[...]], axis=0)
     sides = dot_rows(own_basis[...], vectors)
     load_side = folded(sides[:, : 2 * loads], KP, loads)
     smooth_side = folded(sides[:, 2 * loads :], KP, rows)
     shared = smooth_side[:, loads + 2 * KP :]
-    energy = jnp.zeros((8 * KP, 2 * rows), F32)
-    for side, image in ((0, image_a), (1, image_b)):
-        cols = slice(side * face, (side + 1) * face)
-        energy = energy + dot_rows(coarse[: 8 * KP, cols], stacked(image[:rows, :]))
-    energy = folded(energy, 4 * KP, rows)
+    energy = folded(dot_rows(coarse[: 8 * KP, :], stacked(images)), 4 * KP, rows)
     terms[0, :, :loads] = load_side
     terms[0, :, loads:] = smooth_side[:, :loads]
     terms[1, :, :loads] = energy[:KP, :loads]
@@ -516,12 +515,11 @@
 
     second[...] = dot(first[...], pick[...]).astype(BF16)
 
-    apply_rest(loads, softness[...], operator, place, second, third, next_a, next_b)
-
+    images = apply_rest(
+        loads, softness[...], operator, place, second, third, next_a, next_b
+    )
     for vector in (search, change):
-        column = jnp.sum(vector[:, :face] * next_a[...], axis=1, keepdims=True)
-        column = column + jnp.sum(vector[:, face:] * next_b[...], axis=1, keepdims=True)
-        found.append(column)
+        found.append(jnp.sum(vector[...] * images, axis=1, keepdims=True))
     lane = lax.broadcasted_iota(jnp.int32, (loads, 128), 1)
     value = jnp.zeros(lane.shape, F32)
     for k, column in enumerate(found):

time: 66.8 us -> 66.9 us (level)
  no operation moved by 1% of the time
where the time goes in v8:
time: 66.9 us; the launch traced here: 66.6 us
  blocking collectives  29.9 us (45%)
  Pallas kernels  21.1 us (32%)
  starting transfers between devices  13.5 us (20%)
  between operations  1.39 us (2%)
  waiting for transfers between devices  0.73 us (1%)
    all_to_all x2, blocking collectives, share(): return lax.all_to_all(parts, AXES, 0, 0, tiled=True).reshape(copies.shape)  29.9 us
    ppermute x3, starting transfers between devices, swap(): from_a = lax.ppermute(side_a, AXES, evens)  11.4 us
    pallas_call x1, Pallas kernels, per_device(): pl.pallas_call(functools.partial(second_kernel, extent), out_shape=(vecto...  6.75 us
    pallas_call x1, Pallas kernels, per_device(): pl.pallas_call(functools.partial(first_kernel, extent, modes), out_shape=...  6.04 us
    pallas_call x1, Pallas kernels, per_device(): pl.pallas_call(functools.partial(order_kernel, extent), out_shape=(orderi...  3.93 us
    ppermute x3, starting transfers between devices, swap(): from_b = lax.ppermute(side_b, AXES, odds)  2.04 us
    pallas_call x1, Pallas kernels, per_device(): pl.pallas_call(functools.partial(last_kernel, extent), out_shape=(shaped(...  1.63 us
    pallas_call x1, Pallas kernels, per_device(): pl.pallas_call(functools.partial(pack_kernel, extent), out_shape=(packed,...  1.36 us
  transfers between devices with their start and end apart: 6, of which 1 were waited for; matrix products, arithmetic and copies ran while one was open for 0% of the time, Pallas kernels for 8%

profile of v8, /device:TPU:0, one launch (start us, length us, event | category | flops | bytes accessed | tf_op | source)
XLA Modules:
  0.0 66.6 jit_solution(7789126221393962700)
XLA Ops:
  0.6 1.4 %shard_map.87 = (f32[136,1024]{1,0:T(8,128)S(1)}, f32[136,1024]{1,0:T(8,128)S(1)}, bf16[16,128,128]{2,1,0:T(8,128)(2,1)S(1)}) custom-call(f32[64,2,1024]{2,1,0:T(2,128)} %bitcast.10, f32[6,1,2048]{2,1,0:T(1,128)} %bitcast.12, bf16[16,128,128]{2,1,0:T(8,128)(2,1)} %bitcast.11), custom_call_target="tpu_custom_call" | custom-call | tf_op jit(solution)/shard_map/pallas_call | solution.py:613
  2.0 0.7 %collective-permute-start = (f32[136,1024]{1,0:T(8,128)S(1)}, f32[136,1024]{1,0:T(8,128)S(1)}, u32[]{:S(2)}, u32[]{:S(2)}) collective-permute-start(f32[136,1024]{1,0:T(8,128)S(1)} %get-tuple-element.32.pay), channel_id=1, source_target_pairs={{1,2},{3,4},{5,6},{7,8},{9,10},{11,12},{13,14},{15,16},{17,18},{19... | collective-permute-start | bytes 1671176 | tf_op jit(solution)/shard_map/ppermute | solution.py:598
  2.7 4.3 %collective-permute-start.1 = (f32[136,1024]{1,0:T(8,128)S(1)}, f32[136,1024]{1,0:T(8,128)S(1)}, u32[]{:S(2)}, u32[]{:S(2)}) collective-permute-start(f32[136,1024]{1,0:T(8,128)S(1)} %get-tuple-element.34.pay), channel_id=1, source_target_pairs={{0,1},{2,3},{4,5},{6,7},{8,9},{10,11},{12,13},{14,15},{16,17},{18,... | collective-permute-start | bytes 1671176 | tf_op jit(solution)/shard_map/ppermute | solution.py:599
  7.7 3.9 %shard_map.86 = (bf16[2048,2048]{1,0:T(8,128)(2,1)S(1)}, bf16[2048,2048]{1,0:T(8,128)(2,1)S(1)}, bf16[2048,2048]{1,0:T(8,128)(2,1)S(1)}, f32[1,1]{1,0:T(1,128)}) custom-call(s32[1,2048]{1,0:T(1,128)} %bitcast.15, f32[1,1]{1,0:T(1,128)S(6)} %copy.9.stiffness, bf16[2048,2048]{1,0:T(8,128)(2,1)} %far_operator.1), custom_call_target="tpu_custom_call" | custom-call | flops 99999997952 | bytes 100000000 | tf_op jit(solution)/shard_map/pallas_call | solution.py:628
  11.6 0.0 collective-permute-done.1.got
  11.6 1.3 %shard_map.88 = (f32[64,1024]{1,0:T(8,128)S(1)}, f32[64,1024]{1,0:T(8,128)S(1)}, bf16[96,1024]{1,0:T(8,128)(2,1)S(1)}, bf16[16,1024]{1,0:T(8,128)(2,1)S(1)}, bf1...) custom-call(f32[136,1024]{1,0:T(8,128)S(1)} %get-tuple-element.34.pay, ...), custom_call_target="tpu_custom_call" | custom-call | tf_op jit(solution)/shard_map/pallas_call | solution.py:643
  12.9 0.0 collective-permute-done.got
  12.9 0.0 copy-start
  13.0 6.0 %shard_map.89 = (f32[64,2048]{1,0:T(8,128)S(1)}, f32[64,2048]{1,0:T(8,128)S(1)}, bf16[96,2048]{1,0:T(8,128)(2,1)S(1)}, bf16[8,256,128]{2,1,0:T(8,128)(2,1)S(1)},...) custom-call(f32[1,1]{1,0:T(1,128)} %get-tuple-element.31.softness, ...), custom_call_target="tpu_custom_call" | custom-call | tf_op jit(solution)/shard_map/pallas_call | solution.py:658
  19.0 6.5 %collective-permute-start.2 = (f32[104,1024]{1,0:T(8,128)S(1)}, f32[104,1024]{1,0:T(8,128)S(1)}, u32[]{:S(2)}, u32[]{:S(2)}) collective-permute-start(f32[104,1024]{1,0:T(8,128)S(1)} %get-tuple-element.45.image_a), channel_id=1, source_target_pairs={{0,1},{2,3},{4,5},{6,7},{8,9},{10,11},{12,13},{14,15},{16,17},{18,... | collective-permute-start | bytes 1277960 | tf_op jit(solution)/shard_map/ppermute | solution.py:599
  25.5 0.7 %collective-permute-start.3 = (f32[96,1024]{1,0:T(8,128)S(1)}, f32[96,1024]{1,0:T(8,128)S(1)}, u32[]{:S(2)}, u32[]{:S(2)}) collective-permute-start(f32[96,1024]{1,0:T(8,128)S(1)} %get-tuple-element.51.image_b), channel_id=1, source_target_pairs={{1,2},{3,4},{5,6},{7,8},{9,10},{11,12},{13,14},{15,16},{17,18},{19... | collective-permute-start | bytes 1179656 | tf_op jit(solution)/shard_map/ppermute | solution.py:598
  26.2 0.7 %collective-permute-done.2.got.got_a = f32[104,1024]{1,0:T(8,128)S(1)} collective-permute-done((f32[104,1024]{1,0:T(8,128)S(1)}, f32[104,1024]{1,0:T(8,128)S(1)}, u32[]{:S(2)}, u32[]{:S(2)}) %collective-permute-start.2) | collective-permute-done | bytes 426016 | tf_op jit(solution)/shard_map/ppermute | solution.py:599
  26.9 16.8 %all_to_all.10 = f32[96,4,128]{2,1,0:T(4,128)S(1)} all-to-all(f32[96,4,128]{2,1,0:T(4,128)S(1)} %bitcast.8), channel_id=1, replica_groups=mesh['cluster'=4,'member'=8] {'cluster','member'}, dimensions={0} | all-to-all | bytes 393216 | tf_op jit(solution)/shard_map/all_to_all | solution.py:604
  43.7 0.0 collective-permute-done.3.got_b
  43.7 0.0 copy-done
  43.8 6.8 %shard_map.92 = (f32[64,2048]{1,0:T(8,128)S(1)}, f32[64,2048]{1,0:T(8,128)S(1)}, f32[64,2048]{1,0:T(8,128)S(1)}, f32[64,1024]{1,0:T(8,128)S(1)}, f32[64,1024]{1,0:T(8,128)S(1)}, /*index=5*/f32[4,128]{1,0:T(4,128)S(1)}) custom-call(f32[1,1]{1,0:T(1,128)} %get-tuple-element.31.softness, f32[24,12,128]{2,1,0:T(8,128)S(1)} %shard_map.91.terms, ...), custom_call_target="tpu_custom_call" | custom-call | tf_op jit(solution)/shard_map/pallas_call | solution.py:696
  50.5 0.6 collective-permute-start.4
  51.1 0.7 collective-permute-start.5
  51.8 13.2 %all_to_all.11.scalars = f32[32,4,128]{2,1,0:T(4,128)S(1)} all-to-all(f32[32,4,128]{2,1,0:T(4,128)S(1)} %reshape.40), channel_id=1, replica_groups=mesh['cluster'=4,'member'=8] {'cluster','member'}, dimensions={0} | all-to-all | bytes 131072 | tf_op jit(solution)/shard_map/all_to_all | solution.py:604
  65.0 0.0 collective-permute-done.4.got_a
  65.0 0.0 collective-permute-done.5.got_b
  65.0 1.6 %shard_map.93 = (f32[64,2,1024]{2,1,0:T(2,128)}, f32[64,2,1024]{2,1,0:T(2,128)}) custom-call(f32[32,4,128]{2,1,0:T(4,128)S(1)} %all_to_all.11.scalars, f32[64,2048]{1,0:T(8,128)S(1)} %get-tuple-element.46.residual, f32[64,2048]{1,0:T(8,128)S(1)} %get-tuple-element.53.search, f32[64,2048]{1,0:T(8,128)S(1)} %get-tuple-element.54.applied, ...), custom_call_target="tpu_custom_call" | custom-call | tf_op jit(solution)/shard_map/pallas_call | solution.py:713
  (3 shorter events, 0.1 us)
Async XLA Ops:
  2.0 10.9 %collective-permute-start = (f32[136,1024]{1,0:T(8,128)S(1)}, f32[136,1024]{1,0:T(8,128)S(1)}, u32[]{:S(2)}, u32[]{:S(2)}) collective-permute-start(f32[136,1024]{1,0:T(8,128)S(1)} %get-tuple-element.32.pay), channel_id=1, source_target_pairs={{1,2},{3,4},{5,6},{7,8},{9,10},{11,12},{13,14},{15,16},{17,18},{19... | collective-permute-start | bytes 1671176 | tf_op jit(solution)/shard_map/ppermute | solution.py:598
  2.7 8.9 %collective-permute-start.1 = (f32[136,1024]{1,0:T(8,128)S(1)}, f32[136,1024]{1,0:T(8,128)S(1)}, u32[]{:S(2)}, u32[]{:S(2)}) collective-permute-start(f32[136,1024]{1,0:T(8,128)S(1)} %get-tuple-element.34.pay), channel_id=1, source_target_pairs={{0,1},{2,3},{4,5},{6,7},{8,9},{10,11},{12,13},{14,15},{16,17},{18,... | collective-permute-start | bytes 1671176 | tf_op jit(solution)/shard_map/ppermute | solution.py:599
  12.9 30.8 %copy-start = (f32[24,24]{1,0:T(8,128)S(1)}, f32[24,24]{1,0:T(8,128)}, u32[]{:S(2)}) copy-start(f32[24,24]{1,0:T(8,128)} %inverse.1) | copy-start | bytes 6916
  19.0 7.9 %collective-permute-start.2 = (f32[104,1024]{1,0:T(8,128)S(1)}, f32[104,1024]{1,0:T(8,128)S(1)}, u32[]{:S(2)}, u32[]{:S(2)}) collective-permute-start(f32[104,1024]{1,0:T(8,128)S(1)} %get-tuple-element.45.image_a), channel_id=1, source_target_pairs={{0,1},{2,3},{4,5},{6,7},{8,9},{10,11},{12,13},{14,15},{16,17},{18,... | collective-permute-start | bytes 1277960 | tf_op jit(solution)/shard_map/ppermute | solution.py:599
  25.5 18.2 %collective-permute-start.3 = (f32[96,1024]{1,0:T(8,128)S(1)}, f32[96,1024]{1,0:T(8,128)S(1)}, u32[]{:S(2)}, u32[]{:S(2)}) collective-permute-start(f32[96,1024]{1,0:T(8,128)S(1)} %get-tuple-element.51.image_b), channel_id=1, source_target_pairs={{1,2},{3,4},{5,6},{7,8},{9,10},{11,12},{13,14},{15,16},{17,18},{19... | collective-permute-start | bytes 1179656 | tf_op jit(solution)/shard_map/ppermute | solution.py:598
  50.5 14.4 %collective-permute-start.4 = (f32[64,1024]{1,0:T(8,128)S(1)}, f32[64,1024]{1,0:T(8,128)S(1)}, u32[]{:S(2)}, u32[]{:S(2)}) collective-permute-start(f32[64,1024]{1,0:T(8,128)S(1)} %get-tuple-element.56.next_a), channel_id=1, source_target_pairs={{0,1},{2,3},{4,5},{6,7},{8,9},{10,11},{12,13},{14,15},{16,17},{18,... | collective-permute-start | bytes 786440 | tf_op jit(solution)/shard_map/ppermute | solution.py:599
  51.1 13.9 %collective-permute-start.5 = (f32[64,1024]{1,0:T(8,128)S(1)}, f32[64,1024]{1,0:T(8,128)S(1)}, u32[]{:S(2)}, u32[]{:S(2)}) collective-permute-start(f32[64,1024]{1,0:T(8,128)S(1)} %get-tuple-element.57.next_b), channel_id=1, source_target_pairs={{1,2},{3,4},{5,6},{7,8},{9,10},{11,12},{13,14},{15,16},{17,18},{19... | collective-permute-start | bytes 786440 | tf_op jit(solution)/shard_map/ppermute | solution.py:598
